TPU v7x, 512 devices: a whole 4x8x8 slice. The times are simulated.
512 devices in a mesh: dp: 32 (over x, z_lo, core), fsdp: 2 (over z_hi), tensor: 8 (over y).
Axes of the slice: x: 4, y: 8, z: 8 (z_hi: 2, z_lo: 4; z = z_hi * 4 + z_lo), core: 2. Of those that a mesh axis runs over, the one named last changes fastest.
Arguments:
- hidden: bfloat16 [16384, 4096], P(('dp', 'fsdp')), may hold values from -6 to 6
- lengths: int32 [64], P(('dp', 'fsdp')), may hold values from 64 to 256, as said below
- projection: bfloat16 [4096, 18560], P(('dp', 'fsdp', 'tensor')), may hold values from -0.09375 to 0.09375
- input_gain: float32 [4096], replicated, may hold values from 0.1 to 1.9
- x_kernel: float32 [4, 8192], P(None, 'tensor'), may hold values from -3 to 3
- x_offset: float32 [8192], P('tensor'), may hold values from -3 to 3
- bc_kernel: float32 [4, 2, 1024], P(None, None, 'tensor'), may hold values from -3 to 3
- bc_offset: float32 [2, 1024], P(None, 'tensor'), may hold values from -3 to 3
- step_bias: float32 [128], P('tensor'), may hold values from -5 to -1
- decay_log: float32 [128], P('tensor'), may hold values from -3 to 0.5
- skip_gain: float32 [128], P('tensor'), may hold values from 0.5 to 1.5
- norm_gain: float32 [8192], P('tensor'), may hold values from 0.1 to 1.9
Outputs:
- mixer_out: bfloat16 [16384, 8192], P(('dp', 'fsdp'), 'tensor')
- final_state: float32 [64, 128, 64, 128], P(('dp', 'fsdp'), 'tensor')
Inputs may be any that keep to these rules, and one draw needn't show every extreme that they name: `lengths`: each sequence's valid tokens start at the stretch's first position; some sequence fills the whole stretch.
All inputs are finite; a program needn't handle non-finite values.
Results may differ from a plain program's by a relative error of at most 0.04.
Values may be sent and summed in bfloat16 or wider, within the bound.
No kernel may reach another device: no remote copies, remote signals or barrier semaphores. Data moves between devices by JAX's collectives and lax.ppermute only.
A program may use at most 64 MiB of HBM per device.

v0:
```python
import jax
import jax.numpy as jnp
from jax import lax
from jax.sharding import PartitionSpec as P

H = 128
P_SIZE = 64
G = 8
N = 128


EPSILON = 1e-05


def causal_conv(values, kernel, offset):
    tap_count = kernel.shape[0]
    length = values.shape[1]
    pad_shape = [(0, 0), (tap_count - 1, 0)] + [(0, 0)] * (values.ndim - 2)
    padded = jnp.pad(values, pad_shape)
    summed = jnp.zeros_like(values) + offset
    for tap_index in range(tap_count):
        summed = summed + kernel[tap_index] * padded[:, tap_index : tap_index + length]
    return summed


def mamba_core(
    projected,
    seq_lengths,
    x_kernel,
    x_offset,
    bc_kernel,
    bc_offset,
    step_bias,
    decay_log,
    skip_gain,
    head_count,
    group_count,
):
    seq_count = projected.shape[0]
    length = projected.shape[1]
    inner_width = x_kernel.shape[1]
    head_width = inner_width // head_count
    bc_width = bc_kernel.shape[2]
    state_width = bc_width // group_count
    repeat_count = head_count // group_count
    gate_cols = projected[:, :, :inner_width]
    x_cols = projected[:, :, inner_width : 2 * inner_width]
    bc_cols = projected[:, :, 2 * inner_width : 2 * inner_width + 2 * bc_width].reshape(
        seq_count, length, 2, bc_width
    )
    step_raw = projected[:, :, 2 * inner_width + 2 * bc_width :]
    x_active = jax.nn.silu(causal_conv(x_cols, x_kernel, x_offset)).astype(jnp.bfloat16)
    bc_active = jax.nn.silu(causal_conv(bc_cols, bc_kernel, bc_offset)).astype(jnp.bfloat16)
    position = jnp.arange(length, dtype=jnp.int32)
    live_rows = (position[None, :] < seq_lengths[:, None]).astype(jnp.float32)
    step_size = jax.nn.softplus(step_raw + step_bias) * live_rows[:, :, None]
    decay_sum = jnp.cumsum(-jnp.exp(decay_log) * step_size, axis=1)
    decay_heads = jnp.transpose(decay_sum, (0, 2, 1))
    step_heads = jnp.transpose(step_size, (0, 2, 1))
    b_active = bc_active[:, :, 0].reshape(seq_count, length, group_count, state_width)
    c_active = bc_active[:, :, 1].reshape(seq_count, length, group_count, state_width)
    scores = jnp.einsum("stgn,sugn->sgtu", c_active, b_active, preferred_element_type=jnp.float32)
    scores = jnp.repeat(scores, repeat_count, axis=1)
    causal = position[:, None] >= position[None, :]
    spread = jnp.where(causal, decay_heads[:, :, :, None] - decay_heads[:, :, None, :], 0.0)
    decays = jnp.where(causal, jnp.exp(spread), 0.0)
    mixing = (scores * decays * step_heads[:, :, None, :]).astype(jnp.bfloat16)
    x_heads = x_active.reshape(seq_count, length, head_count, head_width)
    output = jnp.einsum("shtu,suhp->sthp", mixing, x_heads, preferred_element_type=jnp.float32)
    output = output + skip_gain[:, None] * x_heads.astype(jnp.float32)
    gated_out = output.reshape(seq_count, length, inner_width) * jax.nn.silu(gate_cols)
    remaining = jnp.exp(decay_sum[:, -1:, :] - decay_sum) * step_size
    weighted = x_heads.astype(jnp.float32) * remaining[:, :, :, None]
    b_heads = jnp.repeat(b_active, repeat_count, axis=2).astype(jnp.float32)
    final_state = jnp.einsum("suhp,suhn->shpn", weighted, b_heads, precision=lax.Precision.HIGHEST)
    return (gated_out, final_state, live_rows)


def normalize_gated(gated_out, gain, group_count, live_rows):
    seq_count = gated_out.shape[0]
    length = gated_out.shape[1]
    inner_width = gated_out.shape[2]
    grouped = gated_out.reshape(seq_count, length, group_count, inner_width // group_count)
    inverse_rms = lax.rsqrt(jnp.mean(grouped * grouped, axis=-1, keepdims=True) + EPSILON)
    scaled = (grouped * inverse_rms).reshape(seq_count, length, inner_width) * gain
    return (scaled * live_rows[:, :, None]).astype(jnp.bfloat16)


def weight_slices(weight, slices):
    row_count = weight.shape[0]
    inner_width = H * P_SIZE
    bc_width = G * N
    bounds = [
        0,
        inner_width,
        2 * inner_width,
        2 * inner_width + bc_width,
        2 * inner_width + 2 * bc_width,
        weight.shape[1],
    ]
    return [
        weight[:, bounds[member] : bounds[member + 1]].reshape(
            row_count, slices, (bounds[member + 1] - bounds[member]) // slices
        )
        for member in range(5)
    ]


def on_device(
    hidden,
    lengths,
    projection,
    input_gain,
    x_kernel,
    x_offset,
    bc_kernel,
    bc_offset,
    step_bias,
    decay_log,
    skip_gain,
    norm_gain,
):
    dp_count = lax.axis_size("dp")
    fsdp_count = lax.axis_size("fsdp")
    tensor_count = lax.axis_size("tensor")
    token_count = hidden.shape[0]
    feature_count = hidden.shape[1]
    seq_count = lengths.shape[0]
    length = token_count // seq_count
    head_count = step_bias.shape[0]
    inner_width = x_kernel.shape[1]
    group_count = G // tensor_count
    block_rows = feature_count // (dp_count * fsdp_count)
    shard_rows = projection.shape[0]
    widened = hidden.astype(jnp.float32)
    normed = (
        widened
        * lax.rsqrt(jnp.mean(widened * widened, axis=-1, keepdims=True) + EPSILON)
        * input_gain
    ).astype(jnp.bfloat16)
    grouped = jnp.concatenate(weight_slices(projection, tensor_count), axis=2)
    grouped = lax.all_to_all(grouped, "tensor", split_axis=1, concat_axis=0, tiled=True)
    local_weight = grouped.reshape(tensor_count * shard_rows, grouped.shape[2])
    own_half = normed.reshape(token_count, dp_count, fsdp_count, block_rows).transpose(0, 2, 1, 3)
    own_half = own_half.reshape(token_count, fsdp_count, dp_count * block_rows)
    pair_half = lax.all_to_all(own_half, "fsdp", split_axis=1, concat_axis=0, tiled=True)
    pair_half = pair_half.reshape(fsdp_count * token_count, dp_count * block_rows)
    partial_sum = jnp.dot(
        pair_half,
        lax.all_gather(local_weight, "dp", axis=0, tiled=True),
        preferred_element_type=jnp.float32,
    )
    rounded = lax.optimization_barrier(partial_sum.astype(jnp.bfloat16)).astype(jnp.float32)
    projected = lax.psum_scatter(
        rounded.astype(jnp.bfloat16), "fsdp", scatter_dimension=0, tiled=True
    ).astype(jnp.float32)
    gated_out, final_state, live_rows = mamba_core(
        projected.reshape(seq_count, length, projected.shape[1]),
        lengths,
        x_kernel,
        x_offset,
        bc_kernel,
        bc_offset,
        step_bias,
        decay_log,
        skip_gain,
        head_count,
        group_count,
    )
    mixer_out = normalize_gated(gated_out, norm_gain, group_count, live_rows)
    return (mixer_out.reshape(token_count, inner_width), final_state)


def solution(mesh):
    in_specs = (
        P(("dp", "fsdp"), None),
        P(("dp", "fsdp")),
        P(("dp", "fsdp", "tensor"), None),
        P(),
        P(None, "tensor"),
        P("tensor"),
        P(None, None, "tensor"),
        P(None, "tensor"),
        P("tensor"),
        P("tensor"),
        P("tensor"),
        P("tensor"),
    )
    out_specs = (P(("dp", "fsdp"), "tensor"), P(("dp", "fsdp"), "tensor", None, None))
    return jax.shard_map(
        on_device, mesh=mesh, in_specs=in_specs, out_specs=out_specs, check_vma=False
    )
```

profile of v0, /device:TPU:1, one launch (start us, length us, event | category | flops | bytes accessed | tf_op | source)
XLA Modules:
  0.0 259.2 jit_solution(2021865601214476090)
XLA Ops:
  7.2 0.0 all-gather.2.cloned.1.call-start
  7.2 1.0 fusion.36
  8.2 0.7 slice.91
  8.9 0.7 bitcast_dynamic-update-slice_fusion.1
  9.6 0.7 bitcast_dynamic-update-slice_fusion
  10.4 0.1 reshape.308
  10.5 17.4 %all_to_all.30 = bf16[8,8,2320]{2,0,1:T(8,128)(2,1)} all-to-all(bf16[8,8,2320]{2,0,1:T(8,128)(2,1)S(1)} %copy_dynamic-update-slice_fusion), channel_id=1, replica_groups=mesh['dp'=32,'fsdp'=2,'tensor'=8] {'tensor'}, dimensions={1} | all-to-all | bytes 593920 | tf_op jit(solution)/shard_map/all_to_all | solution.py:142
  27.9 0.0 all-gather.2.cloned.1.call-update
  27.9 0.0 copy-start.4
  27.9 0.0 reduce-scatter.2.cloned.1.call-start
  28.0 3.3 %copy.20 = bf16[256,4096]{0,1:T(8,128)(2,1)S(1)} copy(bf16[256,4096]{1,0:T(8,128)(2,1)} %param.12) | data formatting | bytes 4194304 | tf_op args[0]
  31.3 0.6 fusion
  31.9 0.0 copy-done.4
  31.9 0.7 fusion.2
  32.6 0.2 copy.21
  32.8 78.5 %all_to_all.31 = bf16[256,2,2048]{0,2,1:T(8,128)(2,1)S(1)} all-to-all(bf16[256,2,2048]{0,2,1:T(8,128)(2,1)S(1)} %bitcast.94), channel_id=1, replica_groups=mesh['dp'=32,'fsdp'=2,'tensor'=8] {'fsdp'}, dimensions={1} | all-to-all | bytes 4194304 | tf_op jit(solution)/shard_map/all_to_all | solution.py:146
  111.4 2.4 copy.22
  113.8 38.2 %all-gather.2.cloned.1.call-done = bf16[2048,2320]{1,0:T(8,128)(2,1)} async-done(((bf16[64,2320]{1,0:T(8,128)(2,1)}), bf16[2048,2320]{1,0:T(8,128)(2,1)}) %all-gather.2.cloned.1.call-update) | async-done | bytes 9502736 | tf_op jit(solution)/shard_map/all_gather | solution.py:150
  152.0 13.1 %convolution_convert_fusion = bf16[512,2320]{0,1:T(8,128)(2,1)} fusion(bf16[512,2048]{1,0:T(8,128)(2,1)} %bitcast.99, bf16[2048,2320]{1,0:T(8,128)(2,1)} %all-gather.2.cloned.1.call-done), kind=kOutput, calls=%fused_computation.2 | convolution fusion | flops 4866580480 | bytes 13975552 | tf_op jit(solution)/shard_map/dot_general | solution.py:148
  165.1 0.0 copy-start.12
  165.1 0.0 copy-start.9
  165.1 0.0 copy-start.5
  165.1 0.0 reduce-scatter.2.cloned.1.call-update
  165.8 0.0 copy-start.6
  165.9 0.7 iota_compare_fusion
  166.5 0.0 copy-done.12
  166.5 0.0 copy-done.9
  166.5 0.0 copy-done.5
  166.5 0.6 fusion.37
  167.2 67.0 %reduce-scatter.2.cloned.1.call-done = bf16[256,2320]{0,1:T(8,128)(2,1)} async-done(((bf16[512,2320]{0,1:T(8,128)(2,1)}), bf16[256,2320]{0,1:T(8,128)(2,1)}) %reduce-scatter.2.cloned.1.call-update) | async-done | bytes 1187856 | tf_op jit(solution)/shard_map/reduce_scatter | solution.py:154
  234.1 1.4 bitcast_convert_fusion
  235.6 0.1 slice.114
  235.7 0.7 slice.115
  236.4 0.0 copy-done.6
  236.4 0.0 copy-done.10
  236.4 0.1 copy_bitcast_fusion
  236.5 0.6 reduce-window.6
  237.1 0.2 slice_reduce_fusion
  237.2 0.6 copy.25
  237.9 0.0 copy-done.11
  237.9 2.0 multiply_convert_fusion.8
  239.9 0.9 fusion.31
  240.8 0.1 copy.26
  240.9 0.1 broadcast.138
  241.0 0.2 slice_reduce_fusion.1
  241.2 0.4 copy-done.2
  241.6 1.4 multiply_bitcast_fusion
  243.0 0.1 copy.28
  243.1 0.7 bitcast_add_fusion
  243.8 2.5 multiply_convert_fusion.7
  246.3 0.0 copy-start
  246.3 2.6 %fusion.11 = f32[1,256,16,64]{1,3,2,0:T(8,128)S(1)} fusion(bf16[256,16,64]{0,2,1:T(8,128)(2,1)S(1)} %bitcast.96, f32[16,256]{1,0:T(8,128)} %get-tuple-element.9, f32[16,256]{1,0:T(8,128)S(1)} %bitcast_add_fusion, f32[256,256]{1,0:T(8,128)} %fusion.31, pred[256,256]{1,0:T(8,128)(4,1)} %iota_compare_fusion, bf16[1,256,16,64]{1,3,2,0:T(8,128)(2,1)S(1)} %bitcast.97, ...), kind=kOutput, calls=%fused_computation.18 | convolution fusion | flops 141295616 | bytes 2457664 | tf_op jit(solution)/shard_map/shtu,suhp->sthp/dot_general | solution.py:69
  248.9 0.0 copy-done
  248.9 0.0 copy-start.7
  249.0 0.0 copy-start.8
  249.0 0.0 copy-start.3
  249.0 0.4 multiply_reduce_fusion
  249.4 0.3 copy-done.7
  249.6 0.0 copy-done.8
  249.6 0.2 fusion.21
  249.8 1.0 copy.29
  250.9 0.0 copy-done.3
  250.9 0.0 copy-done.1
  250.9 1.5 convolution_bitcast_fusion
  (17 shorter events, 0.1 us)
Async XLA Ops:
  7.2 144.9 %all-gather.2.cloned.1.call-start = ((), (), s32[]{:S(2)}) async-start(), calls=%async_computation.3 | async-start | bytes 10272768 | tf_op jit(solution)/shard_map/all_gather | solution.py:150
  27.9 3.9 %copy-start.4 = (f32[4096]{0:T(1024)S(1)}, f32[4096]{0:T(1024)}, u32[]{:S(2)}) copy-start(f32[4096]{0:T(1024)} %param.15) | copy-start | bytes 49156
  27.9 206.2 %reduce-scatter.2.cloned.1.call-start = ((), (), s32[]{:S(2)}) async-start(), calls=%async_computation.4 | async-start | bytes 3563520 | tf_op jit(solution)/shard_map/reduce_scatter | solution.py:154
  165.1 1.4 copy-start.12
  165.1 1.4 copy-start.9
  165.1 1.4 copy-start.5
  165.8 70.6 %copy-start.6 = (f32[256]{0:T(256)}, f32[256]{0:T(256)S(1)}, u32[]{:S(2)}) copy-start(f32[256]{0:T(256)S(1)} %compare_convert_fusion) | copy-start | bytes 3076
  167.2 69.3 %copy-start.10 = (f32[16]{0:T(128)S(1)}, f32[16]{0:T(128)}, u32[]{:S(2)}) copy-start(f32[16]{0:T(128)} %param.20) | copy-start | bytes 196
  167.2 70.7 %copy-start.11 = (f32[2,128]{1,0:T(2,128)S(1)}, f32[2,128]{1,0:T(2,128)}, u32[]{:S(2)}) copy-start(f32[2,128]{1,0:T(2,128)} %param.19) | copy-start | bytes 3076
  241.0 0.6 copy-start.2
  246.3 2.6 %copy-start = (bf16[1,256,1024]{1,2,0:T(8,128)(2,1)}, bf16[1,256,1024]{1,2,0:T(8,128)(2,1)S(1)}, u32[]{:S(2)}) copy-start(bf16[1,256,1024]{1,2,0:T(8,128)(2,1)S(1)} %multiply_convert_fusion.7) | copy-start | bytes 1572868
  248.9 0.7 copy-start.7
  249.0 0.7 copy-start.8
  249.0 1.9 copy-start.3
  249.3 1.5 copy-start.1
Sparse Core Ops, SparseCore 0:
  28.1 123.9 all-gather.1
  165.3 68.8 reduce-scatter.1
where the time goes:
time: 260 us; the launch traced here: 259 us
  waiting for transfers between devices  105 us (40%)
  blocking collectives  96 us (37%)
  matrix products  18.1 us (7%)
  between operations  14.9 us (6%)
  local copies, waits for them, and re-layouts  13.6 us (5%)
  other arithmetic  11.3 us (4%)
    all_to_all x1, blocking collectives, on_device(): lax.all_to_all(own_half, 'fsdp', split_axis=1, concat_axis=0, tiled=True)  78.5 us
    reduce_scatter x1, waiting for transfers between devices, on_device(): lax.psum_scatter(rounded.astype(jnp.bfloat16), 'fsdp', scatter_dimension=...  67 us
    all_gather x1, waiting for transfers between devices, on_device(): lax.all_gather(local_weight, 'dp', axis=0, tiled=True)  38.2 us
    all_to_all x1, blocking collectives, on_device(): lax.all_to_all(grouped, 'tensor', split_axis=1, concat_axis=0, tiled=True)  17.4 us
    dot_general x1, matrix products, on_device(): jnp.dot(pair_half, lax.all_gather(local_weight, 'dp', axis=0, tiled=True)...  13.1 us
    unnamed x32, local copies, waits for them, and re-layouts  6.48 us
  transfers between devices with their start and end apart: 2, of which 2 were waited for; matrix products, arithmetic and copies ran while one was open for 3% of the time, Pallas kernels for 0%

commit v1 on v0

v1 whole, which is shorter than its diff:
```python
import functools

import jax
import jax.numpy as jnp
from jax import lax
from jax.experimental import pallas as pl
from jax.experimental.pallas import tpu as pltpu
from jax.sharding import Mesh, PartitionSpec as P

EPSILON = 1e-05
F32 = jnp.float32
BF16 = jnp.bfloat16

TOK = 256
D = 4096
QUARTER = 256
NST = 128
HEADS = 4
XC = QUARTER + NST
COLS = XC + QUARTER
WIDE = XC + 128
DEPTH = 512
DZ_ORDER = (0, 1, 7, 2, 6, 3, 5, 4)
DZ_AT = {dz: at for at, dz in enumerate(DZ_ORDER)}

VMEM = pl.BlockSpec(memory_space=pltpu.VMEM)
SMEM = pl.BlockSpec(memory_space=pltpu.SMEM)


def params(mib):
    return pltpu.CompilerParams(vmem_limit_bytes=mib << 20)


def cost(flops, nbytes):
    return pl.CostEstimate(flops=flops, bytes_accessed=nbytes, transcendentals=0)


def silu(value):
    return value * jax.nn.sigmoid(value)


def norm_kernel(at_ref, hidden_ref, gain_ref, out_ref, scale_ref):
    z_at = at_ref[0]
    for rows in range(0, TOK, 32):
        wide = hidden_ref[rows : rows + 32, :].astype(F32)
        mean = jnp.sum(wide * wide, axis=1, keepdims=True) * (1.0 / D)
        scale_ref[rows : rows + 32, :] = jnp.broadcast_to(lax.rsqrt(mean + EPSILON), (32, 128))
    low = lax.broadcasted_iota(jnp.int32, (TOK, 128), 1) < 64
    scale = scale_ref[...]
    for dz in range(4):
        zs = lax.rem(z_at + dz, 8)
        zl = lax.rem(zs, 4)
        here_first = zs < 4
        here = DZ_AT[dz] * DEPTH
        there = DZ_AT[dz + 4] * DEPTH
        here_at = pl.multiple_of(jnp.where(here_first, here, there), 128)
        there_at = pl.multiple_of(jnp.where(here_first, there, here), 128)
        for x in range(4):
            base = pl.multiple_of((x * 4 + zl) * 256, 256)
            second_at = pl.multiple_of(base + 128, 128)
            first = hidden_ref[:, pl.ds(base, 128)].astype(F32) * scale * gain_ref[:, pl.ds(base, 128)]
            second = (
                hidden_ref[:, pl.ds(second_at, 128)].astype(F32)
                * scale
                * gain_ref[:, pl.ds(second_at, 128)]
            )
            low_half = jnp.where(low, first, pltpu.roll(second, 64, 1)).astype(BF16)
            high_half = jnp.where(low, pltpu.roll(first, 64, 1), second).astype(BF16)
            out_ref[:, pl.ds(pl.multiple_of(here_at + x * 128, 128), 128)] = low_half
            out_ref[:, pl.ds(pl.multiple_of(there_at + x * 128, 128), 128)] = high_half


def norm_call(at, hidden, gain):
    return pl.pallas_call(
        norm_kernel,
        out_shape=jax.ShapeDtypeStruct((TOK, D), BF16),
        in_specs=[SMEM, VMEM, VMEM],
        out_specs=VMEM,
        scratch_shapes=[pltpu.VMEM((TOK, 128), F32)],
        compiler_params=params(32),
        cost_estimate=cost(TOK * D * 8, TOK * D * 4),
        name="norm",
    )(at, hidden, gain)


def pieces(weight_refs, plan):
    for weight_ref, (at, depth, steps) in zip(weight_refs, plan):
        yield at, depth, weight_ref, steps


def step_columns(weight_ref, depth):
    tile = weight_ref[depth : depth + 16, :256].astype(F32)
    halves = []
    for half in range(2):
        rows = jnp.concatenate([tile[half * 8 : half * 8 + 8], jnp.zeros((120, 256), F32)], axis=0)
        halves.append(rows.T.astype(BF16))
    return jnp.concatenate(halves, axis=0)


def add_to(total, part):
    return part if total is None else total + part


def products(hidden_refs, weight_refs, plan, lanes, with_steps, use):
    tails = {}
    if with_steps:
        tails = {i: step_columns(w, d) for i, (_, d, w, s) in enumerate(pieces(weight_refs, plan)) if s}
    for seq, hidden_ref in enumerate(hidden_refs):
        total, steps = None, None
        for i, (at, depth, weight_ref, _) in enumerate(pieces(weight_refs, plan)):
            left = hidden_ref[:, at : at + depth]
            right = weight_ref[:depth, lanes]
            total = add_to(total, jnp.dot(left, right, preferred_element_type=F32))
            if i in tails:
                first = at // DEPTH * DEPTH
                left = hidden_ref[:, first : first + DEPTH]
                steps = add_to(steps, jnp.dot(left, tails[i], preferred_element_type=F32))
        use(seq, total, steps)


def plan_of(*dzs):
    return tuple((DZ_AT[dz] * DEPTH, DEPTH, True) for dz in dzs)


def pair_kernel(plan, has_total, keep_last, *refs):
    weight_refs = refs[2 : 2 + len(plan)]
    before_ref = refs[2 + len(plan)]
    out_ref = refs[-2 if keep_last else -1]

    def use(seq, total, steps):
        rows = pl.ds(seq * TOK, TOK)
        for lanes, part in (
            (slice(0, XC), total[:, :XC]),
            (slice(XC, WIDE), steps),
            (slice(WIDE, WIDE + QUARTER), total[:, XC:]),
        ):
            out_ref[rows, lanes] = part + before_ref[rows, lanes] if has_total else part
        if keep_last:
            refs[-1][rows, :] = refs[seq][:, DZ_AT[4] * DEPTH :]

    products(refs[:2], weight_refs, plan, slice(None), True, use)


def pair_call(hiddens, weights, plan, total, name):
    keep_last = total is not None
    operands = [*hiddens, *weights] + ([total] if keep_last else [])
    shapes = [jax.ShapeDtypeStruct((2 * TOK, WIDE + QUARTER), F32)]
    if keep_last:
        shapes.append(jax.ShapeDtypeStruct((2 * TOK, DEPTH), BF16))
    return pl.pallas_call(
        functools.partial(pair_kernel, plan, keep_last, keep_last),
        out_shape=tuple(shapes),
        in_specs=[VMEM] * len(operands),
        out_specs=(VMEM,) * len(shapes),
        compiler_params=params(48),
        cost_estimate=cost(8 * TOK * DEPTH * len(plan) * (WIDE + QUARTER), 8 * TOK * D),
        name=name,
    )(*operands)


def shifted(value, by):
    row = lax.broadcasted_iota(jnp.int32, value.shape, 0)
    return jnp.where(row < by, 0.0, pltpu.roll(value, by, 0))


def causal_conv(value, taps, offset):
    total = offset + taps[0] * shifted(value, 3)
    total = total + taps[1] * shifted(value, 2)
    total = total + taps[2] * shifted(value, 1)
    return total + taps[3] * value


def last_kernel(plan, at_ref, *refs):
    totals, weight_refs = refs[2:4], refs[4 : 4 + len(plan)]
    kernel_ref, offset_ref, x_ref, bc_ref, steps_ref, gate_ref = refs[4 + len(plan) :]
    core = at_ref[1]
    taps = [kernel_ref[tap, pl.ds(core, 1), :] for tap in range(4)]
    offset = offset_ref[pl.ds(core, 1), :]

    def use(seq, total, steps):
        rows = pl.ds(seq * TOK, TOK)
        before = pl.ds(seq % 2 * TOK, TOK)
        total_ref = totals[seq // 2]
        x_ref[rows, :] = total[:, :QUARTER] + total_ref[before, :QUARTER]
        bc = total[:, QUARTER:XC] + total_ref[before, QUARTER:XC]
        bc_ref[rows, :] = silu(causal_conv(bc, taps, offset)).astype(BF16)
        steps_ref[rows, :] = steps + total_ref[before, XC:WIDE]
        gate_ref[rows, :] = silu(total[:, XC:] + total_ref[before, WIDE:])

    hidden_refs = [refs[seq // 2].at[pl.ds(seq % 2 * TOK, TOK), :] for seq in range(4)]
    products(hidden_refs, weight_refs, plan, slice(None), True, use)


def last_call(at, hiddens, totals, weights, plan, bc_kernel, bc_offset):
    return pl.pallas_call(
        functools.partial(last_kernel, plan),
        out_shape=(
            jax.ShapeDtypeStruct((4 * TOK, QUARTER), F32),
            jax.ShapeDtypeStruct((4 * TOK, NST), BF16),
            jax.ShapeDtypeStruct((4 * TOK, 128), F32),
            jax.ShapeDtypeStruct((4 * TOK, QUARTER), F32),
        ),
        in_specs=[SMEM] + [VMEM] * (6 + len(weights)),
        out_specs=(VMEM,) * 4,
        compiler_params=params(40),
        cost_estimate=cost(8 * TOK * DEPTH * (WIDE + QUARTER), 8 * TOK * WIDE),
        name="last",
    )(at, *hiddens, *totals, *weights, bc_kernel, bc_offset)


def core_kernel(
    seq,
    at_ref,
    skip_ref,
    bias_ref,
    decay_ref,
    length_ref,
    gate_ref,
    x_ref,
    bc_own_ref,
    bc_other_ref,
    step_ref,
    x_kernel_ref,
    x_offset_ref,
    *out_refs,
):
    core = at_ref[1]
    group = at_ref[2] * 2 + core
    units = pl.ds(pl.multiple_of(group * QUARTER, QUARTER), QUARTER)
    mine = core == 0
    b_act = jnp.where(mine, bc_own_ref[...], bc_other_ref[...])
    c_act = jnp.where(mine, bc_other_ref[...], bc_own_ref[...])
    x_taps = [x_kernel_ref[tap : tap + 1, units] for tap in range(4)]
    x_act = silu(causal_conv(x_ref[...], x_taps, x_offset_ref[:, units])).astype(BF16)
    x_wide = x_act.astype(F32)

    head_at = lax.broadcasted_iota(jnp.int32, (8, TOK), 0)
    bias = jnp.zeros((8, TOK), F32)
    decay = jnp.zeros((8, TOK), F32)
    for head in range(HEADS):
        bias = jnp.where(head_at == head, bias_ref[group * HEADS + head], bias)
        decay = jnp.where(head_at == head, decay_ref[group * HEADS + head], decay)
    length = length_ref[jnp.bitwise_xor(group, seq)]
    live = lax.broadcasted_iota(jnp.int32, (8, TOK), 1).astype(F32) < length
    raw = step_ref[...].T[:8] + bias
    soft = jnp.maximum(raw, 0.0) + jnp.log1p(jnp.exp(-jnp.abs(raw)))
    step = jnp.where(live, soft, 0.0)
    ends = -jnp.exp(decay) * step
    row = lax.broadcasted_iota(jnp.int32, (TOK, TOK), 0)
    col = lax.broadcasted_iota(jnp.int32, (TOK, TOK), 1)
    ones = jnp.where(row <= col, 1.0, 0.0).astype(F32)
    sums = jnp.dot(ends, ones, precision=lax.Precision.HIGHEST, preferred_element_type=F32)
    left_over = jnp.exp(sums[:, TOK - 1 :] - sums) * step
    packed = jnp.concatenate([sums, left_over, jnp.zeros((112, TOK), F32)], axis=0)
    columns = packed.T

    scores = lax.dot_general(c_act, b_act, (((1,), (1,)), ((), ())), preferred_element_type=F32)
    causal = row >= col
    low = lax.broadcasted_iota(jnp.int32, (TOK, 128), 1) < 64
    outs, weighted = [], []
    for pair in range(HEADS // 2):
        lanes = slice(pair * 128, pair * 128 + 128)
        halves = []
        for head in (2 * pair, 2 * pair + 1):
            spread = jnp.where(causal, columns[:, head : head + 1] - sums[head : head + 1, :], -1e30)
            mixing = (scores * jnp.exp(spread) * step[head : head + 1, :]).astype(BF16)
            halves.append(jnp.dot(mixing, x_act[:, lanes], preferred_element_type=F32))
        skip = jnp.where(
            low[:1], skip_ref[group * HEADS + 2 * pair], skip_ref[group * HEADS + 2 * pair + 1]
        )
        outs.append(jnp.where(low, halves[0], halves[1]) + skip * x_wide[:, lanes])
        at = 8 + 2 * pair
        weighted.append(
            x_wide[:, lanes] * jnp.where(low, columns[:, at : at + 1], columns[:, at + 1 : at + 2])
        )
    gated = jnp.concatenate(outs, axis=1) * gate_ref[...]
    spread_x = jnp.concatenate(weighted, axis=1)
    state = jnp.dot(spread_x.T.astype(BF16), b_act, preferred_element_type=F32)
    if seq == 0:
        out_refs[0][...] = gated
        out_refs[1][...] = state
    else:
        out_refs[0][:, :QUARTER] = gated.astype(BF16)
        out_refs[0][:, QUARTER:] = state.astype(BF16)


def core_call(seq, at, skip, bias, decay, lengths, gate, x_cols, bc_own, bc_other, steps, x_kernel, x_offset):
    if seq == 0:
        out_shape = (
            jax.ShapeDtypeStruct((TOK, QUARTER), F32),
            jax.ShapeDtypeStruct((QUARTER, NST), F32),
        )
    else:
        out_shape = (jax.ShapeDtypeStruct((TOK, QUARTER + NST), BF16),)

    def rows(at_block, width):
        return pl.BlockSpec((TOK, width), lambda i: (at_block, 0))

    def whole(array):
        return pl.BlockSpec(array.shape, lambda i: (0,) * array.ndim)

    return pl.pallas_call(
        functools.partial(core_kernel, seq),
        grid=(1,),
        out_shape=out_shape,
        in_specs=[
            SMEM,
            SMEM,
            SMEM,
            SMEM,
            SMEM,
            rows(seq, QUARTER),
            rows(seq, QUARTER),
            rows(seq, NST),
            rows(seq ^ 1, NST),
            rows(seq, 128),
            whole(x_kernel),
            whole(x_offset),
        ],
        out_specs=tuple(pl.BlockSpec(s.shape, lambda i: (0, 0)) for s in out_shape),
        compiler_params=params(32),
        cost_estimate=cost(8 * TOK * TOK * 200, 8 * TOK * QUARTER),
        name=("core_own", "core_other", "core_x", "core_far")[seq],
    )(at, skip, bias, decay, lengths, gate, x_cols, bc_own, bc_other, steps, x_kernel, x_offset)


def final_kernel(at_ref, length_ref, own_ref, state_ref, a_ref, b_ref, c_ref, gain_ref, out_ref, final_ref):
    group = at_ref[2] * 2 + at_ref[1]
    own = own_ref[...]
    squares = jnp.sum(own * own, axis=1, keepdims=True)
    parts = [(0, own)]
    for flip, ref in ((1, a_ref), (2, b_ref), (3, c_ref)):
        part = ref[:, :QUARTER].astype(F32)
        squares = squares + jnp.sum(part * part, axis=1, keepdims=True)
        parts.append((flip, part))
    live = lax.broadcasted_iota(jnp.int32, (TOK, 1), 0) < length_ref[0]
    scale = jnp.where(live, lax.rsqrt(squares * (1.0 / (4 * QUARTER)) + EPSILON), 0.0)
    for flip, part in parts:
        at = pl.ds(pl.multiple_of(jnp.bitwise_xor(group, flip) * QUARTER, QUARTER), QUARTER)
        out_ref[:, at] = (part * scale * gain_ref[:, at]).astype(BF16)
        if flip == 0:
            final_ref[at, :] = state_ref[...]
        else:
            final_ref[at, :] = (a_ref, b_ref, c_ref)[flip - 1][:, QUARTER:].astype(F32)


def final_call(at, length, own, state, got, gain):
    return pl.pallas_call(
        final_kernel,
        out_shape=(
            jax.ShapeDtypeStruct((TOK, 4 * QUARTER), BF16),
            jax.ShapeDtypeStruct((4 * QUARTER, NST), F32),
        ),
        in_specs=[SMEM, SMEM] + [VMEM] * 6,
        out_specs=(VMEM, VMEM),
        compiler_params=params(32),
        cost_estimate=cost(TOK * QUARTER * 40, TOK * QUARTER * 32),
        name="gated_norm",
    )(at, length, own, state, *got, gain)


def from_z(value, distance):
    flat = lambda z: (z % 4) * 2 + z // 4
    return lax.ppermute(
        value, ("zl", "zh"), [(flat((i + distance) % 8), flat(i)) for i in range(8)]
    )


def swap_core(value):
    return lax.ppermute(value, "core", [(0, 1), (1, 0)])


def swap_x(value):
    return lax.ppermute(value, "xb", [(0, 1), (1, 0)])


def swap_both(value):
    return lax.ppermute(value, ("xb", "core"), [(0, 3), (1, 2), (2, 1), (3, 0)])


def device_slices(projection, length):
    inner = 32 * QUARTER
    gate, x_cols = (
        projection[:, at : at + inner].reshape(8, 8, 2, 2, QUARTER).transpose(0, 2, 3, 1, 4)
        for at in (0, inner)
    )
    bc = projection[:, 2 * inner : 2 * inner + 2048].reshape(8, 1, 2, 8, NST)
    steps = projection[:, 2 * inner + 2048 :].reshape(8, 8, 2, 2, HEADS).transpose(0, 2, 3, 1, 4)
    length = jnp.broadcast_to(length.astype(BF16), (8, 2, 2, 8, 1))
    joined = jnp.concatenate(
        [x_cols, jnp.broadcast_to(bc, (8, 2, 2, 8, NST)), gate, steps, length], axis=4
    )
    width = joined.shape[4]
    return jnp.broadcast_to(joined[:, None], (8, 2, 2, 2, 8, width)).reshape(8, 64, width)


def on_device(
    hidden,
    lengths,
    projection,
    input_gain,
    x_kernel,
    x_offset,
    bc_kernel,
    bc_offset,
    step_bias,
    decay_log,
    skip_gain,
    norm_gain,
):
    z_at = lax.axis_index("zh") * 4 + lax.axis_index("zl")
    at = jnp.stack([z_at, lax.axis_index("core"), lax.axis_index("xb")])
    gain = input_gain.reshape(1, D)

    block = lax.all_to_all(
        device_slices(projection, lengths),
        ("xa", "xb", "core", "y"),
        split_axis=1,
        concat_axis=0,
        tiled=True,
    ).reshape(DEPTH, COLS + HEADS + 1)
    own = norm_call(at, hidden, gain)
    block, own = lax.optimization_barrier((block, own))

    step_rows = jnp.pad(block[:, COLS : COLS + HEADS].T, ((0, 4), (0, 0)))
    step_rows = jnp.concatenate([step_rows[:, :256], step_rows[:, 256:]], axis=0)
    w0 = jnp.concatenate(
        [block[:, :COLS], jnp.pad(step_rows, ((0, 0), (0, COLS - 256)))], axis=0
    )
    lengths_all = block[:, COLS + HEADS].reshape(2, 4, 64)
    lengths_all = lax.dynamic_index_in_dim(lengths_all, lax.axis_index("xa"), 0, keepdims=False)
    lengths_all = lax.dynamic_index_in_dim(lengths_all, lax.axis_index("y") * 8, 1, keepdims=False)
    lengths_all = lengths_all.astype(F32)
    w1, w7 = from_z(w0, 1), from_z(w0, -1)
    own_x = swap_x(own)
    other = swap_core(own)
    w2, w6 = from_z(w1, 1), from_z(w7, -1)
    w2, w6, own_x = lax.optimization_barrier((w2, w6, own_x))
    far = swap_core(own_x)
    w3, w5 = from_z(w2, 1), from_z(w6, -1)

    near = pair_call([own, other], [w0, w1, w7, w2, w6], plan_of(0, 1, 7, 2, 6), None, "near")[0]
    w3, w5, near, lengths_all = lax.optimization_barrier((w3, w5, near, lengths_all))
    w4a, w4b = from_z(w3[:256], 1), from_z(w5[256:], -1)
    away = pair_call([own_x, far], [w0, w1, w7, w2, w6], plan_of(0, 1, 7, 2, 6), None, "away")[0]
    near, near_last = pair_call([own, other], [w3, w5], plan_of(3, 5), near, "near_late")
    away, away_last = pair_call([own_x, far], [w3, w5], plan_of(3, 5), away, "away_late")
    last = ((0, 256, False), (256, 256, True))
    lasts, totals, weights = (near_last, away_last), (near, away), (w4a, w4b)
    x_cols, bc_own, steps, gate = last_call(
        at, lasts, totals, weights, last, bc_kernel, bc_offset
    )
    bc_other = swap_core(bc_own)
    arguments = (
        gate,
        x_cols,
        bc_own,
        bc_other,
        steps,
        x_kernel,
        x_offset.reshape(1, 4 * QUARTER),
    )

    def core(seq):
        return core_call(seq, at, skip_gain, step_bias, decay_log, lengths_all, *arguments)

    sent = core(3)[0]
    arguments, sent = lax.optimization_barrier((arguments, sent))
    got_far = swap_both(sent)
    sent = core(2)[0]
    arguments, sent = lax.optimization_barrier((arguments, sent))
    got_x = swap_x(sent)
    sent = core(1)[0]
    arguments, sent = lax.optimization_barrier((arguments, sent))
    got_other = swap_core(sent)
    gated, state = core(0)
    mixer_out, final_state = final_call(
        at, lengths, gated, state, (got_other, got_x, got_far), norm_gain.reshape(1, 4 * QUARTER)
    )
    return mixer_out, final_state.reshape(1, 4 * HEADS, QUARTER // HEADS, NST)


def solution(mesh):
    names = ("xa", "xb", "zl", "core", "zh", "y")
    fine = Mesh(mesh.devices.reshape(2, 2, 4, 2, 2, 8), names)
    replica = names[:5]
    in_specs = (
        P(replica, None),
        P(replica),
        P(names, None),
        P(),
        P(None, "y"),
        P("y"),
        P(None, None, "y"),
        P(None, "y"),
        P("y"),
        P("y"),
        P("y"),
        P("y"),
    )
    out_specs = (P(replica, "y"), P(replica, "y", None, None))
    return jax.shard_map(
        on_device, mesh=fine, in_specs=in_specs, out_specs=out_specs, check_vma=False
    )
```

time: 260 us -> 170 us (0.65)
  blocking collectives: 96 us -> 0 us
  starting transfers between devices: 0.08 us -> 69.4 us
  waiting for transfers between devices: 105 us -> 50.3 us
  Pallas kernels: 0 us -> 31.1 us
  matrix products: 18.1 us -> 0 us
  between operations: 14.9 us -> 1.75 us
  other arithmetic: 11.3 us -> 1.41 us
    all_to_all x2 -> x0, blocking collectives: 96 us -> none  [the longest x1 78.5 us: on_device(): lax.all_to_all(own_half, 'fsdp', split_axis=1, concat_axis=0, tiled=True)]
    reduce_scatter x1 -> x0, waiting for transfers between devices: 67 us -> none  [on_device(): lax.psum_scatter(rounded.astype(jnp.bfloat16), 'fsdp', scatter_dimension=...]
    ppermute x0 -> x15, starting transfers between devices: none -> 57.8 us  [the longest x8 33.4 us: from_z(): lax.ppermute(value, ('zl', 'zh'), [(flat((i + distance) % 8), flat(i)) fo...]
    all_gather x1 -> x0, waiting for transfers between devices: 38.2 us -> none  [on_device(): lax.all_gather(local_weight, 'dp', axis=0, tiled=True)]
    ppermute x0 -> x15, waiting for transfers between devices: none -> 31.3 us  [the longest x8 24.8 us: from_z(): lax.ppermute(value, ('zl', 'zh'), [(flat((i + distance) % 8), flat(i)) fo...]
    pallas_call x0 -> x11, Pallas kernels: none -> 31.1 us  [the longest x4 18.1 us: pair_call(): pl.pallas_call(functools.partial(pair_kernel, plan, keep_last, keep_last)...]
    all_to_all x0 -> x1, waiting for transfers between devices: none -> 19 us  [on_device(): lax.all_to_all(device_slices(projection, lengths), ('xa', 'xb', 'core', '...]
    dot_general x4 -> x0, matrix products: 18.1 us -> none  [the longest x1 13.1 us: on_device(): jnp.dot(pair_half, lax.all_gather(local_weight, 'dp', axis=0, tiled=True)...]
  transfers between devices with their start and end apart: 2 -> 16, of which waited for: 2 -> 9; matrix products, arithmetic and copies ran while one was open for 3% -> 3% of each run, Pallas kernels for 0% -> 13%
where the time goes in v1:
time: 170 us; the launch traced here: 169 us
  starting transfers between devices  69.4 us (41%)
  waiting for transfers between devices  50.3 us (30%)
  Pallas kernels  31.1 us (18%)
  local copies, waits for them, and re-layouts  15.4 us (9%)
  between operations  1.75 us (1%)
    ppermute x8, starting transfers between devices, from_z(): lax.ppermute(value, ('zl', 'zh'), [(flat((i + distance) % 8), flat(i)) fo...  33.4 us
    ppermute x8, waiting for transfers between devices, from_z(): lax.ppermute(value, ('zl', 'zh'), [(flat((i + distance) % 8), flat(i)) fo...  24.8 us
    all_to_all x1, waiting for transfers between devices, on_device(): lax.all_to_all(device_slices(projection, lengths), ('xa', 'xb', 'core', '...  19 us
    pallas_call x4, Pallas kernels, pair_call(): pl.pallas_call(functools.partial(pair_kernel, plan, keep_last, keep_last)...  18.1 us
    ppermute x4, starting transfers between devices, swap_core(): return lax.ppermute(value, 'core', [(0, 1), (1, 0)])  16.1 us
    all_to_all x1, starting transfers between devices, on_device(): lax.all_to_all(device_slices(projection, lengths), ('xa', 'xb', 'core', '...  11.6 us
    unnamed x37, local copies, waits for them, and re-layouts  7.62 us
    pallas_call x4, Pallas kernels, core_call(): pl.pallas_call(functools.partial(core_kernel, seq), grid=(1,), out_shape=...  7.09 us
  transfers between devices with their start and end apart: 16, of which 9 were waited for; matrix products, arithmetic and copies ran while one was open for 3% of the time, Pallas kernels for 13%

profile of v1, /device:TPU:1, one launch (start us, length us, event | category | flops | bytes accessed | tf_op | source)
XLA Modules:
  0.0 169.4 jit_solution(4963209543914046483)
XLA Ops:
  0.6 0.7 slice.36
  1.3 0.8 slice.34
  2.1 1.0 fusion.3
  3.7 0.1 copy.35
  3.8 0.3 copy.32
  4.2 0.1 concatenate.9
  4.3 0.0 copy-start.6
  4.3 0.9 broadcast_in_dim.19
  5.3 11.6 %all-to-all-start = ((bf16[8,64,645]{2,0,1:T(8,128)(2,1)}), bf16[8,64,645]{2,0,1:T(8,128)(2,1)S(1)}, u32[]{:S(2)}, u32[]{:S(2)}) async-start(bf16[8,64,645]{2,0,1:T(8,128)(2,1)} %bitcast.11), calls=%async_computation | async-start | bytes 1572864 | tf_op jit(solution)/shard_map/all_to_all | solution.py:415
  16.9 0.1 pad_add_fusion.at_ref
  17.0 1.6 copy-done.1
  18.6 2.0 %norm.1.refs_0_ = bf16[256,4096]{1,0:T(8,128)(2,1)S(1)} custom-call(s32[3]{0:T(128)S(1)} %pad_add_fusion.at_ref, bf16[256,4096]{1,0:T(8,128)(2,1)S(1)} %copy-done.1, f32[1,4096]{1,0:T(1,128)S(1)} %bitcast.30), custom_call_target="tpu_custom_call" | custom-call | flops 8388608 | bytes 4194304 | tf_op jit(solution)/shard_map/norm/pallas_call | solution.py:74
  20.7 19.0 %all-to-all-done = bf16[8,64,645]{2,0,1:T(8,128)(2,1)S(1)} async-done(((bf16[8,64,645]{2,0,1:T(8,128)(2,1)}), bf16[8,64,645]{2,0,1:T(8,128)(2,1)S(1)}, u32[]{:S(2)}, u32[]{:S(2)}) %all-to-all-start) | async-done | bytes 660512 | tf_op jit(solution)/shard_map/all_to_all | solution.py:415
  39.6 2.7 %collective-permute-start.4 = (bf16[256,4096]{1,0:T(8,128)(2,1)S(1)}, bf16[256,4096]{1,0:T(8,128)(2,1)}, u32[]{:S(2)}, u32[]{:S(2)}) collective-permute-start(bf16[256,4096]{1,0:T(8,128)(2,1)S(1)} %norm.1.refs_0_), channel_id=1, source_target_pairs={{0,128},{128,0},{1,129},{129,1},{2,130},{130,2},{3,131},{131,3},{4... | collective-permute-start | bytes 6291464 | tf_op jit(solution)/shard_map/ppermute | solution.py:374
  42.4 0.9 slice.37
  43.3 1.1 copy.34
  44.4 0.7 slice_bitcast_fusion
  45.1 1.1 pad_maximum_fusion.refs_2_
  46.3 4.0 %collective-permute-start.2 = (bf16[528,640]{1,0:T(8,128)(2,1)S(1)}, bf16[528,640]{1,0:T(8,128)(2,1)S(1)}, u32[]{:S(2)}, u32[]{:S(2)}) collective-permute-start(bf16[528,640]{1,0:T(8,128)(2,1)S(1)} %pad_maximum_fusion.refs_2_), channel_id=1, source_target_pairs={{104,0},{0,32},{32,64},{64,96},{96,8},{8,40},{40,72},{72,104},{105... | collective-permute-start | bytes 2027528 | tf_op jit(solution)/shard_map/ppermute | solution.py:364
  50.3 8.6 %collective-permute-start = (bf16[528,640]{1,0:T(8,128)(2,1)S(1)}, bf16[528,640]{1,0:T(8,128)(2,1)S(1)}, u32[]{:S(2)}, u32[]{:S(2)}) collective-permute-start(bf16[528,640]{1,0:T(8,128)(2,1)S(1)} %pad_maximum_fusion.refs_2_), channel_id=1, source_target_pairs={{32,0},{64,32},{96,64},{8,96},{40,8},{72,40},{104,72},{0,104},{33,... | collective-permute-start | bytes 2027528 | tf_op jit(solution)/shard_map/ppermute | solution.py:364
  58.9 0.8 copy-done.2
  59.7 11.0 %collective-permute-done.2.refs_4_ = bf16[528,640]{1,0:T(8,128)(2,1)S(1)} collective-permute-done((bf16[528,640]{1,0:T(8,128)(2,1)S(1)}, bf16[528,640]{1,0:T(8,128)(2,1)S(1)}, u32[]{:S(2)}, u32[]{:S(2)}) %collective-permute-start.2) | collective-permute-done | bytes 675872 | tf_op jit(solution)/shard_map/ppermute | solution.py:364
  70.7 1.9 %collective-permute-start.3 = (bf16[528,640]{1,0:T(8,128)(2,1)S(1)}, bf16[528,640]{1,0:T(8,128)(2,1)}, u32[]{:S(2)}, u32[]{:S(2)}) collective-permute-start(bf16[528,640]{1,0:T(8,128)(2,1)S(1)} %collective-permute-done.2.refs_4_), channel_id=1, source_target_pairs={{104,0},{0,32},{32,64},{64,96},{96,8},{8,40},{40,72},{72,104},{105... | collective-permute-start | bytes 2027528 | tf_op jit(solution)/shard_map/ppermute | solution.py:364
  72.6 0.8 copy-done.13
  73.5 4.6 %collective-permute-start.1 = (bf16[528,640]{1,0:T(8,128)(2,1)S(1)}, bf16[528,640]{1,0:T(8,128)(2,1)}, u32[]{:S(2)}, u32[]{:S(2)}) collective-permute-start(bf16[528,640]{1,0:T(8,128)(2,1)S(1)} %collective-permute-done.refs_3_), channel_id=1, source_target_pairs={{32,0},{64,32},{96,64},{8,96},{40,8},{72,40},{104,72},{0,104},{33,... | collective-permute-start | bytes 2027528 | tf_op jit(solution)/shard_map/ppermute | solution.py:364
  78.1 0.9 copy-done.15
  79.0 4.8 %collective-permute-start.7 = (bf16[256,4096]{1,0:T(8,128)(2,1)S(1)}, bf16[256,4096]{1,0:T(8,128)(2,1)}, u32[]{:S(2)}, u32[]{:S(2)}) collective-permute-start(bf16[256,4096]{1,0:T(8,128)(2,1)S(1)} %norm.1.refs_0_), channel_id=1, source_target_pairs={{0,16},{16,0},{1,17},{17,1},{2,18},{18,2},{3,19},{19,3},{4,20},{20... | collective-permute-start | bytes 6291464 | tf_op jit(solution)/shard_map/ppermute | solution.py:370
  83.8 4.5 %collective-permute-done.3.refs_6_ = bf16[528,640]{1,0:T(8,128)(2,1)} collective-permute-done((bf16[528,640]{1,0:T(8,128)(2,1)S(1)}, bf16[528,640]{1,0:T(8,128)(2,1)}, u32[]{:S(2)}, u32[]{:S(2)}) %collective-permute-start.3) | collective-permute-done | bytes 675872 | tf_op jit(solution)/shard_map/ppermute | solution.py:364
  88.2 1.6 collective-permute-done.1.refs_5_
  89.9 5.4 %collective-permute-start.8 = (bf16[256,4096]{1,0:T(8,128)(2,1)}, bf16[256,4096]{1,0:T(8,128)(2,1)}, u32[]{:S(2)}, u32[]{:S(2)}) collective-permute-start(bf16[256,4096]{1,0:T(8,128)(2,1)} %collective-permute-done.4.refs_0_), channel_id=1, source_target_pairs={{0,16},{16,0},{1,17},{17,1},{2,18},{18,2},{3,19},{19,3},{4,20},{20... | collective-permute-start | bytes 6291464 | tf_op jit(solution)/shard_map/ppermute | solution.py:370
  95.3 6.9 %collective-permute-start.5 = (bf16[528,640]{1,0:T(8,128)(2,1)}, bf16[528,640]{1,0:T(8,128)(2,1)S(1)}, u32[]{:S(2)}, u32[]{:S(2)}) collective-permute-start(bf16[528,640]{1,0:T(8,128)(2,1)} %collective-permute-done.1.refs_5_), channel_id=1, source_target_pairs={{32,0},{64,32},{96,64},{8,96},{40,8},{72,40},{104,72},{0,104},{33,... | collective-permute-start | bytes 2027528 | tf_op jit(solution)/shard_map/ppermute | solution.py:364
  102.3 1.9 %collective-permute-start.6 = (bf16[528,640]{1,0:T(8,128)(2,1)}, bf16[528,640]{1,0:T(8,128)(2,1)S(1)}, u32[]{:S(2)}, u32[]{:S(2)}) collective-permute-start(bf16[528,640]{1,0:T(8,128)(2,1)} %collective-permute-done.3.refs_6_), channel_id=1, source_target_pairs={{104,0},{0,32},{32,64},{64,96},{96,8},{8,40},{40,72},{72,104},{105... | collective-permute-start | bytes 2027528 | tf_op jit(solution)/shard_map/ppermute | solution.py:364
  104.2 1.1 slice_reduce_fusion
  105.3 0.1 reshape_squeeze.3
  105.4 0.2 convert_reduce_fusion.length_ref
  105.6 1.1 copy-done.3
  106.7 1.1 copy-done.14
  107.8 1.1 copy-done.16
  108.9 5.5 %near.1.refs_4_ = f32[512,768]{1,0:T(8,128)S(1)} custom-call(bf16[256,4096]{1,0:T(8,128)(2,1)} %copy-done, bf16[256,4096]{1,0:T(8,128)(2,1)} %collective-permute-done.7.refs_1_, bf16[528,640]{1,0:T(8,128)(2,1)S(1)} %copy-done.3, bf16[528,640]{1,0:T(8,128)(2,1)S(1)} %copy-done.16, bf16[528,640]{1,0:T(8,128)(2,1)S(1)} %copy-done.14, ...), custom_call_target="tpu_custom_call" | custom-call | flops 4026531840 | bytes 8388608 | tf_op jit(solution)/shard_map/near/pallas_call | solution.py:150
  114.4 2.8 %collective-permute-done.5.refs_2_ = bf16[528,640]{1,0:T(8,128)(2,1)S(1)} collective-permute-done((bf16[528,640]{1,0:T(8,128)(2,1)}, bf16[528,640]{1,0:T(8,128)(2,1)S(1)}, u32[]{:S(2)}, u32[]{:S(2)}) %collective-permute-start.5) | collective-permute-done | bytes 675872 | tf_op jit(solution)/shard_map/ppermute | solution.py:364
  117.1 4.9 %collective-permute-done.6.refs_3_ = bf16[528,640]{1,0:T(8,128)(2,1)S(1)} collective-permute-done((bf16[528,640]{1,0:T(8,128)(2,1)}, bf16[528,640]{1,0:T(8,128)(2,1)S(1)}, u32[]{:S(2)}, u32[]{:S(2)}) %collective-permute-start.6) | collective-permute-done | bytes 675872 | tf_op jit(solution)/shard_map/ppermute | solution.py:364
  122.1 1.9 %collective-permute-start.9 = (bf16[256,640]{1,0:T(8,128)(2,1)S(1)}, bf16[256,640]{1,0:T(8,128)(2,1)S(1)}, u32[]{:S(2)}, u32[]{:S(2)}) collective-permute-start(bf16[256,640]{1,0:T(8,128)(2,1)S(1)} %slice.42), channel_id=1, source_target_pairs={{32,0},{64,32},{96,64},{8,96},{40,8},{72,40},{104,72},{0,104},{33,... | collective-permute-start | bytes 983048 | tf_op jit(solution)/shard_map/ppermute | solution.py:364
  124.1 3.5 %collective-permute-start.10 = (bf16[272,640]{1,0:T(8,128)(2,1)S(1)}, bf16[272,640]{1,0:T(8,128)(2,1)S(1)}, u32[]{:S(2)}, u32[]{:S(2)}) collective-permute-start(bf16[272,640]{1,0:T(8,128)(2,1)S(1)} %slice.43), channel_id=1, source_target_pairs={{104,0},{0,32},{32,64},{64,96},{96,8},{8,40},{40,72},{72,104},{105... | collective-permute-start | bytes 1044488 | tf_op jit(solution)/shard_map/ppermute | solution.py:364
  127.6 3.6 %near_late.1 = (f32[512,768]{1,0:T(8,128)S(1)}, bf16[512,512]{1,0:T(8,128)(2,1)S(1)}) custom-call(bf16[256,4096]{1,0:T(8,128)(2,1)} %copy-done, bf16[256,4096]{1,0:T(8,128)(2,1)} %collective-permute-done.7.refs_1_, bf16[528,640]{1,0:T(8,128)(2,1)S(1)} %collective-permute-done.5.refs_2_, bf16[528,640]{1,0:T(8,128)(2,1)S(1)} %collective-permute-done.6.refs_3_, ...), custom_call_target="tpu_custom_call" | custom-call | flops 1610612736 | bytes 8388608 | tf_op jit(solution)/shard_map/near_late/pallas_call | solution.py:150
  131.2 5.5 %away.1.refs_4_ = f32[512,768]{1,0:T(8,128)S(1)} custom-call(bf16[256,4096]{1,0:T(8,128)(2,1)} %collective-permute-done.4.refs_0_, bf16[256,4096]{1,0:T(8,128)(2,1)} %collective-permute-done.8.refs_1_, bf16[528,640]{1,0:T(8,128)(2,1)S(1)} %copy-done.3, bf16[528,640]{1,0:T(8,128)(2,1)S(1)} %copy-done.16, bf16[528,640]{1,0:T(8,128)(2,1)S(1)} %copy-done.14, ...), custom_call_target="tpu_custom_call" | custom-call | flops 4026531840 | bytes 8388608 | tf_op jit(solution)/shard_map/away/pallas_call | solution.py:150
  136.7 0.0 copy-start.11
  136.7 0.0 copy-start.12
  136.7 3.6 %away_late.1 = (f32[512,768]{1,0:T(8,128)S(1)}, bf16[512,512]{1,0:T(8,128)(2,1)S(1)}) custom-call(bf16[256,4096]{1,0:T(8,128)(2,1)} %collective-permute-done.4.refs_0_, bf16[256,4096]{1,0:T(8,128)(2,1)} %collective-permute-done.8.refs_1_, bf16[528,640]{1,0:T(8,128)(2,1)S(1)} %collective-permute-done.5.refs_2_, ...), custom_call_target="tpu_custom_call" | custom-call | flops 1610612736 | bytes 8388608 | tf_op jit(solution)/shard_map/away_late/pallas_call | solution.py:150
  140.3 0.0 copy-start.5
  140.3 0.0 copy-start.7
  140.4 2.0 %last.1 = (f32[1024,256]{1,0:T(8,128)S(1)}, bf16[1024,128]{1,0:T(8,128)(2,1)S(1)}, f32[1024,128]{1,0:T(8,128)S(1)}, f32[1024,256]{1,0:T(8,128)S(1)}) custom-call(s32[3]{0:T(128)S(1)} %pad_add_fusion.at_ref, bf16[512,512]{1,0:T(8,128)(2,1)S(1)} %get-tuple-element.55.refs_0_, bf16[512,512]{1,0:T(8,128)(2,1)S(1)} %get-tuple-element.57.refs_1_, ...), custom_call_target="tpu_custom_call" | custom-call | flops 805306368 | bytes 1048576 | tf_op jit(solution)/shard_map/last/pallas_call | solution.py:195
  142.4 3.6 %collective-permute-start.11 = (bf16[1024,128]{1,0:T(8,128)(2,1)S(1)}, bf16[1024,128]{1,0:T(8,128)(2,1)S(1)}, u32[]{:S(2)}, u32[]{:S(2)}) collective-permute-start(bf16[1024,128]{1,0:T(8,128)(2,1)S(1)} %get-tuple-element.80.bc_own_ref), channel_id=1, source_target_pairs={{0,16},{16,0},{1,17},{17,1},{2,18},{18,2},{3,19},{19,3},{4,20},{20... | collective-permute-start | bytes 786440 | tf_op jit(solution)/shard_map/ppermute | solution.py:370
  146.0 1.1 collective-permute-done.11.bc_other_ref
  147.2 1.8 %core_far.1 = bf16[256,384]{1,0:T(8,128)(2,1)S(1)} custom-call(s32[3]{0:T(128)S(1)} %pad_add_fusion.at_ref, f32[16]{0:T(128)S(1)} %copy-done.7, f32[16]{0:T(128)S(1)} %copy-done.8, f32[16]{0:T(128)S(1)} %copy-done.9, f32[4]{0:T(128)S(1)} %convert_reduce_fusion.length_ref, f32[1024,256]{1,0:T(8,128)S(1)} %get-tuple-element.78.gate_ref, ...), custom_call_target="tpu_custom_call" | custom-call | flops 104857600 | bytes 524288 | tf_op jit(solution)/shard_map/core_far/pallas_call | solution.py:302
  148.9 1.8 %core_x.1 = bf16[256,384]{1,0:T(8,128)(2,1)S(1)} custom-call(s32[3]{0:T(128)S(1)} %pad_add_fusion.at_ref, f32[16]{0:T(128)S(1)} %copy-done.7, f32[16]{0:T(128)S(1)} %copy-done.8, f32[16]{0:T(128)S(1)} %copy-done.9, f32[4]{0:T(128)S(1)} %convert_reduce_fusion.length_ref, f32[1024,256]{1,0:T(8,128)S(1)} %get-tuple-element.78.gate_ref, ...), custom_call_target="tpu_custom_call" | custom-call | flops 104857600 | bytes 524288 | tf_op jit(solution)/shard_map/core_x/pallas_call | solution.py:302
  150.7 1.8 %core_other.1 = bf16[256,384]{1,0:T(8,128)(2,1)S(1)} custom-call(s32[3]{0:T(128)S(1)} %pad_add_fusion.at_ref, f32[16]{0:T(128)S(1)} %copy-done.7, f32[16]{0:T(128)S(1)} %copy-done.8, f32[16]{0:T(128)S(1)} %copy-done.9, f32[4]{0:T(128)S(1)} %convert_reduce_fusion.length_ref, f32[1024,256]{1,0:T(8,128)S(1)} %get-tuple-element.78.gate_ref, ...), custom_call_target="tpu_custom_call" | custom-call | flops 104857600 | bytes 524288 | tf_op jit(solution)/shard_map/core_other/pallas_call | solution.py:302
  152.5 0.0 copy-start.10
  152.5 2.3 %collective-permute-start.12 = (bf16[256,384]{1,0:T(8,128)(2,1)S(1)}, bf16[256,384]{1,0:T(8,128)(2,1)S(1)}, u32[]{:S(2)}, u32[]{:S(2)}) collective-permute-start(bf16[256,384]{1,0:T(8,128)(2,1)S(1)} %core_other.1), channel_id=1, source_target_pairs={{0,16},{16,0},{1,17},{17,1},{2,18},{18,2},{3,19},{19,3},{4,20},{20... | collective-permute-start | bytes 589832 | tf_op jit(solution)/shard_map/ppermute | solution.py:370
  154.8 2.7 %collective-permute-start.13 = (bf16[256,384]{1,0:T(8,128)(2,1)S(1)}, bf16[256,384]{1,0:T(8,128)(2,1)S(1)}, u32[]{:S(2)}, u32[]{:S(2)}) collective-permute-start(bf16[256,384]{1,0:T(8,128)(2,1)S(1)} %core_x.1), channel_id=1, source_target_pairs={{0,128},{128,0},{1,129},{129,1},{2,130},{130,2},{3,131},{131,3},{4... | collective-permute-start | bytes 589832 | tf_op jit(solution)/shard_map/ppermute | solution.py:374
  157.5 2.9 %collective-permute-start.14 = (bf16[256,384]{1,0:T(8,128)(2,1)S(1)}, bf16[256,384]{1,0:T(8,128)(2,1)S(1)}, u32[]{:S(2)}, u32[]{:S(2)}) collective-permute-start(bf16[256,384]{1,0:T(8,128)(2,1)S(1)} %core_far.1), channel_id=1, source_target_pairs={{0,144},{16,128},{128,16},{144,0},{1,145},{17,129},{129,17},{145,1... | collective-permute-start | bytes 589832 | tf_op jit(solution)/shard_map/ppermute | solution.py:378
  160.4 1.8 %core_own.1 = (f32[256,256]{1,0:T(8,128)S(1)}, f32[256,128]{1,0:T(8,128)S(1)}) custom-call(s32[3]{0:T(128)S(1)} %pad_add_fusion.at_ref, f32[16]{0:T(128)S(1)} %copy-done.7, f32[16]{0:T(128)S(1)} %copy-done.8, f32[16]{0:T(128)S(1)} %copy-done.9, f32[4]{0:T(128)S(1)} %convert_reduce_fusion.length_ref, f32[1024,256]{1,0:T(8,128)S(1)} %get-tuple-element.78.gate_ref, ...), custom_call_target="tpu_custom_call" | custom-call | flops 104857600 | bytes 524288 | tf_op jit(solution)/shard_map/core_own/pallas_call | solution.py:302
  162.2 0.9 collective-permute-done.13.b_ref
  163.0 4.5 %collective-permute-done.14.c_ref = bf16[256,384]{1,0:T(8,128)(2,1)S(1)} collective-permute-done((bf16[256,384]{1,0:T(8,128)(2,1)S(1)}, bf16[256,384]{1,0:T(8,128)(2,1)S(1)}, u32[]{:S(2)}, u32[]{:S(2)}) %collective-permute-start.14) | collective-permute-done | bytes 196640 | tf_op jit(solution)/shard_map/ppermute | solution.py:378
  167.5 1.9 %gated_norm.1 = (bf16[256,1024]{1,0:T(8,128)(2,1)}, f32[1024,128]{1,0:T(8,128)}) custom-call(s32[3]{0:T(128)S(1)} %pad_add_fusion.at_ref, s32[1]{0:T(128)S(6)} %copy.36.length_ref, f32[256,256]{1,0:T(8,128)S(1)} %get-tuple-element.85.own_ref, f32[256,128]{1,0:T(8,128)S(1)} %get-tuple-element.86.state_ref, ...), custom_call_target="tpu_custom_call" | custom-call | flops 2621440 | bytes 2097152 | tf_op jit(solution)/shard_map/gated_norm/pallas_call | solution.py:348
  (38 shorter events, 0.2 us)
Async XLA Ops:
  4.3 12.7 %copy-start.6 = (f32[4096]{0:T(1024)S(1)}, f32[4096]{0:T(1024)}, u32[]{:S(2)}) copy-start(f32[4096]{0:T(1024)} %param.15) | copy-start | bytes 49156
  5.3 34.4 %all-to-all-start = ((bf16[8,64,645]{2,0,1:T(8,128)(2,1)}), bf16[8,64,645]{2,0,1:T(8,128)(2,1)S(1)}, u32[]{:S(2)}, u32[]{:S(2)}) async-start(bf16[8,64,645]{2,0,1:T(8,128)(2,1)} %bitcast.11), calls=%async_computation | async-start | bytes 1572864 | tf_op jit(solution)/shard_map/all_to_all | solution.py:415
  17.0 1.6 copy-start.1
  20.6 57.4 %copy-start = (bf16[256,4096]{1,0:T(8,128)(2,1)}, bf16[256,4096]{1,0:T(8,128)(2,1)S(1)}, u32[]{:S(2)}) copy-start(bf16[256,4096]{1,0:T(8,128)(2,1)S(1)} %norm.1.refs_0_) | copy-start | bytes 6291460
  39.6 50.3 %copy-start.17 = (bf16[8,64,645]{2,0,1:T(8,128)(2,1)}, bf16[8,64,645]{2,0,1:T(8,128)(2,1)S(1)}, u32[]{:S(2)}) copy-start(bf16[8,64,645]{2,0,1:T(8,128)(2,1)S(1)} %all-to-all-done) | copy-start | bytes 1981444
  39.6 50.3 %collective-permute-start.4 = (bf16[256,4096]{1,0:T(8,128)(2,1)S(1)}, bf16[256,4096]{1,0:T(8,128)(2,1)}, u32[]{:S(2)}, u32[]{:S(2)}) collective-permute-start(bf16[256,4096]{1,0:T(8,128)(2,1)S(1)} %norm.1.refs_0_), channel_id=1, source_target_pairs={{0,128},{128,0},{1,129},{129,1},{2,130},{130,2},{3,131},{131,3},{4... | collective-permute-start | bytes 6291464 | tf_op jit(solution)/shard_map/ppermute | solution.py:374
  46.3 24.4 %collective-permute-start.2 = (bf16[528,640]{1,0:T(8,128)(2,1)S(1)}, bf16[528,640]{1,0:T(8,128)(2,1)S(1)}, u32[]{:S(2)}, u32[]{:S(2)}) collective-permute-start(bf16[528,640]{1,0:T(8,128)(2,1)S(1)} %pad_maximum_fusion.refs_2_), channel_id=1, source_target_pairs={{104,0},{0,32},{32,64},{64,96},{96,8},{8,40},{40,72},{72,104},{105... | collective-permute-start | bytes 2027528 | tf_op jit(solution)/shard_map/ppermute | solution.py:364
  50.3 23.2 %collective-permute-start = (bf16[528,640]{1,0:T(8,128)(2,1)S(1)}, bf16[528,640]{1,0:T(8,128)(2,1)S(1)}, u32[]{:S(2)}, u32[]{:S(2)}) collective-permute-start(bf16[528,640]{1,0:T(8,128)(2,1)S(1)} %pad_maximum_fusion.refs_2_), channel_id=1, source_target_pairs={{32,0},{64,32},{96,64},{8,96},{40,8},{72,40},{104,72},{0,104},{33,... | collective-permute-start | bytes 2027528 | tf_op jit(solution)/shard_map/ppermute | solution.py:364
  58.9 0.8 copy-start.2
  70.7 17.5 %collective-permute-start.3 = (bf16[528,640]{1,0:T(8,128)(2,1)S(1)}, bf16[528,640]{1,0:T(8,128)(2,1)}, u32[]{:S(2)}, u32[]{:S(2)}) collective-permute-start(bf16[528,640]{1,0:T(8,128)(2,1)S(1)} %collective-permute-done.2.refs_4_), channel_id=1, source_target_pairs={{104,0},{0,32},{32,64},{64,96},{96,8},{8,40},{40,72},{72,104},{105... | collective-permute-start | bytes 2027528 | tf_op jit(solution)/shard_map/ppermute | solution.py:364
  72.6 0.9 copy-start.13
  73.5 16.4 %collective-permute-start.1 = (bf16[528,640]{1,0:T(8,128)(2,1)S(1)}, bf16[528,640]{1,0:T(8,128)(2,1)}, u32[]{:S(2)}, u32[]{:S(2)}) collective-permute-start(bf16[528,640]{1,0:T(8,128)(2,1)S(1)} %collective-permute-done.refs_3_), channel_id=1, source_target_pairs={{32,0},{64,32},{96,64},{8,96},{40,8},{72,40},{104,72},{0,104},{33,... | collective-permute-start | bytes 2027528 | tf_op jit(solution)/shard_map/ppermute | solution.py:364
  78.1 0.9 copy-start.15
  79.0 26.6 %collective-permute-start.7 = (bf16[256,4096]{1,0:T(8,128)(2,1)S(1)}, bf16[256,4096]{1,0:T(8,128)(2,1)}, u32[]{:S(2)}, u32[]{:S(2)}) collective-permute-start(bf16[256,4096]{1,0:T(8,128)(2,1)S(1)} %norm.1.refs_0_), channel_id=1, source_target_pairs={{0,16},{16,0},{1,17},{17,1},{2,18},{18,2},{3,19},{19,3},{4,20},{20... | collective-permute-start | bytes 6291464 | tf_op jit(solution)/shard_map/ppermute | solution.py:370
  89.9 41.3 %collective-permute-start.8 = (bf16[256,4096]{1,0:T(8,128)(2,1)}, bf16[256,4096]{1,0:T(8,128)(2,1)}, u32[]{:S(2)}, u32[]{:S(2)}) collective-permute-start(bf16[256,4096]{1,0:T(8,128)(2,1)} %collective-permute-done.4.refs_0_), channel_id=1, source_target_pairs={{0,16},{16,0},{1,17},{17,1},{2,18},{18,2},{3,19},{19,3},{4,20},{20... | collective-permute-start | bytes 6291464 | tf_op jit(solution)/shard_map/ppermute | solution.py:370
  95.3 21.8 %collective-permute-start.5 = (bf16[528,640]{1,0:T(8,128)(2,1)}, bf16[528,640]{1,0:T(8,128)(2,1)S(1)}, u32[]{:S(2)}, u32[]{:S(2)}) collective-permute-start(bf16[528,640]{1,0:T(8,128)(2,1)} %collective-permute-done.1.refs_5_), channel_id=1, source_target_pairs={{32,0},{64,32},{96,64},{8,96},{40,8},{72,40},{104,72},{0,104},{33,... | collective-permute-start | bytes 2027528 | tf_op jit(solution)/shard_map/ppermute | solution.py:364
  102.3 19.8 %collective-permute-start.6 = (bf16[528,640]{1,0:T(8,128)(2,1)}, bf16[528,640]{1,0:T(8,128)(2,1)S(1)}, u32[]{:S(2)}, u32[]{:S(2)}) collective-permute-start(bf16[528,640]{1,0:T(8,128)(2,1)} %collective-permute-done.3.refs_6_), channel_id=1, source_target_pairs={{104,0},{0,32},{32,64},{64,96},{96,8},{8,40},{40,72},{72,104},{105... | collective-permute-start | bytes 2027528 | tf_op jit(solution)/shard_map/ppermute | solution.py:364
  105.6 1.1 copy-start.3
  106.7 1.1 copy-start.14
  107.8 1.1 copy-start.16
  122.1 18.2 %collective-permute-start.9 = (bf16[256,640]{1,0:T(8,128)(2,1)S(1)}, bf16[256,640]{1,0:T(8,128)(2,1)S(1)}, u32[]{:S(2)}, u32[]{:S(2)}) collective-permute-start(bf16[256,640]{1,0:T(8,128)(2,1)S(1)} %slice.42), channel_id=1, source_target_pairs={{32,0},{64,32},{96,64},{8,96},{40,8},{72,40},{104,72},{0,104},{33,... | collective-permute-start | bytes 983048 | tf_op jit(solution)/shard_map/ppermute | solution.py:364
  124.1 16.2 %collective-permute-start.10 = (bf16[272,640]{1,0:T(8,128)(2,1)S(1)}, bf16[272,640]{1,0:T(8,128)(2,1)S(1)}, u32[]{:S(2)}, u32[]{:S(2)}) collective-permute-start(bf16[272,640]{1,0:T(8,128)(2,1)S(1)} %slice.43), channel_id=1, source_target_pairs={{104,0},{0,32},{32,64},{64,96},{96,8},{8,40},{40,72},{72,104},{105... | collective-permute-start | bytes 1044488 | tf_op jit(solution)/shard_map/ppermute | solution.py:364
  136.7 3.6 %copy-start.11 = (f32[4,2,128]{2,1,0:T(2,128)S(1)}, f32[4,2,128]{2,1,0:T(2,128)}, u32[]{:S(2)}) copy-start(f32[4,2,128]{2,1,0:T(2,128)} %refs_6_.1) | copy-start | bytes 12292
  136.7 3.6 %copy-start.12 = (f32[2,128]{1,0:T(2,128)S(1)}, f32[2,128]{1,0:T(2,128)}, u32[]{:S(2)}) copy-start(f32[2,128]{1,0:T(2,128)} %refs_7_.1) | copy-start | bytes 3076
  140.3 6.8 %copy-start.4 = (f32[4,1024]{1,0:T(4,128)S(1)}, f32[4,1024]{1,0:T(4,128)}, u32[]{:S(2)}) copy-start(f32[4,1024]{1,0:T(4,128)} %x_kernel_ref.4) | copy-start | bytes 49156
  140.3 6.8 %copy-start.5 = (f32[1024]{0:T(1024)S(1)}, f32[1024]{0:T(1024)}, u32[]{:S(2)}) copy-start(f32[1024]{0:T(1024)} %param.17) | copy-start | bytes 12292
  140.3 6.8 %copy-start.7 = (f32[16]{0:T(128)S(1)}, f32[16]{0:T(128)}, u32[]{:S(2)}) copy-start(f32[16]{0:T(128)} %skip_ref.7) | copy-start | bytes 196
  140.4 6.8 %copy-start.8 = (f32[16]{0:T(128)S(1)}, f32[16]{0:T(128)}, u32[]{:S(2)}) copy-start(f32[16]{0:T(128)} %bias_ref.7) | copy-start | bytes 196
  140.4 6.8 %copy-start.9 = (f32[16]{0:T(128)S(1)}, f32[16]{0:T(128)}, u32[]{:S(2)}) copy-start(f32[16]{0:T(128)} %decay_ref.7) | copy-start | bytes 196
  142.4 4.7 %collective-permute-start.11 = (bf16[1024,128]{1,0:T(8,128)(2,1)S(1)}, bf16[1024,128]{1,0:T(8,128)(2,1)S(1)}, u32[]{:S(2)}, u32[]{:S(2)}) collective-permute-start(bf16[1024,128]{1,0:T(8,128)(2,1)S(1)} %get-tuple-element.80.bc_own_ref), channel_id=1, source_target_pairs={{0,16},{16,0},{1,17},{17,1},{2,18},{18,2},{3,19},{19,3},{4,20},{20... | collective-permute-start | bytes 786440 | tf_op jit(solution)/shard_map/ppermute | solution.py:370
  152.5 15.0 %copy-start.10 = (f32[1024]{0:T(1024)S(1)}, f32[1024]{0:T(1024)}, u32[]{:S(2)}) copy-start(f32[1024]{0:T(1024)} %param.23) | copy-start | bytes 12292
  152.5 9.7 %collective-permute-start.12 = (bf16[256,384]{1,0:T(8,128)(2,1)S(1)}, bf16[256,384]{1,0:T(8,128)(2,1)S(1)}, u32[]{:S(2)}, u32[]{:S(2)}) collective-permute-start(bf16[256,384]{1,0:T(8,128)(2,1)S(1)} %core_other.1), channel_id=1, source_target_pairs={{0,16},{16,0},{1,17},{17,1},{2,18},{18,2},{3,19},{19,3},{4,20},{20... | collective-permute-start | bytes 589832 | tf_op jit(solution)/shard_map/ppermute | solution.py:370
  154.8 8.3 %collective-permute-start.13 = (bf16[256,384]{1,0:T(8,128)(2,1)S(1)}, bf16[256,384]{1,0:T(8,128)(2,1)S(1)}, u32[]{:S(2)}, u32[]{:S(2)}) collective-permute-start(bf16[256,384]{1,0:T(8,128)(2,1)S(1)} %core_x.1), channel_id=1, source_target_pairs={{0,128},{128,0},{1,129},{129,1},{2,130},{130,2},{3,131},{131,3},{4... | collective-permute-start | bytes 589832 | tf_op jit(solution)/shard_map/ppermute | solution.py:374
  157.5 10.0 %collective-permute-start.14 = (bf16[256,384]{1,0:T(8,128)(2,1)S(1)}, bf16[256,384]{1,0:T(8,128)(2,1)S(1)}, u32[]{:S(2)}, u32[]{:S(2)}) collective-permute-start(bf16[256,384]{1,0:T(8,128)(2,1)S(1)} %core_far.1), channel_id=1, source_target_pairs={{0,144},{16,128},{128,16},{144,0},{1,145},{17,129},{129,17},{145,1... | collective-permute-start | bytes 589832 | tf_op jit(solution)/shard_map/ppermute | solution.py:378

commit v2 on v1

v2 whole, which is shorter than its diff:
```python
import functools

import jax
import jax.numpy as jnp
from jax import lax
from jax.experimental import pallas as pl
from jax.experimental.pallas import tpu as pltpu
from jax.sharding import Mesh, PartitionSpec as P

EPSILON = 1e-05
F32 = jnp.float32
BF16 = jnp.bfloat16

TOK = 256
D = 4096
QUARTER = 256
NST = 128
HEADS = 4
XC = QUARTER + NST
COLS = XC + QUARTER
WIDE = XC + 128
HALF = 256
DEPTH = 2 * HALF
PACKED = DEPTH + 16
SENT = 768
DZ_ORDER = (0, 1, 7, 2, 6, 3, 5, 4)
DZ_AT = {dz: at for at, dz in enumerate(DZ_ORDER)}

VMEM = pl.BlockSpec(memory_space=pltpu.VMEM)
SMEM = pl.BlockSpec(memory_space=pltpu.SMEM)


def params(mib):
    return pltpu.CompilerParams(vmem_limit_bytes=mib << 20)


def cost(flops, nbytes):
    return pl.CostEstimate(flops=flops, bytes_accessed=nbytes, transcendentals=0)


def silu(value):
    return value * jax.nn.sigmoid(value)


def norm_kernel(at_ref, hidden_ref, gain_ref, out_ref, scale_ref):
    z_at = at_ref[0]
    for rows in range(0, TOK, 32):
        wide = hidden_ref[rows : rows + 32, :].astype(F32)
        mean = jnp.sum(wide * wide, axis=1, keepdims=True) * (1.0 / D)
        scale_ref[rows : rows + 32, :] = jnp.broadcast_to(lax.rsqrt(mean + EPSILON), (32, 128))
    low = lax.broadcasted_iota(jnp.int32, (TOK, 128), 1) < 64
    scale = scale_ref[...]
    for dz in range(4):
        zs = lax.rem(z_at + dz, 8)
        zl = lax.rem(zs, 4)
        here_first = zs < 4
        here = DZ_AT[dz] * DEPTH
        there = DZ_AT[dz + 4] * DEPTH
        here_at = pl.multiple_of(jnp.where(here_first, here, there), 128)
        there_at = pl.multiple_of(jnp.where(here_first, there, here), 128)
        for part in range(4):
            base = pl.multiple_of((part * 4 + zl) * 256, 256)
            second_at = pl.multiple_of(base + 128, 128)
            first = hidden_ref[:, pl.ds(base, 128)].astype(F32) * scale * gain_ref[:, pl.ds(base, 128)]
            second = (
                hidden_ref[:, pl.ds(second_at, 128)].astype(F32)
                * scale
                * gain_ref[:, pl.ds(second_at, 128)]
            )
            low_half = jnp.where(low, first, pltpu.roll(second, 64, 1)).astype(BF16)
            high_half = jnp.where(low, pltpu.roll(first, 64, 1), second).astype(BF16)
            out_ref[:, pl.ds(pl.multiple_of(here_at + part * 128, 128), 128)] = low_half
            out_ref[:, pl.ds(pl.multiple_of(there_at + part * 128, 128), 128)] = high_half


def norm_call(at, hidden, gain):
    return pl.pallas_call(
        norm_kernel,
        out_shape=jax.ShapeDtypeStruct((TOK, D), BF16),
        in_specs=[SMEM, VMEM, VMEM],
        out_specs=VMEM,
        scratch_shapes=[pltpu.VMEM((TOK, 128), F32)],
        compiler_params=params(32),
        cost_estimate=cost(TOK * D * 8, TOK * D * 4),
        name="norm",
    )(at, hidden, gain)


def cut_kernel(length_ref, rows_ref, out_ref):
    inner = 32 * QUARTER
    lane = lax.broadcasted_iota(jnp.int32, (8, 128), 1)
    length = length_ref[0].astype(F32)
    steps = rows_ref[:, 2 * inner + 2048 :].astype(F32)
    for to in range(32):
        group, y = to // 8, to % 8
        units = y * 4 * QUARTER + group * QUARTER
        bc = 2 * inner + (group % 2) * 1024 + y * NST
        at = y * 16 + group * HEADS
        mine = steps if at == 0 else pltpu.roll(steps, 128 - at, 1)
        tail = jnp.where(lane < HEADS, mine, jnp.where(lane == HEADS, length, 0.0))
        for side in (to, to + 32):
            out_ref[side, :, :QUARTER] = rows_ref[:, inner + units : inner + units + QUARTER]
            out_ref[side, :, QUARTER:XC] = rows_ref[:, bc : bc + NST]
            out_ref[side, :, XC:COLS] = rows_ref[:, units : units + QUARTER]
            out_ref[side, :, COLS:] = tail.astype(BF16)


def cut_call(length, rows):
    return pl.pallas_call(
        cut_kernel,
        out_shape=jax.ShapeDtypeStruct((64, 8, SENT), BF16),
        in_specs=[SMEM, VMEM],
        out_specs=VMEM,
        compiler_params=params(32),
        cost_estimate=cost(1000, 1000),
        name="cut",
    )(length, rows)


def pack_kernel(block_ref, out_ref, lengths_ref):
    out_ref[:DEPTH, :] = block_ref[:, :COLS]
    tail = block_ref[:, COLS:].astype(F32).T
    row = lax.broadcasted_iota(jnp.int32, (8, HALF), 0)
    halves = [jnp.where(row < HEADS, tail[:8, at : at + HALF], 0.0) for at in (0, HALF)]
    out_ref[DEPTH:, :HALF] = jnp.concatenate(halves, axis=0).astype(BF16)
    out_ref[DEPTH:, HALF:] = jnp.zeros((16, COLS - HALF), BF16)
    lengths_ref[...] = tail[:8]


def pack_call(block):
    return pl.pallas_call(
        pack_kernel,
        out_shape=(
            jax.ShapeDtypeStruct((PACKED, COLS), BF16),
            jax.ShapeDtypeStruct((8, DEPTH), F32),
        ),
        in_specs=[VMEM],
        out_specs=(VMEM, VMEM),
        compiler_params=params(32),
        cost_estimate=cost(1000, 1000),
        name="pack",
    )(block)


def step_columns(tile):
    wide = jnp.concatenate([tile.astype(F32), jnp.zeros((112, HALF), F32)], axis=0).T
    return [wide.astype(BF16), pltpu.roll(wide, 120, 1).astype(BF16)]


def products(hidden_refs, weight_refs, first, use):
    rows = [ref[: ref.shape[0] // HALF * HALF, :] for ref in weight_refs]
    steps = []
    for ref in weight_refs:
        if ref.shape[0] % HALF:
            steps += step_columns(ref[ref.shape[0] - 16 :, :HALF])
    rows = jnp.concatenate(rows, axis=0)
    steps = jnp.concatenate(steps, axis=0)
    right = jnp.concatenate([rows[:, :XC], steps, rows[:, XC:]], axis=1)
    for seq, ref in enumerate(hidden_refs):
        left = ref[:, first : first + right.shape[0]]
        use(seq, jnp.dot(left, right, preferred_element_type=F32))


def pair_kernel(count, first, has_total, *refs):
    weight_refs = refs[2 : 2 + count]
    out_ref = refs[-2 if has_total else -1]

    def use(seq, part):
        rows = pl.ds(seq * TOK, TOK)
        out_ref[rows, :] = part + refs[2 + count][rows, :] if has_total else part
        if has_total:
            refs[-1][rows, :] = refs[seq][:, DZ_AT[4] * DEPTH :]

    products(refs[:2], weight_refs, first, use)


def pair_call(hiddens, weights, first, total, name):
    operands = [*hiddens, *weights] + ([] if total is None else [total])
    shapes = [jax.ShapeDtypeStruct((2 * TOK, WIDE + QUARTER), F32)]
    if total is not None:
        shapes.append(jax.ShapeDtypeStruct((2 * TOK, DEPTH), BF16))
    return pl.pallas_call(
        functools.partial(pair_kernel, len(weights), first, total is not None),
        out_shape=tuple(shapes),
        in_specs=[VMEM] * len(operands),
        out_specs=(VMEM,) * len(shapes),
        compiler_params=params(48),
        cost_estimate=cost(4 * TOK * DEPTH * len(weights) * (WIDE + QUARTER), 4 * TOK * D),
        name=name,
    )(*operands)


def shifted(value, by):
    row = lax.broadcasted_iota(jnp.int32, value.shape, 0)
    return jnp.where(row < by, 0.0, pltpu.roll(value, by, 0))


def causal_conv(value, taps, offset):
    total = offset + taps[0] * shifted(value, 3)
    total = total + taps[1] * shifted(value, 2)
    total = total + taps[2] * shifted(value, 1)
    return total + taps[3] * value


def last_kernel(count, at_ref, *refs):
    totals, weight_refs = refs[2:4], refs[4 : 4 + count]
    kernel_ref, offset_ref, x_ref, bc_ref, steps_ref, gate_ref = refs[4 + count :]
    core = at_ref[1]
    taps = [kernel_ref[tap, pl.ds(core, 1), :] for tap in range(4)]
    offset = offset_ref[pl.ds(core, 1), :]

    def use(seq, part):
        rows = pl.ds(seq * TOK, TOK)
        part = part + totals[seq // 2][pl.ds(seq % 2 * TOK, TOK), :]
        x_ref[rows, :] = part[:, :QUARTER]
        bc_ref[rows, :] = silu(causal_conv(part[:, QUARTER:XC], taps, offset)).astype(BF16)
        steps_ref[rows, :] = part[:, XC:WIDE]
        gate_ref[rows, :] = silu(part[:, WIDE:])

    hidden_refs = [refs[seq // 2].at[pl.ds(seq % 2 * TOK, TOK), :] for seq in range(4)]
    products(hidden_refs, weight_refs, 0, use)


def last_call(at, hiddens, totals, weights, bc_kernel, bc_offset):
    return pl.pallas_call(
        functools.partial(last_kernel, len(weights)),
        out_shape=(
            jax.ShapeDtypeStruct((4 * TOK, QUARTER), F32),
            jax.ShapeDtypeStruct((4 * TOK, NST), BF16),
            jax.ShapeDtypeStruct((4 * TOK, 128), F32),
            jax.ShapeDtypeStruct((4 * TOK, QUARTER), F32),
        ),
        in_specs=[SMEM] + [VMEM] * (6 + len(weights)),
        out_specs=(VMEM,) * 4,
        compiler_params=params(40),
        cost_estimate=cost(8 * TOK * DEPTH * (WIDE + QUARTER), 8 * TOK * WIDE),
        name="last",
    )(at, *hiddens, *totals, *weights, bc_kernel, bc_offset)


def core_of(seq, refs, out_refs):
    (
        at_ref,
        skip_ref,
        bias_ref,
        decay_ref,
        length_ref,
        gate_ref,
        x_ref,
        bc_own_ref,
        bc_other_ref,
        step_ref,
        x_kernel_ref,
        x_offset_ref,
    ) = refs
    rows = slice(seq * TOK, seq * TOK + TOK)
    turned = slice((seq ^ 1) * TOK, (seq ^ 1) * TOK + TOK)
    core = at_ref[1]
    group = at_ref[2] * 2 + core
    units = pl.ds(pl.multiple_of(group * QUARTER, QUARTER), QUARTER)
    mine = core == 0
    b_act = jnp.where(mine, bc_own_ref[rows, :], bc_other_ref[turned, :])
    c_act = jnp.where(mine, bc_other_ref[turned, :], bc_own_ref[rows, :])
    x_taps = [x_kernel_ref[tap : tap + 1, units] for tap in range(4)]
    x_act = silu(causal_conv(x_ref[rows, :], x_taps, x_offset_ref[:, units])).astype(BF16)
    x_wide = x_act.astype(F32)

    head_at = lax.broadcasted_iota(jnp.int32, (8, TOK), 0)
    bias = jnp.zeros((8, TOK), F32)
    decay = jnp.zeros((8, TOK), F32)
    for head in range(HEADS):
        bias = jnp.where(head_at == head, bias_ref[group * HEADS + head], bias)
        decay = jnp.where(head_at == head, decay_ref[group * HEADS + head], decay)
    holder = ((at_ref[3] * 4 + jnp.bitwise_xor(group, seq)) * 8 + at_ref[4]) * 8
    lane = lax.broadcasted_iota(jnp.int32, (1, DEPTH), 1)
    length = jnp.sum(jnp.where(lane == holder, length_ref[HEADS : HEADS + 1, :], 0.0))
    live = lax.broadcasted_iota(jnp.int32, (8, TOK), 1).astype(F32) < length
    raw = step_ref[rows, :].T[:8] + bias
    soft = jnp.maximum(raw, 0.0) + jnp.log1p(jnp.exp(-jnp.abs(raw)))
    step = jnp.where(live, soft, 0.0)
    ends = -jnp.exp(decay) * step
    row = lax.broadcasted_iota(jnp.int32, (TOK, TOK), 0)
    col = lax.broadcasted_iota(jnp.int32, (TOK, TOK), 1)
    ones = jnp.where(row <= col, 1.0, 0.0).astype(F32)
    sums = jnp.dot(ends, ones, precision=lax.Precision.HIGHEST, preferred_element_type=F32)
    left_over = jnp.exp(sums[:, TOK - 1 :] - sums) * step
    packed = jnp.concatenate([sums, left_over, jnp.zeros((112, TOK), F32)], axis=0)
    columns = packed.T

    scores = lax.dot_general(c_act, b_act, (((1,), (1,)), ((), ())), preferred_element_type=F32)
    causal = row >= col
    low = lax.broadcasted_iota(jnp.int32, (TOK, 128), 1) < 64
    outs, weighted = [], []
    for pair in range(HEADS // 2):
        lanes = slice(pair * 128, pair * 128 + 128)
        halves = []
        for head in (2 * pair, 2 * pair + 1):
            spread = jnp.where(causal, columns[:, head : head + 1] - sums[head : head + 1, :], -1e30)
            mixing = (scores * jnp.exp(spread) * step[head : head + 1, :]).astype(BF16)
            halves.append(jnp.dot(mixing, x_act[:, lanes], preferred_element_type=F32))
        skip = jnp.where(
            low[:1], skip_ref[group * HEADS + 2 * pair], skip_ref[group * HEADS + 2 * pair + 1]
        )
        outs.append(jnp.where(low, halves[0], halves[1]) + skip * x_wide[:, lanes])
        at = 8 + 2 * pair
        weighted.append(
            x_wide[:, lanes] * jnp.where(low, columns[:, at : at + 1], columns[:, at + 1 : at + 2])
        )
    gated = jnp.concatenate(outs, axis=1) * gate_ref[rows, :]
    spread_x = jnp.concatenate(weighted, axis=1)
    state = jnp.dot(spread_x.T.astype(BF16), b_act, preferred_element_type=F32)
    if seq == 0:
        out_refs[0][...] = gated
        out_refs[1][...] = state
    else:
        out_refs[0][:, :QUARTER] = gated.astype(BF16)
        out_refs[0][:, QUARTER:] = state.astype(BF16)


def core_kernel(seqs, *refs):
    for at, seq in enumerate(seqs):
        core_of(seq, refs[:12], refs[12 + at :])


def core_call(seqs, *operands):
    shapes = [jax.ShapeDtypeStruct((TOK, QUARTER + NST), BF16) for seq in seqs if seq]
    if seqs[-1] == 0:
        shapes += [
            jax.ShapeDtypeStruct((TOK, QUARTER), F32),
            jax.ShapeDtypeStruct((QUARTER, NST), F32),
        ]
    return pl.pallas_call(
        functools.partial(core_kernel, seqs),
        out_shape=tuple(shapes),
        in_specs=[SMEM] * 4 + [VMEM] * 8,
        out_specs=(VMEM,) * len(shapes),
        compiler_params=params(40),
        cost_estimate=cost(1000, 1000),
        name="core" + "".join(str(seq) for seq in seqs),
    )(*operands)


def final_kernel(at_ref, length_ref, own_ref, state_ref, c_ref, b_ref, a_ref, gain_ref, out_ref, final_ref):
    group = at_ref[2] * 2 + at_ref[1]
    own = own_ref[...]
    squares = jnp.sum(own * own, axis=1, keepdims=True)
    parts = [(0, own)]
    for flip, ref in ((1, a_ref), (2, b_ref), (3, c_ref)):
        part = ref[:, :QUARTER].astype(F32)
        squares = squares + jnp.sum(part * part, axis=1, keepdims=True)
        parts.append((flip, part))
    live = lax.broadcasted_iota(jnp.int32, (TOK, 1), 0) < length_ref[0]
    scale = jnp.where(live, lax.rsqrt(squares * (1.0 / (4 * QUARTER)) + EPSILON), 0.0)
    for flip, part in parts:
        at = pl.ds(pl.multiple_of(jnp.bitwise_xor(group, flip) * QUARTER, QUARTER), QUARTER)
        out_ref[:, at] = (part * scale * gain_ref[:, at]).astype(BF16)
        if flip == 0:
            final_ref[at, :] = state_ref[...]
        else:
            final_ref[at, :] = (a_ref, b_ref, c_ref)[flip - 1][:, QUARTER:].astype(F32)


def final_call(at, length, own, state, got, gain):
    return pl.pallas_call(
        final_kernel,
        out_shape=(
            jax.ShapeDtypeStruct((TOK, 4 * QUARTER), BF16),
            jax.ShapeDtypeStruct((4 * QUARTER, NST), F32),
        ),
        in_specs=[SMEM, SMEM] + [VMEM] * 6,
        out_specs=(VMEM, VMEM),
        compiler_params=params(32),
        cost_estimate=cost(TOK * QUARTER * 40, TOK * QUARTER * 32),
        name="gated_norm",
    )(at, length, own, state, *got, gain)


def from_z(value, distance):
    flat = lambda z: (z % 4) * 2 + z // 4
    return lax.ppermute(
        value, ("zl", "zh"), [(flat((i + distance) % 8), flat(i)) for i in range(8)]
    )


def swap_core(value):
    return lax.ppermute(value, "core", [(0, 1), (1, 0)])


def swap_x(value):
    return lax.ppermute(value, "xb", [(0, 1), (1, 0)])


def swap_both(value):
    return lax.ppermute(value, ("xb", "core"), [(0, 3), (1, 2), (2, 1), (3, 0)])


def on_device(
    hidden,
    lengths,
    projection,
    input_gain,
    x_kernel,
    x_offset,
    bc_kernel,
    bc_offset,
    step_bias,
    decay_log,
    skip_gain,
    norm_gain,
):
    z_at = lax.axis_index("zh") * 4 + lax.axis_index("zl")
    at = jnp.stack([z_at, *(lax.axis_index(name) for name in ("core", "xb", "xa", "y"))])
    block = lax.all_to_all(
        cut_call(lengths, projection),
        ("xa", "xb", "core", "y"),
        split_axis=0,
        concat_axis=0,
        tiled=True,
    ).reshape(DEPTH, SENT)
    own = norm_call(at, hidden, input_gain.reshape(1, D))
    own_x = swap_x(own)
    other = swap_core(own)
    block, own = lax.optimization_barrier((block, own))

    together = lax.optimization_barrier
    w0, lengths_all = pack_call(block)
    w1, w7 = from_z(w0, 1), from_z(w0, -1)
    w1, w7, other = together((w1, w7, other))
    w2, w6 = from_z(w1, 1), from_z(w7, -1)
    w2, w6, own_x = together((w2, w6, own_x))
    far = swap_core(own_x)
    w3, w5 = from_z(w2, 1), from_z(w6, -1)
    early = [w0, w1, w7, w2, w6]
    near = pair_call([own, other], early, 0, None, "near")[0]
    away = pair_call([own_x, far], early, 0, None, "away")[0]
    w3, w5, near, away = together((w3, w5, near, away))
    a4, b4 = from_z(w3[:HALF], 1), from_z(w5[HALF:], -1)
    late = [w3, w5]
    near, near_last = pair_call([own, other], late, DZ_AT[3] * DEPTH, near, "near_late")
    away, away_last = pair_call([own_x, far], late, DZ_AT[3] * DEPTH, away, "away_late")
    x_cols, bc_own, steps, gate = last_call(
        at, (near_last, away_last), (near, away), (a4, b4), bc_kernel, bc_offset
    )
    bc_other = swap_core(bc_own)
    arguments = (
        at,
        skip_gain,
        step_bias,
        decay_log,
        lengths_all,
        gate,
        x_cols,
        bc_own,
        bc_other,
        steps,
        x_kernel,
        x_offset.reshape(1, 4 * QUARTER),
    )
    far_out, x_out = core_call((3, 2), *arguments)
    arguments, far_out, x_out = together((arguments, far_out, x_out))
    got_far, got_x = swap_both(far_out), swap_x(x_out)
    (other_out,) = core_call((1,), *arguments)
    arguments, other_out = together((arguments, other_out))
    got_other = swap_core(other_out)
    gated, state = core_call((0,), *arguments)
    mixer_out, final_state = final_call(
        at, lengths, gated, state, (got_far, got_x, got_other), norm_gain.reshape(1, 4 * QUARTER)
    )
    return mixer_out, final_state.reshape(1, 4 * HEADS, QUARTER // HEADS, NST)


def solution(mesh):
    names = ("xa", "xb", "zl", "core", "zh", "y")
    fine = Mesh(mesh.devices.reshape(2, 2, 4, 2, 2, 8), names)
    replica = names[:5]
    in_specs = (
        P(replica, None),
        P(replica),
        P(names, None),
        P(),
        P(None, "y"),
        P("y"),
        P(None, None, "y"),
        P(None, "y"),
        P("y"),
        P("y"),
        P("y"),
        P("y"),
    )
    out_specs = (P(replica, "y"), P(replica, "y", None, None))
    return jax.shard_map(
        on_device, mesh=fine, in_specs=in_specs, out_specs=out_specs, check_vma=False
    )
```

time: 170 us -> 155 us (0.912)
  local copies, waits for them, and re-layouts: 15.4 us -> 4.15 us
  starting transfers between devices: 69.4 us -> 62.8 us
  waiting for transfers between devices: 50.3 us -> 56.7 us
  Pallas kernels: 31.1 us -> 28.7 us
    ppermute x8, waiting for transfers between devices: 24.8 us -> 34 us  [from_z(): lax.ppermute(value, ('zl', 'zh'), [(flat((i + distance) % 8), flat(i)) fo...]
    all_to_all x1, waiting for transfers between devices: 19 us -> 13.4 us  [on_device(): lax.all_to_all(cut_call(lengths, projection), ('xa', 'xb', 'core', 'y'),...]
    ppermute x2, waiting for transfers between devices: 0.86 us -> 6.34 us  [swap_x(): return lax.ppermute(value, 'xb', [(0, 1), (1, 0)])]
    slice x8 -> x2, local copies, waits for them, and re-layouts: 4.54 us -> 0.06 us  [on_device(): a4, b4 = (from_z(w3[:HALF], 1), from_z(w5[HALF:], -1))]
    ppermute x8, starting transfers between devices: 33.4 us -> 29.6 us  [from_z(): lax.ppermute(value, ('zl', 'zh'), [(flat((i + distance) % 8), flat(i)) fo...]
    unnamed x37 -> x26, local copies, waits for them, and re-layouts: 7.62 us -> 4 us
    ppermute x4, starting transfers between devices: 16.1 us -> 13.1 us  [swap_core(): return lax.ppermute(value, 'core', [(0, 1), (1, 0)])]
    ppermute x1, waiting for transfers between devices: 4.47 us -> 1.91 us  [swap_both(): return lax.ppermute(value, ('xb', 'core'), [(0, 3), (1, 2), (2, 1), (3, 0)])]
  transfers between devices with their start and end apart: 16 -> 16, of which waited for: 9 -> 11; matrix products, arithmetic and copies ran while one was open for 3% -> 0% of each run, Pallas kernels for 13% -> 13%
where the time goes in v2:
time: 155 us; the launch traced here: 154 us
  starting transfers between devices  62.8 us (41%)
  waiting for transfers between devices  56.7 us (37%)
  Pallas kernels  28.7 us (19%)
  local copies, waits for them, and re-layouts  4.15 us (3%)
  between operations  1.66 us (1%)
    ppermute x8, waiting for transfers between devices, from_z(): lax.ppermute(value, ('zl', 'zh'), [(flat((i + distance) % 8), flat(i)) fo...  34 us
    ppermute x8, starting transfers between devices, from_z(): lax.ppermute(value, ('zl', 'zh'), [(flat((i + distance) % 8), flat(i)) fo...  29.6 us
    pallas_call x4, Pallas kernels, pair_call(): pl.pallas_call(functools.partial(pair_kernel, len(weights), first, total...  15.8 us
    all_to_all x1, waiting for transfers between devices, on_device(): lax.all_to_all(cut_call(lengths, projection), ('xa', 'xb', 'core', 'y'),...  13.4 us
    ppermute x4, starting transfers between devices, swap_core(): return lax.ppermute(value, 'core', [(0, 1), (1, 0)])  13.1 us
    all_to_all x1, starting transfers between devices, on_device(): lax.all_to_all(cut_call(lengths, projection), ('xa', 'xb', 'core', 'y'),...  11.6 us
    ppermute x2, waiting for transfers between devices, swap_x(): return lax.ppermute(value, 'xb', [(0, 1), (1, 0)])  6.34 us
    pallas_call x3, Pallas kernels, core_call(): pl.pallas_call(functools.partial(core_kernel, seqs), out_shape=tuple(shap...  6.22 us
  transfers between devices with their start and end apart: 16, of which 11 were waited for; matrix products, arithmetic and copies ran while one was open for 0% of the time, Pallas kernels for 13%

profile of v2, /device:TPU:1, one launch (start us, length us, event | category | flops | bytes accessed | tf_op | source)
XLA Modules:
  0.0 154.0 jit_solution(847187291886893098)
XLA Ops:
  1.3 0.0 copy-start.2
  1.3 1.0 copy-done.2
  2.2 1.0 cut.1
  3.2 11.6 %all-to-all-start = ((bf16[64,8,768]{2,1,0:T(8,128)(2,1)}), bf16[64,8,768]{2,1,0:T(8,128)(2,1)S(1)}, u32[]{:S(2)}, u32[]{:S(2)}) async-start(bf16[64,8,768]{2,1,0:T(8,128)(2,1)} %cut.1), calls=%async_computation | async-start | bytes 1572864 | tf_op jit(solution)/shard_map/all_to_all | solution.py:413
  14.9 0.1 stack.23.at_ref.refs_0_
  15.0 0.0 copy-done.5
  15.0 1.6 %copy-done.1 = bf16[256,4096]{1,0:T(8,128)(2,1)S(1)} copy-done((bf16[256,4096]{1,0:T(8,128)(2,1)S(1)}, bf16[256,4096]{1,0:T(8,128)(2,1)}, u32[]{:S(2)}) %copy-start.1) | copy-done | bytes 2097176
  16.6 2.0 %norm.1.refs_0_ = bf16[256,4096]{1,0:T(8,128)(2,1)S(1)} custom-call(s32[5]{0:T(128)S(1)} %stack.23.at_ref.refs_0_, bf16[256,4096]{1,0:T(8,128)(2,1)S(1)} %copy-done.1, f32[1,4096]{1,0:T(1,128)S(1)} %bitcast.14), custom_call_target="tpu_custom_call" | custom-call | flops 8388608 | bytes 4194304 | tf_op jit(solution)/shard_map/norm/pallas_call | solution.py:77
  18.6 0.0 copy-start
  18.6 2.4 %collective-permute-start.2 = (bf16[256,4096]{1,0:T(8,128)(2,1)S(1)}, bf16[256,4096]{1,0:T(8,128)(2,1)}, u32[]{:S(2)}, u32[]{:S(2)}) collective-permute-start(bf16[256,4096]{1,0:T(8,128)(2,1)S(1)} %norm.1.refs_0_), channel_id=1, source_target_pairs={{0,16},{16,0},{1,17},{17,1},{2,18},{18,2},{3,19},{19,3},{4,20},{20... | collective-permute-start | bytes 6291464 | tf_op jit(solution)/shard_map/ppermute | solution.py:386
  21.0 3.2 %collective-permute-start.5 = (bf16[256,4096]{1,0:T(8,128)(2,1)S(1)}, bf16[256,4096]{1,0:T(8,128)(2,1)}, u32[]{:S(2)}, u32[]{:S(2)}) collective-permute-start(bf16[256,4096]{1,0:T(8,128)(2,1)S(1)} %norm.1.refs_0_), channel_id=1, source_target_pairs={{0,128},{128,0},{1,129},{129,1},{2,130},{130,2},{3,131},{131,3},{4... | collective-permute-start | bytes 6291464 | tf_op jit(solution)/shard_map/ppermute | solution.py:390
  24.2 13.4 %all-to-all-done = bf16[64,8,768]{2,1,0:T(8,128)(2,1)S(1)} async-done(((bf16[64,8,768]{2,1,0:T(8,128)(2,1)}), bf16[64,8,768]{2,1,0:T(8,128)(2,1)S(1)}, u32[]{:S(2)}, u32[]{:S(2)}) %all-to-all-start) | async-done | bytes 786464 | tf_op jit(solution)/shard_map/all_to_all | solution.py:413
  37.6 0.1 pack.1
  37.7 10.7 %collective-permute-start = (bf16[528,640]{1,0:T(8,128)(2,1)S(1)}, bf16[528,640]{1,0:T(8,128)(2,1)S(1)}, u32[]{:S(2)}, u32[]{:S(2)}) collective-permute-start(bf16[528,640]{1,0:T(8,128)(2,1)S(1)} %get-tuple-element.60.refs_2_), channel_id=1, source_target_pairs={{32,0},{64,32},{96,64},{8,96},{40,8},{72,40},{104,72},{0,104},{33,... | collective-permute-start | bytes 2027528 | tf_op jit(solution)/shard_map/ppermute | solution.py:380
  48.3 1.9 %collective-permute-start.1 = (bf16[528,640]{1,0:T(8,128)(2,1)S(1)}, bf16[528,640]{1,0:T(8,128)(2,1)S(1)}, u32[]{:S(2)}, u32[]{:S(2)}) collective-permute-start(bf16[528,640]{1,0:T(8,128)(2,1)S(1)} %get-tuple-element.60.refs_2_), channel_id=1, source_target_pairs={{104,0},{0,32},{32,64},{64,96},{96,8},{8,40},{40,72},{72,104},{105... | collective-permute-start | bytes 2027528 | tf_op jit(solution)/shard_map/ppermute | solution.py:380
  50.3 0.0 collective-permute-done.2.refs_1_
  50.3 11.6 %collective-permute-done.refs_3_ = bf16[528,640]{1,0:T(8,128)(2,1)S(1)} collective-permute-done((bf16[528,640]{1,0:T(8,128)(2,1)S(1)}, bf16[528,640]{1,0:T(8,128)(2,1)S(1)}, u32[]{:S(2)}, u32[]{:S(2)}) %collective-permute-start) | collective-permute-done | bytes 675872 | tf_op jit(solution)/shard_map/ppermute | solution.py:380
  61.8 5.0 %collective-permute-done.1.refs_4_ = bf16[528,640]{1,0:T(8,128)(2,1)S(1)} collective-permute-done((bf16[528,640]{1,0:T(8,128)(2,1)S(1)}, bf16[528,640]{1,0:T(8,128)(2,1)S(1)}, u32[]{:S(2)}, u32[]{:S(2)}) %collective-permute-start.1) | collective-permute-done | bytes 675872 | tf_op jit(solution)/shard_map/ppermute | solution.py:380
  66.9 1.9 %collective-permute-start.3 = (bf16[528,640]{1,0:T(8,128)(2,1)S(1)}, bf16[528,640]{1,0:T(8,128)(2,1)S(1)}, u32[]{:S(2)}, u32[]{:S(2)}) collective-permute-start(bf16[528,640]{1,0:T(8,128)(2,1)S(1)} %collective-permute-done.refs_3_), channel_id=1, source_target_pairs={{32,0},{64,32},{96,64},{8,96},{40,8},{72,40},{104,72},{0,104},{33,... | collective-permute-start | bytes 2027528 | tf_op jit(solution)/shard_map/ppermute | solution.py:380
  68.8 3.4 %collective-permute-start.4 = (bf16[528,640]{1,0:T(8,128)(2,1)S(1)}, bf16[528,640]{1,0:T(8,128)(2,1)S(1)}, u32[]{:S(2)}, u32[]{:S(2)}) collective-permute-start(bf16[528,640]{1,0:T(8,128)(2,1)S(1)} %collective-permute-done.1.refs_4_), channel_id=1, source_target_pairs={{104,0},{0,32},{32,64},{64,96},{96,8},{8,40},{40,72},{72,104},{105... | collective-permute-start | bytes 2027528 | tf_op jit(solution)/shard_map/ppermute | solution.py:380
  72.2 2.8 %collective-permute-done.5.refs_0_ = bf16[256,4096]{1,0:T(8,128)(2,1)} collective-permute-done((bf16[256,4096]{1,0:T(8,128)(2,1)S(1)}, bf16[256,4096]{1,0:T(8,128)(2,1)}, u32[]{:S(2)}, u32[]{:S(2)}) %collective-permute-start.5) | collective-permute-done | bytes 2097184 | tf_op jit(solution)/shard_map/ppermute | solution.py:390
  74.9 8.3 %collective-permute-done.3.refs_5_ = bf16[528,640]{1,0:T(8,128)(2,1)S(1)} collective-permute-done((bf16[528,640]{1,0:T(8,128)(2,1)S(1)}, bf16[528,640]{1,0:T(8,128)(2,1)S(1)}, u32[]{:S(2)}, u32[]{:S(2)}) %collective-permute-start.3) | collective-permute-done | bytes 675872 | tf_op jit(solution)/shard_map/ppermute | solution.py:380
  83.3 3.1 %collective-permute-done.4.refs_6_ = bf16[528,640]{1,0:T(8,128)(2,1)S(1)} collective-permute-done((bf16[528,640]{1,0:T(8,128)(2,1)S(1)}, bf16[528,640]{1,0:T(8,128)(2,1)S(1)}, u32[]{:S(2)}, u32[]{:S(2)}) %collective-permute-start.4) | collective-permute-done | bytes 675872 | tf_op jit(solution)/shard_map/ppermute | solution.py:380
  86.4 5.0 %collective-permute-start.8 = (bf16[256,4096]{1,0:T(8,128)(2,1)}, bf16[256,4096]{1,0:T(8,128)(2,1)S(1)}, u32[]{:S(2)}, u32[]{:S(2)}) collective-permute-start(bf16[256,4096]{1,0:T(8,128)(2,1)} %collective-permute-done.5.refs_0_), channel_id=1, source_target_pairs={{0,16},{16,0},{1,17},{17,1},{2,18},{18,2},{3,19},{19,3},{4,20},{20... | collective-permute-start | bytes 6291464 | tf_op jit(solution)/shard_map/ppermute | solution.py:386
  91.4 1.9 %collective-permute-start.6 = (bf16[528,640]{1,0:T(8,128)(2,1)S(1)}, bf16[528,640]{1,0:T(8,128)(2,1)S(1)}, u32[]{:S(2)}, u32[]{:S(2)}) collective-permute-start(bf16[528,640]{1,0:T(8,128)(2,1)S(1)} %collective-permute-done.3.refs_5_), channel_id=1, source_target_pairs={{32,0},{64,32},{96,64},{8,96},{40,8},{72,40},{104,72},{0,104},{33,... | collective-permute-start | bytes 2027528 | tf_op jit(solution)/shard_map/ppermute | solution.py:380
  93.3 3.4 %collective-permute-start.7 = (bf16[528,640]{1,0:T(8,128)(2,1)S(1)}, bf16[528,640]{1,0:T(8,128)(2,1)S(1)}, u32[]{:S(2)}, u32[]{:S(2)}) collective-permute-start(bf16[528,640]{1,0:T(8,128)(2,1)S(1)} %collective-permute-done.4.refs_6_), channel_id=1, source_target_pairs={{104,0},{0,32},{32,64},{64,96},{96,8},{8,40},{40,72},{72,104},{105... | collective-permute-start | bytes 2027528 | tf_op jit(solution)/shard_map/ppermute | solution.py:380
  96.7 0.0 copy-done
  96.7 4.5 %near.1.refs_4_ = f32[512,768]{1,0:T(8,128)S(1)} custom-call(bf16[256,4096]{1,0:T(8,128)(2,1)} %copy-done, bf16[256,4096]{1,0:T(8,128)(2,1)} %collective-permute-done.2.refs_1_, bf16[528,640]{1,0:T(8,128)(2,1)S(1)} %get-tuple-element.60.refs_2_, bf16[528,640]{1,0:T(8,128)(2,1)S(1)} %collective-permute-done.refs_3_, ...), custom_call_target="tpu_custom_call" | custom-call | flops 2013265920 | bytes 4194304 | tf_op jit(solution)/shard_map/near/pallas_call | solution.py:182
  101.2 0.0 collective-permute-done.8.refs_1_
  101.3 0.0 copy-start.12
  101.3 1.4 copy-done.12
  102.7 4.5 %away.1.refs_4_ = f32[512,768]{1,0:T(8,128)S(1)} custom-call(bf16[256,4096]{1,0:T(8,128)(2,1)} %collective-permute-done.5.refs_0_, bf16[256,4096]{1,0:T(8,128)(2,1)} %copy-done.12, bf16[528,640]{1,0:T(8,128)(2,1)S(1)} %get-tuple-element.60.refs_2_, bf16[528,640]{1,0:T(8,128)(2,1)S(1)} %collective-permute-done.refs_3_, ...), custom_call_target="tpu_custom_call" | custom-call | flops 2013265920 | bytes 4194304 | tf_op jit(solution)/shard_map/away/pallas_call | solution.py:182
  107.2 2.9 %collective-permute-done.6.refs_2_ = bf16[528,640]{1,0:T(8,128)(2,1)S(1)} collective-permute-done((bf16[528,640]{1,0:T(8,128)(2,1)S(1)}, bf16[528,640]{1,0:T(8,128)(2,1)S(1)}, u32[]{:S(2)}, u32[]{:S(2)}) %collective-permute-start.6) | collective-permute-done | bytes 675872 | tf_op jit(solution)/shard_map/ppermute | solution.py:380
  110.1 3.1 %collective-permute-done.7.refs_3_ = bf16[528,640]{1,0:T(8,128)(2,1)S(1)} collective-permute-done((bf16[528,640]{1,0:T(8,128)(2,1)S(1)}, bf16[528,640]{1,0:T(8,128)(2,1)S(1)}, u32[]{:S(2)}, u32[]{:S(2)}) %collective-permute-start.7) | collective-permute-done | bytes 675872 | tf_op jit(solution)/shard_map/ppermute | solution.py:380
  113.2 1.9 %collective-permute-start.10 = (bf16[272,640]{1,0:T(8,128)(2,1)S(1)}, bf16[272,640]{1,0:T(8,128)(2,1)S(1)}, u32[]{:S(2)}, u32[]{:S(2)}) collective-permute-start(bf16[272,640]{1,0:T(8,128)(2,1)S(1)} %slice.7), channel_id=1, source_target_pairs={{104,0},{0,32},{32,64},{64,96},{96,8},{8,40},{40,72},{72,104},{105... | collective-permute-start | bytes 1044488 | tf_op jit(solution)/shard_map/ppermute | solution.py:380
  115.2 4.6 %collective-permute-start.9 = (bf16[256,640]{1,0:T(8,128)(2,1)S(1)}, bf16[256,640]{1,0:T(8,128)(2,1)S(1)}, u32[]{:S(2)}, u32[]{:S(2)}) collective-permute-start(bf16[256,640]{1,0:T(8,128)(2,1)S(1)} %slice.6), channel_id=1, source_target_pairs={{32,0},{64,32},{96,64},{8,96},{40,8},{72,40},{104,72},{0,104},{33,... | collective-permute-start | bytes 983048 | tf_op jit(solution)/shard_map/ppermute | solution.py:380
  119.8 3.4 %near_late.1 = (f32[512,768]{1,0:T(8,128)S(1)}, bf16[512,512]{1,0:T(8,128)(2,1)S(1)}) custom-call(bf16[256,4096]{1,0:T(8,128)(2,1)} %copy-done, bf16[256,4096]{1,0:T(8,128)(2,1)} %collective-permute-done.2.refs_1_, bf16[528,640]{1,0:T(8,128)(2,1)S(1)} %collective-permute-done.6.refs_2_, bf16[528,640]{1,0:T(8,128)(2,1)S(1)} %collective-permute-done.7.refs_3_, ...), custom_call_target="tpu_custom_call" | custom-call | flops 805306368 | bytes 4194304 | tf_op jit(solution)/shard_map/near_late/pallas_call | solution.py:182
  123.2 0.0 copy-start.10
  123.2 0.0 copy-start.11
  123.2 3.4 %away_late.1 = (f32[512,768]{1,0:T(8,128)S(1)}, bf16[512,512]{1,0:T(8,128)(2,1)S(1)}) custom-call(bf16[256,4096]{1,0:T(8,128)(2,1)} %collective-permute-done.5.refs_0_, bf16[256,4096]{1,0:T(8,128)(2,1)} %copy-done.12, bf16[528,640]{1,0:T(8,128)(2,1)S(1)} %collective-permute-done.6.refs_2_, bf16[528,640]{1,0:T(8,128)(2,1)S(1)} %collective-permute-done.7.refs_3_, ...), custom_call_target="tpu_custom_call" | custom-call | flops 805306368 | bytes 4194304 | tf_op jit(solution)/shard_map/away_late/pallas_call | solution.py:182
  126.6 0.0 collective-permute-done.9.refs_4_
  126.6 0.0 collective-permute-done.10.refs_5_
  126.6 0.0 copy-done.10
  126.6 0.0 copy-done.11
  126.6 0.0 copy-start.3
  126.6 0.0 copy-start.4
  126.6 0.0 copy-start.6
  126.7 0.0 copy-start.7
  126.7 0.0 copy-start.8
  126.7 1.7 %last.1 = (f32[1024,256]{1,0:T(8,128)S(1)}, bf16[1024,128]{1,0:T(8,128)(2,1)S(1)}, f32[1024,128]{1,0:T(8,128)S(1)}, f32[1024,256]{1,0:T(8,128)S(1)}) custom-call(s32[5]{0:T(128)S(1)} %stack.23.at_ref.refs_0_, bf16[512,512]{1,0:T(8,128)(2,1)S(1)} %get-tuple-element.70.refs_0_, bf16[512,512]{1,0:T(8,128)(2,1)S(1)} %get-tuple-element.72.refs_1_, ...), custom_call_target="tpu_custom_call" | custom-call | flops 805306368 | bytes 1048576 | tf_op jit(solution)/shard_map/last/pallas_call | solution.py:225
  128.4 3.4 %collective-permute-start.11 = (bf16[1024,128]{1,0:T(8,128)(2,1)S(1)}, bf16[1024,128]{1,0:T(8,128)(2,1)S(1)}, u32[]{:S(2)}, u32[]{:S(2)}) collective-permute-start(bf16[1024,128]{1,0:T(8,128)(2,1)S(1)} %get-tuple-element.100.refs_7_), channel_id=1, source_target_pairs={{0,16},{16,0},{1,17},{17,1},{2,18},{18,2},{3,19},{19,3},{4,20},{20... | collective-permute-start | bytes 786440 | tf_op jit(solution)/shard_map/ppermute | solution.py:386
  131.8 1.0 collective-permute-done.11.refs_8_
  132.8 0.0 copy-done.3
  132.8 2.7 %core32.1 = (bf16[256,384]{1,0:T(8,128)(2,1)S(1)}, bf16[256,384]{1,0:T(8,128)(2,1)S(1)}) custom-call(s32[5]{0:T(128)S(1)} %stack.23.at_ref.refs_0_, f32[16]{0:T(128)S(1)} %copy-done.6, f32[16]{0:T(128)S(1)} %copy-done.7, f32[16]{0:T(128)S(1)} %copy-done.8, f32[8,512]{1,0:T(8,128)S(1)} %get-tuple-element.97.refs_4_, ...), custom_call_target="tpu_custom_call" | custom-call | flops 1000 | bytes 1000 | tf_op jit(solution)/shard_map/core32/pallas_call | solution.py:332
  135.5 1.8 %core1.1 = bf16[256,384]{1,0:T(8,128)(2,1)S(1)} custom-call(s32[5]{0:T(128)S(1)} %stack.23.at_ref.refs_0_, f32[16]{0:T(128)S(1)} %copy-done.6, f32[16]{0:T(128)S(1)} %copy-done.7, f32[16]{0:T(128)S(1)} %copy-done.8, f32[8,512]{1,0:T(8,128)S(1)} %get-tuple-element.97.refs_4_, f32[1024,256]{1,0:T(8,128)S(1)} %get-tuple-element.98.refs_5_, ...), custom_call_target="tpu_custom_call" | custom-call | flops 1000 | bytes 1000 | tf_op jit(solution)/shard_map/core1/pallas_call | solution.py:332
  137.3 0.0 copy-start.9
  137.3 2.3 %collective-permute-start.14 = (bf16[256,384]{1,0:T(8,128)(2,1)S(1)}, bf16[256,384]{1,0:T(8,128)(2,1)S(1)}, u32[]{:S(2)}, u32[]{:S(2)}) collective-permute-start(bf16[256,384]{1,0:T(8,128)(2,1)S(1)} %core1.1), channel_id=1, source_target_pairs={{0,16},{16,0},{1,17},{17,1},{2,18},{18,2},{3,19},{19,3},{4,20},{20... | collective-permute-start | bytes 589832 | tf_op jit(solution)/shard_map/ppermute | solution.py:386
  139.6 2.3 %collective-permute-start.12 = (bf16[256,384]{1,0:T(8,128)(2,1)S(1)}, bf16[256,384]{1,0:T(8,128)(2,1)S(1)}, u32[]{:S(2)}, u32[]{:S(2)}) collective-permute-start(bf16[256,384]{1,0:T(8,128)(2,1)S(1)} %get-tuple-element.107), channel_id=1, source_target_pairs={{0,144},{16,128},{128,16},{144,0},{1,145},{17,129},{129,17},{145,1... | collective-permute-start | bytes 589832 | tf_op jit(solution)/shard_map/ppermute | solution.py:394
  141.9 3.0 %collective-permute-start.13 = (bf16[256,384]{1,0:T(8,128)(2,1)S(1)}, bf16[256,384]{1,0:T(8,128)(2,1)S(1)}, u32[]{:S(2)}, u32[]{:S(2)}) collective-permute-start(bf16[256,384]{1,0:T(8,128)(2,1)S(1)} %get-tuple-element.108), channel_id=1, source_target_pairs={{0,128},{128,0},{1,129},{129,1},{2,130},{130,2},{3,131},{131,3},{4... | collective-permute-start | bytes 589832 | tf_op jit(solution)/shard_map/ppermute | solution.py:390
  144.9 1.8 %core0.1 = (f32[256,256]{1,0:T(8,128)S(1)}, f32[256,128]{1,0:T(8,128)S(1)}) custom-call(s32[5]{0:T(128)S(1)} %stack.23.at_ref.refs_0_, f32[16]{0:T(128)S(1)} %copy-done.6, f32[16]{0:T(128)S(1)} %copy-done.7, f32[16]{0:T(128)S(1)} %copy-done.8, f32[8,512]{1,0:T(8,128)S(1)} %get-tuple-element.97.refs_4_, f32[1024,256]{1,0:T(8,128)S(1)} %get-tuple-element.98.refs_5_, ...), custom_call_target="tpu_custom_call" | custom-call | flops 1000 | bytes 1000 | tf_op jit(solution)/shard_map/core0/pallas_call | solution.py:332
  146.7 0.0 collective-permute-done.14.a_ref
  146.7 1.9 %collective-permute-done.12.c_ref = bf16[256,384]{1,0:T(8,128)(2,1)S(1)} collective-permute-done((bf16[256,384]{1,0:T(8,128)(2,1)S(1)}, bf16[256,384]{1,0:T(8,128)(2,1)S(1)}, u32[]{:S(2)}, u32[]{:S(2)}) %collective-permute-start.12) | collective-permute-done | bytes 196640 | tf_op jit(solution)/shard_map/ppermute | solution.py:394
  148.6 3.6 %collective-permute-done.13.b_ref = bf16[256,384]{1,0:T(8,128)(2,1)S(1)} collective-permute-done((bf16[256,384]{1,0:T(8,128)(2,1)S(1)}, bf16[256,384]{1,0:T(8,128)(2,1)S(1)}, u32[]{:S(2)}, u32[]{:S(2)}) %collective-permute-start.13) | collective-permute-done | bytes 196640 | tf_op jit(solution)/shard_map/ppermute | solution.py:390
  152.2 1.9 %gated_norm.1 = (bf16[256,1024]{1,0:T(8,128)(2,1)}, f32[1024,128]{1,0:T(8,128)}) custom-call(s32[5]{0:T(128)S(1)} %stack.23.at_ref.refs_0_, s32[1]{0:T(128)S(6)} %copy.14.length_ref, f32[256,256]{1,0:T(8,128)S(1)} %get-tuple-element.105.own_ref, f32[256,128]{1,0:T(8,128)S(1)} %get-tuple-element.106.state_ref, ...), custom_call_target="tpu_custom_call" | custom-call | flops 2621440 | bytes 2097152 | tf_op jit(solution)/shard_map/gated_norm/pallas_call | solution.py:364
  (9 shorter events, 0.1 us)
Async XLA Ops:
  1.3 1.0 copy-start.2
  2.2 12.7 %copy-start.5 = (f32[4096]{0:T(1024)S(1)}, f32[4096]{0:T(1024)}, u32[]{:S(2)}) copy-start(f32[4096]{0:T(1024)} %param.15) | copy-start | bytes 49156
  3.2 34.4 %all-to-all-start = ((bf16[64,8,768]{2,1,0:T(8,128)(2,1)}), bf16[64,8,768]{2,1,0:T(8,128)(2,1)S(1)}, u32[]{:S(2)}, u32[]{:S(2)}) async-start(bf16[64,8,768]{2,1,0:T(8,128)(2,1)} %cut.1), calls=%async_computation | async-start | bytes 1572864 | tf_op jit(solution)/shard_map/all_to_all | solution.py:413
  15.0 1.6 %copy-start.1 = (bf16[256,4096]{1,0:T(8,128)(2,1)S(1)}, bf16[256,4096]{1,0:T(8,128)(2,1)}, u32[]{:S(2)}) copy-start(bf16[256,4096]{1,0:T(8,128)(2,1)} %hidden_ref.1) | copy-start | bytes 6291460
  18.6 78.1 %copy-start = (bf16[256,4096]{1,0:T(8,128)(2,1)}, bf16[256,4096]{1,0:T(8,128)(2,1)S(1)}, u32[]{:S(2)}) copy-start(bf16[256,4096]{1,0:T(8,128)(2,1)S(1)} %norm.1.refs_0_) | copy-start | bytes 6291460
  18.6 31.7 %collective-permute-start.2 = (bf16[256,4096]{1,0:T(8,128)(2,1)S(1)}, bf16[256,4096]{1,0:T(8,128)(2,1)}, u32[]{:S(2)}, u32[]{:S(2)}) collective-permute-start(bf16[256,4096]{1,0:T(8,128)(2,1)S(1)} %norm.1.refs_0_), channel_id=1, source_target_pairs={{0,16},{16,0},{1,17},{17,1},{2,18},{18,2},{3,19},{19,3},{4,20},{20... | collective-permute-start | bytes 6291464 | tf_op jit(solution)/shard_map/ppermute | solution.py:386
  21.0 54.0 %collective-permute-start.5 = (bf16[256,4096]{1,0:T(8,128)(2,1)S(1)}, bf16[256,4096]{1,0:T(8,128)(2,1)}, u32[]{:S(2)}, u32[]{:S(2)}) collective-permute-start(bf16[256,4096]{1,0:T(8,128)(2,1)S(1)} %norm.1.refs_0_), channel_id=1, source_target_pairs={{0,128},{128,0},{1,129},{129,1},{2,130},{130,2},{3,131},{131,3},{4... | collective-permute-start | bytes 6291464 | tf_op jit(solution)/shard_map/ppermute | solution.py:390
  37.7 24.2 %collective-permute-start = (bf16[528,640]{1,0:T(8,128)(2,1)S(1)}, bf16[528,640]{1,0:T(8,128)(2,1)S(1)}, u32[]{:S(2)}, u32[]{:S(2)}) collective-permute-start(bf16[528,640]{1,0:T(8,128)(2,1)S(1)} %get-tuple-element.60.refs_2_), channel_id=1, source_target_pairs={{32,0},{64,32},{96,64},{8,96},{40,8},{72,40},{104,72},{0,104},{33,... | collective-permute-start | bytes 2027528 | tf_op jit(solution)/shard_map/ppermute | solution.py:380
  48.3 18.5 %collective-permute-start.1 = (bf16[528,640]{1,0:T(8,128)(2,1)S(1)}, bf16[528,640]{1,0:T(8,128)(2,1)S(1)}, u32[]{:S(2)}, u32[]{:S(2)}) collective-permute-start(bf16[528,640]{1,0:T(8,128)(2,1)S(1)} %get-tuple-element.60.refs_2_), channel_id=1, source_target_pairs={{104,0},{0,32},{32,64},{64,96},{96,8},{8,40},{40,72},{72,104},{105... | collective-permute-start | bytes 2027528 | tf_op jit(solution)/shard_map/ppermute | solution.py:380
  66.9 16.4 %collective-permute-start.3 = (bf16[528,640]{1,0:T(8,128)(2,1)S(1)}, bf16[528,640]{1,0:T(8,128)(2,1)S(1)}, u32[]{:S(2)}, u32[]{:S(2)}) collective-permute-start(bf16[528,640]{1,0:T(8,128)(2,1)S(1)} %collective-permute-done.refs_3_), channel_id=1, source_target_pairs={{32,0},{64,32},{96,64},{8,96},{40,8},{72,40},{104,72},{0,104},{33,... | collective-permute-start | bytes 2027528 | tf_op jit(solution)/shard_map/ppermute | solution.py:380
  68.8 17.6 %collective-permute-start.4 = (bf16[528,640]{1,0:T(8,128)(2,1)S(1)}, bf16[528,640]{1,0:T(8,128)(2,1)S(1)}, u32[]{:S(2)}, u32[]{:S(2)}) collective-permute-start(bf16[528,640]{1,0:T(8,128)(2,1)S(1)} %collective-permute-done.1.refs_4_), channel_id=1, source_target_pairs={{104,0},{0,32},{32,64},{64,96},{96,8},{8,40},{40,72},{72,104},{105... | collective-permute-start | bytes 2027528 | tf_op jit(solution)/shard_map/ppermute | solution.py:380
  86.4 14.9 %collective-permute-start.8 = (bf16[256,4096]{1,0:T(8,128)(2,1)}, bf16[256,4096]{1,0:T(8,128)(2,1)S(1)}, u32[]{:S(2)}, u32[]{:S(2)}) collective-permute-start(bf16[256,4096]{1,0:T(8,128)(2,1)} %collective-permute-done.5.refs_0_), channel_id=1, source_target_pairs={{0,16},{16,0},{1,17},{17,1},{2,18},{18,2},{3,19},{19,3},{4,20},{20... | collective-permute-start | bytes 6291464 | tf_op jit(solution)/shard_map/ppermute | solution.py:386
  91.4 18.7 %collective-permute-start.6 = (bf16[528,640]{1,0:T(8,128)(2,1)S(1)}, bf16[528,640]{1,0:T(8,128)(2,1)S(1)}, u32[]{:S(2)}, u32[]{:S(2)}) collective-permute-start(bf16[528,640]{1,0:T(8,128)(2,1)S(1)} %collective-permute-done.3.refs_5_), channel_id=1, source_target_pairs={{32,0},{64,32},{96,64},{8,96},{40,8},{72,40},{104,72},{0,104},{33,... | collective-permute-start | bytes 2027528 | tf_op jit(solution)/shard_map/ppermute | solution.py:380
  93.3 19.9 %collective-permute-start.7 = (bf16[528,640]{1,0:T(8,128)(2,1)S(1)}, bf16[528,640]{1,0:T(8,128)(2,1)S(1)}, u32[]{:S(2)}, u32[]{:S(2)}) collective-permute-start(bf16[528,640]{1,0:T(8,128)(2,1)S(1)} %collective-permute-done.4.refs_6_), channel_id=1, source_target_pairs={{104,0},{0,32},{32,64},{64,96},{96,8},{8,40},{40,72},{72,104},{105... | collective-permute-start | bytes 2027528 | tf_op jit(solution)/shard_map/ppermute | solution.py:380
  101.3 1.4 copy-start.12
  113.2 13.4 %collective-permute-start.10 = (bf16[272,640]{1,0:T(8,128)(2,1)S(1)}, bf16[272,640]{1,0:T(8,128)(2,1)S(1)}, u32[]{:S(2)}, u32[]{:S(2)}) collective-permute-start(bf16[272,640]{1,0:T(8,128)(2,1)S(1)} %slice.7), channel_id=1, source_target_pairs={{104,0},{0,32},{32,64},{64,96},{96,8},{8,40},{40,72},{72,104},{105... | collective-permute-start | bytes 1044488 | tf_op jit(solution)/shard_map/ppermute | solution.py:380
  115.2 11.4 %collective-permute-start.9 = (bf16[256,640]{1,0:T(8,128)(2,1)S(1)}, bf16[256,640]{1,0:T(8,128)(2,1)S(1)}, u32[]{:S(2)}, u32[]{:S(2)}) collective-permute-start(bf16[256,640]{1,0:T(8,128)(2,1)S(1)} %slice.6), channel_id=1, source_target_pairs={{32,0},{64,32},{96,64},{8,96},{40,8},{72,40},{104,72},{0,104},{33,... | collective-permute-start | bytes 983048 | tf_op jit(solution)/shard_map/ppermute | solution.py:380
  123.2 3.4 %copy-start.10 = (f32[4,2,128]{2,1,0:T(2,128)S(1)}, f32[4,2,128]{2,1,0:T(2,128)}, u32[]{:S(2)}) copy-start(f32[4,2,128]{2,1,0:T(2,128)} %refs_6_.1) | copy-start | bytes 12292
  123.2 3.4 %copy-start.11 = (f32[2,128]{1,0:T(2,128)S(1)}, f32[2,128]{1,0:T(2,128)}, u32[]{:S(2)}) copy-start(f32[2,128]{1,0:T(2,128)} %refs_7_.1) | copy-start | bytes 3076
  126.6 6.2 %copy-start.3 = (f32[4,1024]{1,0:T(4,128)S(1)}, f32[4,1024]{1,0:T(4,128)}, u32[]{:S(2)}) copy-start(f32[4,1024]{1,0:T(4,128)} %refs_10_.3) | copy-start | bytes 49156
  126.6 6.1 %copy-start.4 = (f32[1024]{0:T(1024)S(1)}, f32[1024]{0:T(1024)}, u32[]{:S(2)}) copy-start(f32[1024]{0:T(1024)} %param.17) | copy-start | bytes 12292
  126.6 6.1 %copy-start.6 = (f32[16]{0:T(128)S(1)}, f32[16]{0:T(128)}, u32[]{:S(2)}) copy-start(f32[16]{0:T(128)} %refs_1_.3) | copy-start | bytes 196
  126.7 6.1 %copy-start.7 = (f32[16]{0:T(128)S(1)}, f32[16]{0:T(128)}, u32[]{:S(2)}) copy-start(f32[16]{0:T(128)} %refs_2_.3) | copy-start | bytes 196
  126.7 6.1 %copy-start.8 = (f32[16]{0:T(128)S(1)}, f32[16]{0:T(128)}, u32[]{:S(2)}) copy-start(f32[16]{0:T(128)} %refs_3_.3) | copy-start | bytes 196
  128.4 4.4 %collective-permute-start.11 = (bf16[1024,128]{1,0:T(8,128)(2,1)S(1)}, bf16[1024,128]{1,0:T(8,128)(2,1)S(1)}, u32[]{:S(2)}, u32[]{:S(2)}) collective-permute-start(bf16[1024,128]{1,0:T(8,128)(2,1)S(1)} %get-tuple-element.100.refs_7_), channel_id=1, source_target_pairs={{0,16},{16,0},{1,17},{17,1},{2,18},{18,2},{3,19},{19,3},{4,20},{20... | collective-permute-start | bytes 786440 | tf_op jit(solution)/shard_map/ppermute | solution.py:386
  137.3 14.9 %copy-start.9 = (f32[1024]{0:T(1024)S(1)}, f32[1024]{0:T(1024)}, u32[]{:S(2)}) copy-start(f32[1024]{0:T(1024)} %param.23) | copy-start | bytes 12292
  137.3 9.4 %collective-permute-start.14 = (bf16[256,384]{1,0:T(8,128)(2,1)S(1)}, bf16[256,384]{1,0:T(8,128)(2,1)S(1)}, u32[]{:S(2)}, u32[]{:S(2)}) collective-permute-start(bf16[256,384]{1,0:T(8,128)(2,1)S(1)} %core1.1), channel_id=1, source_target_pairs={{0,16},{16,0},{1,17},{17,1},{2,18},{18,2},{3,19},{19,3},{4,20},{20... | collective-permute-start | bytes 589832 | tf_op jit(solution)/shard_map/ppermute | solution.py:386
  139.6 9.0 %collective-permute-start.12 = (bf16[256,384]{1,0:T(8,128)(2,1)S(1)}, bf16[256,384]{1,0:T(8,128)(2,1)S(1)}, u32[]{:S(2)}, u32[]{:S(2)}) collective-permute-start(bf16[256,384]{1,0:T(8,128)(2,1)S(1)} %get-tuple-element.107), channel_id=1, source_target_pairs={{0,144},{16,128},{128,16},{144,0},{1,145},{17,129},{129,17},{145,1... | collective-permute-start | bytes 589832 | tf_op jit(solution)/shard_map/ppermute | solution.py:394
  141.9 10.3 %collective-permute-start.13 = (bf16[256,384]{1,0:T(8,128)(2,1)S(1)}, bf16[256,384]{1,0:T(8,128)(2,1)S(1)}, u32[]{:S(2)}, u32[]{:S(2)}) collective-permute-start(bf16[256,384]{1,0:T(8,128)(2,1)S(1)} %get-tuple-element.108), channel_id=1, source_target_pairs={{0,128},{128,0},{1,129},{129,1},{2,130},{130,2},{3,131},{131,3},{4... | collective-permute-start | bytes 589832 | tf_op jit(solution)/shard_map/ppermute | solution.py:390

commit v3 on v2

--- a/solution.py
+++ b/solution.py
@@ -281,23 +281,38 @@
     ends = -jnp.exp(decay) * step
     row = lax.broadcasted_iota(jnp.int32, (TOK, TOK), 0)
     col = lax.broadcasted_iota(jnp.int32, (TOK, TOK), 1)
-    ones = jnp.where(row <= col, 1.0, 0.0).astype(F32)
-    sums = jnp.dot(ends, ones, precision=lax.Precision.HIGHEST, preferred_element_type=F32)
+    ones = jnp.where(row <= col, 1.0, 0.0).astype(BF16)
+    high = ends.astype(BF16)
+    rest = ends - high.astype(F32)
+    middle = rest.astype(BF16)
+    lowest = (rest - middle.astype(F32)).astype(BF16)
+    split = jnp.concatenate([part.astype(F32) for part in (high, middle, lowest)], axis=0)
+    summed = jnp.dot(split.astype(BF16), ones, preferred_element_type=F32)
+    sums = summed[:8] + summed[8:16] + summed[16:]
     left_over = jnp.exp(sums[:, TOK - 1 :] - sums) * step
     packed = jnp.concatenate([sums, left_over, jnp.zeros((112, TOK), F32)], axis=0)
     columns = packed.T
 
     scores = lax.dot_general(c_act, b_act, (((1,), (1,)), ((), ())), preferred_element_type=F32)
-    causal = row >= col
+    half = TOK // 2
+    causal = (row >= col)[:half, :half]
     low = lax.broadcasted_iota(jnp.int32, (TOK, 128), 1) < 64
     outs, weighted = [], []
     for pair in range(HEADS // 2):
         lanes = slice(pair * 128, pair * 128 + 128)
         halves = []
         for head in (2 * pair, 2 * pair + 1):
-            spread = jnp.where(causal, columns[:, head : head + 1] - sums[head : head + 1, :], -1e30)
-            mixing = (scores * jnp.exp(spread) * step[head : head + 1, :]).astype(BF16)
-            halves.append(jnp.dot(mixing, x_act[:, lanes], preferred_element_type=F32))
+            def quarter(t_at, u_at):
+                t, u = slice(t_at, t_at + half), slice(u_at, u_at + half)
+                spread = columns[t, head : head + 1] - sums[head : head + 1, u]
+                if t_at == u_at:
+                    spread = jnp.where(causal, spread, -1e30)
+                return (scores[t, u] * jnp.exp(spread) * step[head : head + 1, u]).astype(BF16)
+
+            first = jnp.dot(quarter(0, 0), x_act[:half, lanes], preferred_element_type=F32)
+            mixing = jnp.concatenate([quarter(half, 0), quarter(half, half)], axis=1)
+            second = jnp.dot(mixing, x_act[:, lanes], preferred_element_type=F32)
+            halves.append(jnp.concatenate([first, second], axis=0))
         skip = jnp.where(
             low[:1], skip_ref[group * HEADS + 2 * pair], skip_ref[group * HEADS + 2 * pair + 1]
         )
@@ -335,12 +350,12 @@
         in_specs=[SMEM] * 4 + [VMEM] * 8,
         out_specs=(VMEM,) * len(shapes),
         compiler_params=params(40),
-        cost_estimate=cost(1000, 1000),
+        cost_estimate=cost(len(seqs) * 8 * TOK * TOK * 200, len(seqs) * 8 * TOK * QUARTER),
         name="core" + "".join(str(seq) for seq in seqs),
     )(*operands)
 
 
-def final_kernel(at_ref, length_ref, own_ref, state_ref, c_ref, b_ref, a_ref, gain_ref, out_ref, final_ref):
+def final_kernel(at_ref, length_ref, own_ref, state_ref, a_ref, b_ref, c_ref, gain_ref, out_ref, final_ref):
     group = at_ref[2] * 2 + at_ref[1]
     own = own_ref[...]
     squares = jnp.sum(own * own, axis=1, keepdims=True)
@@ -456,15 +471,12 @@
         x_kernel,
         x_offset.reshape(1, 4 * QUARTER),
     )
-    far_out, x_out = core_call((3, 2), *arguments)
-    arguments, far_out, x_out = together((arguments, far_out, x_out))
-    got_far, got_x = swap_both(far_out), swap_x(x_out)
-    (other_out,) = core_call((1,), *arguments)
-    arguments, other_out = together((arguments, other_out))
-    got_other = swap_core(other_out)
+    got_far = swap_both(core_call((3,), *arguments)[0])
+    got_x = swap_x(core_call((2,), *arguments)[0])
+    got_other = swap_core(core_call((1,), *arguments)[0])
     gated, state = core_call((0,), *arguments)
     mixer_out, final_state = final_call(
-        at, lengths, gated, state, (got_far, got_x, got_other), norm_gain.reshape(1, 4 * QUARTER)
+        at, lengths, gated, state, (got_other, got_x, got_far), norm_gain.reshape(1, 4 * QUARTER)
     )
     return mixer_out, final_state.reshape(1, 4 * HEADS, QUARTER // HEADS, NST)
 

time: 155 us -> 150 us (0.968)
  waiting for transfers between devices: 56.7 us -> 51.5 us
    ppermute x2, waiting for transfers between devices: 6.34 us -> 3.02 us  [swap_x(): return lax.ppermute(value, 'xb', [(0, 1), (1, 0)])]
    ppermute x1, waiting for transfers between devices: 1.91 us -> 0.01 us  [swap_both(): return lax.ppermute(value, ('xb', 'core'), [(0, 3), (1, 2), (2, 1), (3, 0)])]
    pallas_call x3 -> x4, Pallas kernels: 6.22 us -> 6.4 us  [core_call(): pl.pallas_call(functools.partial(core_kernel, seqs), out_shape=tuple(shap...]
  transfers between devices with their start and end apart: 16 -> 16, of which waited for: 11 -> 10; matrix products, arithmetic and copies ran while one was open for 0% -> 0% of each run, Pallas kernels for 13% -> 15%
where the time goes in v3:
time: 150 us; the launch traced here: 149 us
  starting transfers between devices  63.1 us (42%)
  waiting for transfers between devices  51.5 us (34%)
  Pallas kernels  28.9 us (19%)
  local copies, waits for them, and re-layouts  4.13 us (3%)
  between operations  1.66 us (1%)
    ppermute x8, waiting for transfers between devices, from_z(): lax.ppermute(value, ('zl', 'zh'), [(flat((i + distance) % 8), flat(i)) fo...  34.1 us
    ppermute x8, starting transfers between devices, from_z(): lax.ppermute(value, ('zl', 'zh'), [(flat((i + distance) % 8), flat(i)) fo...  29.6 us
    pallas_call x4, Pallas kernels, pair_call(): pl.pallas_call(functools.partial(pair_kernel, len(weights), first, total...  15.8 us
    all_to_all x1, waiting for transfers between devices, on_device(): lax.all_to_all(cut_call(lengths, projection), ('xa', 'xb', 'core', 'y'),...  13.4 us
    ppermute x4, starting transfers between devices, swap_core(): return lax.ppermute(value, 'core', [(0, 1), (1, 0)])  13.1 us
    all_to_all x1, starting transfers between devices, on_device(): lax.all_to_all(cut_call(lengths, projection), ('xa', 'xb', 'core', 'y'),...  11.6 us
    pallas_call x4, Pallas kernels, core_call(): pl.pallas_call(functools.partial(core_kernel, seqs), out_shape=tuple(shap...  6.4 us
    ppermute x2, starting transfers between devices, swap_x(): return lax.ppermute(value, 'xb', [(0, 1), (1, 0)])  6.21 us
  transfers between devices with their start and end apart: 16, of which 10 were waited for; matrix products, arithmetic and copies ran while one was open for 0% of the time, Pallas kernels for 15%

profile of v3, /device:TPU:1, one launch (start us, length us, event | category | flops | bytes accessed | tf_op | source)
XLA Modules:
  0.0 149.2 jit_solution(12178922173596735660)
XLA Ops:
  1.3 0.0 copy-start.2
  1.3 1.0 copy-done.2
  2.2 1.0 cut.1
  3.2 11.6 %all-to-all-start = ((bf16[64,8,768]{2,1,0:T(8,128)(2,1)}), bf16[64,8,768]{2,1,0:T(8,128)(2,1)S(1)}, u32[]{:S(2)}, u32[]{:S(2)}) async-start(bf16[64,8,768]{2,1,0:T(8,128)(2,1)} %cut.1), calls=%async_computation | async-start | bytes 1572864 | tf_op jit(solution)/shard_map/all_to_all | solution.py:428
  14.9 0.1 stack.23.at_ref.refs_0_
  14.9 0.0 copy-done.5
  15.0 1.6 %copy-done.1 = bf16[256,4096]{1,0:T(8,128)(2,1)S(1)} copy-done((bf16[256,4096]{1,0:T(8,128)(2,1)S(1)}, bf16[256,4096]{1,0:T(8,128)(2,1)}, u32[]{:S(2)}) %copy-start.1) | copy-done | bytes 2097176
  16.5 2.0 %norm.1.refs_0_ = bf16[256,4096]{1,0:T(8,128)(2,1)S(1)} custom-call(s32[5]{0:T(128)S(1)} %stack.23.at_ref.refs_0_, bf16[256,4096]{1,0:T(8,128)(2,1)S(1)} %copy-done.1, f32[1,4096]{1,0:T(1,128)S(1)} %bitcast.15), custom_call_target="tpu_custom_call" | custom-call | flops 8388608 | bytes 4194304 | tf_op jit(solution)/shard_map/norm/pallas_call | solution.py:77
  18.6 2.4 %collective-permute-start.2 = (bf16[256,4096]{1,0:T(8,128)(2,1)S(1)}, bf16[256,4096]{1,0:T(8,128)(2,1)}, u32[]{:S(2)}, u32[]{:S(2)}) collective-permute-start(bf16[256,4096]{1,0:T(8,128)(2,1)S(1)} %norm.1.refs_0_), channel_id=1, source_target_pairs={{0,16},{16,0},{1,17},{17,1},{2,18},{18,2},{3,19},{19,3},{4,20},{20... | collective-permute-start | bytes 6291464 | tf_op jit(solution)/shard_map/ppermute | solution.py:401
  21.0 3.2 %collective-permute-start.5 = (bf16[256,4096]{1,0:T(8,128)(2,1)S(1)}, bf16[256,4096]{1,0:T(8,128)(2,1)}, u32[]{:S(2)}, u32[]{:S(2)}) collective-permute-start(bf16[256,4096]{1,0:T(8,128)(2,1)S(1)} %norm.1.refs_0_), channel_id=1, source_target_pairs={{0,128},{128,0},{1,129},{129,1},{2,130},{130,2},{3,131},{131,3},{4... | collective-permute-start | bytes 6291464 | tf_op jit(solution)/shard_map/ppermute | solution.py:405
  24.2 13.4 %all-to-all-done = bf16[64,8,768]{2,1,0:T(8,128)(2,1)S(1)} async-done(((bf16[64,8,768]{2,1,0:T(8,128)(2,1)}), bf16[64,8,768]{2,1,0:T(8,128)(2,1)S(1)}, u32[]{:S(2)}, u32[]{:S(2)}) %all-to-all-start) | async-done | bytes 786464 | tf_op jit(solution)/shard_map/all_to_all | solution.py:428
  37.6 0.1 pack.1
  37.7 10.7 %collective-permute-start = (bf16[528,640]{1,0:T(8,128)(2,1)S(1)}, bf16[528,640]{1,0:T(8,128)(2,1)S(1)}, u32[]{:S(2)}, u32[]{:S(2)}) collective-permute-start(bf16[528,640]{1,0:T(8,128)(2,1)S(1)} %get-tuple-element.31.refs_2_), channel_id=1, source_target_pairs={{32,0},{64,32},{96,64},{8,96},{40,8},{72,40},{104,72},{0,104},{33,... | collective-permute-start | bytes 2027528 | tf_op jit(solution)/shard_map/ppermute | solution.py:395
  48.3 1.9 %collective-permute-start.1 = (bf16[528,640]{1,0:T(8,128)(2,1)S(1)}, bf16[528,640]{1,0:T(8,128)(2,1)S(1)}, u32[]{:S(2)}, u32[]{:S(2)}) collective-permute-start(bf16[528,640]{1,0:T(8,128)(2,1)S(1)} %get-tuple-element.31.refs_2_), channel_id=1, source_target_pairs={{104,0},{0,32},{32,64},{64,96},{96,8},{8,40},{40,72},{72,104},{105... | collective-permute-start | bytes 2027528 | tf_op jit(solution)/shard_map/ppermute | solution.py:395
  50.3 0.0 collective-permute-done.2.refs_1_
  50.3 11.6 %collective-permute-done.refs_3_ = bf16[528,640]{1,0:T(8,128)(2,1)S(1)} collective-permute-done((bf16[528,640]{1,0:T(8,128)(2,1)S(1)}, bf16[528,640]{1,0:T(8,128)(2,1)S(1)}, u32[]{:S(2)}, u32[]{:S(2)}) %collective-permute-start) | collective-permute-done | bytes 675872 | tf_op jit(solution)/shard_map/ppermute | solution.py:395
  61.8 5.0 %collective-permute-done.1.refs_4_ = bf16[528,640]{1,0:T(8,128)(2,1)S(1)} collective-permute-done((bf16[528,640]{1,0:T(8,128)(2,1)S(1)}, bf16[528,640]{1,0:T(8,128)(2,1)S(1)}, u32[]{:S(2)}, u32[]{:S(2)}) %collective-permute-start.1) | collective-permute-done | bytes 675872 | tf_op jit(solution)/shard_map/ppermute | solution.py:395
  66.9 1.9 %collective-permute-start.3 = (bf16[528,640]{1,0:T(8,128)(2,1)S(1)}, bf16[528,640]{1,0:T(8,128)(2,1)S(1)}, u32[]{:S(2)}, u32[]{:S(2)}) collective-permute-start(bf16[528,640]{1,0:T(8,128)(2,1)S(1)} %collective-permute-done.refs_3_), channel_id=1, source_target_pairs={{32,0},{64,32},{96,64},{8,96},{40,8},{72,40},{104,72},{0,104},{33,... | collective-permute-start | bytes 2027528 | tf_op jit(solution)/shard_map/ppermute | solution.py:395
  68.8 3.4 %collective-permute-start.4 = (bf16[528,640]{1,0:T(8,128)(2,1)S(1)}, bf16[528,640]{1,0:T(8,128)(2,1)S(1)}, u32[]{:S(2)}, u32[]{:S(2)}) collective-permute-start(bf16[528,640]{1,0:T(8,128)(2,1)S(1)} %collective-permute-done.1.refs_4_), channel_id=1, source_target_pairs={{104,0},{0,32},{32,64},{64,96},{96,8},{8,40},{40,72},{72,104},{105... | collective-permute-start | bytes 2027528 | tf_op jit(solution)/shard_map/ppermute | solution.py:395
  72.1 2.8 %collective-permute-done.5.refs_0_ = bf16[256,4096]{1,0:T(8,128)(2,1)} collective-permute-done((bf16[256,4096]{1,0:T(8,128)(2,1)S(1)}, bf16[256,4096]{1,0:T(8,128)(2,1)}, u32[]{:S(2)}, u32[]{:S(2)}) %collective-permute-start.5) | collective-permute-done | bytes 2097184 | tf_op jit(solution)/shard_map/ppermute | solution.py:405
  74.9 8.3 %collective-permute-done.3.refs_5_ = bf16[528,640]{1,0:T(8,128)(2,1)S(1)} collective-permute-done((bf16[528,640]{1,0:T(8,128)(2,1)S(1)}, bf16[528,640]{1,0:T(8,128)(2,1)S(1)}, u32[]{:S(2)}, u32[]{:S(2)}) %collective-permute-start.3) | collective-permute-done | bytes 675872 | tf_op jit(solution)/shard_map/ppermute | solution.py:395
  83.2 3.1 %collective-permute-done.4.refs_6_ = bf16[528,640]{1,0:T(8,128)(2,1)S(1)} collective-permute-done((bf16[528,640]{1,0:T(8,128)(2,1)S(1)}, bf16[528,640]{1,0:T(8,128)(2,1)S(1)}, u32[]{:S(2)}, u32[]{:S(2)}) %collective-permute-start.4) | collective-permute-done | bytes 675872 | tf_op jit(solution)/shard_map/ppermute | solution.py:395
  86.4 5.0 %collective-permute-start.8 = (bf16[256,4096]{1,0:T(8,128)(2,1)}, bf16[256,4096]{1,0:T(8,128)(2,1)S(1)}, u32[]{:S(2)}, u32[]{:S(2)}) collective-permute-start(bf16[256,4096]{1,0:T(8,128)(2,1)} %collective-permute-done.5.refs_0_), channel_id=1, source_target_pairs={{0,16},{16,0},{1,17},{17,1},{2,18},{18,2},{3,19},{19,3},{4,20},{20... | collective-permute-start | bytes 6291464 | tf_op jit(solution)/shard_map/ppermute | solution.py:401
  91.4 1.9 %collective-permute-start.6 = (bf16[528,640]{1,0:T(8,128)(2,1)S(1)}, bf16[528,640]{1,0:T(8,128)(2,1)S(1)}, u32[]{:S(2)}, u32[]{:S(2)}) collective-permute-start(bf16[528,640]{1,0:T(8,128)(2,1)S(1)} %collective-permute-done.3.refs_5_), channel_id=1, source_target_pairs={{32,0},{64,32},{96,64},{8,96},{40,8},{72,40},{104,72},{0,104},{33,... | collective-permute-start | bytes 2027528 | tf_op jit(solution)/shard_map/ppermute | solution.py:395
  93.3 3.4 %collective-permute-start.7 = (bf16[528,640]{1,0:T(8,128)(2,1)S(1)}, bf16[528,640]{1,0:T(8,128)(2,1)S(1)}, u32[]{:S(2)}, u32[]{:S(2)}) collective-permute-start(bf16[528,640]{1,0:T(8,128)(2,1)S(1)} %collective-permute-done.4.refs_6_), channel_id=1, source_target_pairs={{104,0},{0,32},{32,64},{64,96},{96,8},{8,40},{40,72},{72,104},{105... | collective-permute-start | bytes 2027528 | tf_op jit(solution)/shard_map/ppermute | solution.py:395
  96.7 0.0 copy-done
  96.7 4.5 %near.1.refs_4_ = f32[512,768]{1,0:T(8,128)S(1)} custom-call(bf16[256,4096]{1,0:T(8,128)(2,1)} %copy-done, bf16[256,4096]{1,0:T(8,128)(2,1)} %collective-permute-done.2.refs_1_, bf16[528,640]{1,0:T(8,128)(2,1)S(1)} %get-tuple-element.31.refs_2_, bf16[528,640]{1,0:T(8,128)(2,1)S(1)} %collective-permute-done.refs_3_, ...), custom_call_target="tpu_custom_call" | custom-call | flops 2013265920 | bytes 4194304 | tf_op jit(solution)/shard_map/near/pallas_call | solution.py:182
  101.2 0.0 collective-permute-done.8.refs_1_
  101.2 0.0 copy-start.12
  101.3 1.4 copy-done.12
  102.6 4.5 %away.1.refs_4_ = f32[512,768]{1,0:T(8,128)S(1)} custom-call(bf16[256,4096]{1,0:T(8,128)(2,1)} %collective-permute-done.5.refs_0_, bf16[256,4096]{1,0:T(8,128)(2,1)} %copy-done.12, bf16[528,640]{1,0:T(8,128)(2,1)S(1)} %get-tuple-element.31.refs_2_, bf16[528,640]{1,0:T(8,128)(2,1)S(1)} %collective-permute-done.refs_3_, ...), custom_call_target="tpu_custom_call" | custom-call | flops 2013265920 | bytes 4194304 | tf_op jit(solution)/shard_map/away/pallas_call | solution.py:182
  107.2 2.9 %collective-permute-done.6.refs_2_ = bf16[528,640]{1,0:T(8,128)(2,1)S(1)} collective-permute-done((bf16[528,640]{1,0:T(8,128)(2,1)S(1)}, bf16[528,640]{1,0:T(8,128)(2,1)S(1)}, u32[]{:S(2)}, u32[]{:S(2)}) %collective-permute-start.6) | collective-permute-done | bytes 675872 | tf_op jit(solution)/shard_map/ppermute | solution.py:395
  110.1 3.1 %collective-permute-done.7.refs_3_ = bf16[528,640]{1,0:T(8,128)(2,1)S(1)} collective-permute-done((bf16[528,640]{1,0:T(8,128)(2,1)S(1)}, bf16[528,640]{1,0:T(8,128)(2,1)S(1)}, u32[]{:S(2)}, u32[]{:S(2)}) %collective-permute-start.7) | collective-permute-done | bytes 675872 | tf_op jit(solution)/shard_map/ppermute | solution.py:395
  113.2 1.9 %collective-permute-start.10 = (bf16[272,640]{1,0:T(8,128)(2,1)S(1)}, bf16[272,640]{1,0:T(8,128)(2,1)S(1)}, u32[]{:S(2)}, u32[]{:S(2)}) collective-permute-start(bf16[272,640]{1,0:T(8,128)(2,1)S(1)} %slice.7), channel_id=1, source_target_pairs={{104,0},{0,32},{32,64},{64,96},{96,8},{8,40},{40,72},{72,104},{105... | collective-permute-start | bytes 1044488 | tf_op jit(solution)/shard_map/ppermute | solution.py:395
  115.2 4.6 %collective-permute-start.9 = (bf16[256,640]{1,0:T(8,128)(2,1)S(1)}, bf16[256,640]{1,0:T(8,128)(2,1)S(1)}, u32[]{:S(2)}, u32[]{:S(2)}) collective-permute-start(bf16[256,640]{1,0:T(8,128)(2,1)S(1)} %slice.6), channel_id=1, source_target_pairs={{32,0},{64,32},{96,64},{8,96},{40,8},{72,40},{104,72},{0,104},{33,... | collective-permute-start | bytes 983048 | tf_op jit(solution)/shard_map/ppermute | solution.py:395
  119.8 3.4 %near_late.1 = (f32[512,768]{1,0:T(8,128)S(1)}, bf16[512,512]{1,0:T(8,128)(2,1)S(1)}) custom-call(bf16[256,4096]{1,0:T(8,128)(2,1)} %copy-done, bf16[256,4096]{1,0:T(8,128)(2,1)} %collective-permute-done.2.refs_1_, bf16[528,640]{1,0:T(8,128)(2,1)S(1)} %collective-permute-done.6.refs_2_, bf16[528,640]{1,0:T(8,128)(2,1)S(1)} %collective-permute-done.7.refs_3_, ...), custom_call_target="tpu_custom_call" | custom-call | flops 805306368 | bytes 4194304 | tf_op jit(solution)/shard_map/near_late/pallas_call | solution.py:182
  123.2 0.0 copy-start.10
  123.2 0.0 copy-start.11
  123.2 3.4 %away_late.1 = (f32[512,768]{1,0:T(8,128)S(1)}, bf16[512,512]{1,0:T(8,128)(2,1)S(1)}) custom-call(bf16[256,4096]{1,0:T(8,128)(2,1)} %collective-permute-done.5.refs_0_, bf16[256,4096]{1,0:T(8,128)(2,1)} %copy-done.12, bf16[528,640]{1,0:T(8,128)(2,1)S(1)} %collective-permute-done.6.refs_2_, bf16[528,640]{1,0:T(8,128)(2,1)S(1)} %collective-permute-done.7.refs_3_, ...), custom_call_target="tpu_custom_call" | custom-call | flops 805306368 | bytes 4194304 | tf_op jit(solution)/shard_map/away_late/pallas_call | solution.py:182
  126.6 0.0 collective-permute-done.9.refs_4_
  126.6 0.0 collective-permute-done.10.refs_5_
  126.6 0.0 copy-done.10
  126.6 0.0 copy-done.11
  126.6 0.0 copy-start.3
  126.6 0.0 copy-start.4
  126.6 0.0 copy-start.6
  126.6 0.0 copy-start.7
  126.7 0.0 copy-start.8
  126.7 1.7 %last.1 = (f32[1024,256]{1,0:T(8,128)S(1)}, bf16[1024,128]{1,0:T(8,128)(2,1)S(1)}, f32[1024,128]{1,0:T(8,128)S(1)}, f32[1024,256]{1,0:T(8,128)S(1)}) custom-call(s32[5]{0:T(128)S(1)} %stack.23.at_ref.refs_0_, bf16[512,512]{1,0:T(8,128)(2,1)S(1)} %get-tuple-element.41.refs_0_, bf16[512,512]{1,0:T(8,128)(2,1)S(1)} %get-tuple-element.43.refs_1_, ...), custom_call_target="tpu_custom_call" | custom-call | flops 805306368 | bytes 1048576 | tf_op jit(solution)/shard_map/last/pallas_call | solution.py:225
  128.4 3.4 %collective-permute-start.11 = (bf16[1024,128]{1,0:T(8,128)(2,1)S(1)}, bf16[1024,128]{1,0:T(8,128)(2,1)S(1)}, u32[]{:S(2)}, u32[]{:S(2)}) collective-permute-start(bf16[1024,128]{1,0:T(8,128)(2,1)S(1)} %get-tuple-element.48.refs_7_), channel_id=1, source_target_pairs={{0,16},{16,0},{1,17},{17,1},{2,18},{18,2},{3,19},{19,3},{4,20},{20... | collective-permute-start | bytes 786440 | tf_op jit(solution)/shard_map/ppermute | solution.py:401
  131.8 1.0 collective-permute-done.11.refs_8_
  132.8 0.0 copy-done.6
  132.8 1.6 %core3.1 = bf16[256,384]{1,0:T(8,128)(2,1)S(1)} custom-call(s32[5]{0:T(128)S(1)} %stack.23.at_ref.refs_0_, f32[16]{0:T(128)S(1)} %copy-done.6, f32[16]{0:T(128)S(1)} %copy-done.7, f32[16]{0:T(128)S(1)} %copy-done.8, f32[8,512]{1,0:T(8,128)S(1)} %get-tuple-element.29.refs_4_, f32[1024,256]{1,0:T(8,128)S(1)} %get-tuple-element.46.refs_5_, ...), custom_call_target="tpu_custom_call" | custom-call | flops 104857600 | bytes 524288 | tf_op jit(solution)/shard_map/core3/pallas_call | solution.py:347
  134.4 2.5 %collective-permute-start.14 = (bf16[256,384]{1,0:T(8,128)(2,1)S(1)}, bf16[256,384]{1,0:T(8,128)(2,1)S(1)}, u32[]{:S(2)}, u32[]{:S(2)}) collective-permute-start(bf16[256,384]{1,0:T(8,128)(2,1)S(1)} %core3.1), channel_id=1, source_target_pairs={{0,144},{16,128},{128,16},{144,0},{1,145},{17,129},{129,17},{145,1... | collective-permute-start | bytes 589832 | tf_op jit(solution)/shard_map/ppermute | solution.py:409
  136.9 1.6 %core2.1 = bf16[256,384]{1,0:T(8,128)(2,1)S(1)} custom-call(s32[5]{0:T(128)S(1)} %stack.23.at_ref.refs_0_, f32[16]{0:T(128)S(1)} %copy-done.6, f32[16]{0:T(128)S(1)} %copy-done.7, f32[16]{0:T(128)S(1)} %copy-done.8, f32[8,512]{1,0:T(8,128)S(1)} %get-tuple-element.29.refs_4_, f32[1024,256]{1,0:T(8,128)S(1)} %get-tuple-element.46.refs_5_, ...), custom_call_target="tpu_custom_call" | custom-call | flops 104857600 | bytes 524288 | tf_op jit(solution)/shard_map/core2/pallas_call | solution.py:347
  138.5 3.0 %collective-permute-start.13 = (bf16[256,384]{1,0:T(8,128)(2,1)S(1)}, bf16[256,384]{1,0:T(8,128)(2,1)S(1)}, u32[]{:S(2)}, u32[]{:S(2)}) collective-permute-start(bf16[256,384]{1,0:T(8,128)(2,1)S(1)} %core2.1), channel_id=1, source_target_pairs={{0,128},{128,0},{1,129},{129,1},{2,130},{130,2},{3,131},{131,3},{4... | collective-permute-start | bytes 589832 | tf_op jit(solution)/shard_map/ppermute | solution.py:405
  141.6 1.6 %core1.1 = bf16[256,384]{1,0:T(8,128)(2,1)S(1)} custom-call(s32[5]{0:T(128)S(1)} %stack.23.at_ref.refs_0_, f32[16]{0:T(128)S(1)} %copy-done.6, f32[16]{0:T(128)S(1)} %copy-done.7, f32[16]{0:T(128)S(1)} %copy-done.8, f32[8,512]{1,0:T(8,128)S(1)} %get-tuple-element.29.refs_4_, f32[1024,256]{1,0:T(8,128)S(1)} %get-tuple-element.46.refs_5_, ...), custom_call_target="tpu_custom_call" | custom-call | flops 104857600 | bytes 524288 | tf_op jit(solution)/shard_map/core1/pallas_call | solution.py:347
  143.2 0.0 copy-start.9
  143.2 2.3 %collective-permute-start.12 = (bf16[256,384]{1,0:T(8,128)(2,1)S(1)}, bf16[256,384]{1,0:T(8,128)(2,1)S(1)}, u32[]{:S(2)}, u32[]{:S(2)}) collective-permute-start(bf16[256,384]{1,0:T(8,128)(2,1)S(1)} %core1.1), channel_id=1, source_target_pairs={{0,16},{16,0},{1,17},{17,1},{2,18},{18,2},{3,19},{19,3},{4,20},{20... | collective-permute-start | bytes 589832 | tf_op jit(solution)/shard_map/ppermute | solution.py:401
  145.5 1.6 %core0.1 = (f32[256,256]{1,0:T(8,128)S(1)}, f32[256,128]{1,0:T(8,128)S(1)}) custom-call(s32[5]{0:T(128)S(1)} %stack.23.at_ref.refs_0_, f32[16]{0:T(128)S(1)} %copy-done.6, f32[16]{0:T(128)S(1)} %copy-done.7, f32[16]{0:T(128)S(1)} %copy-done.8, f32[8,512]{1,0:T(8,128)S(1)} %get-tuple-element.29.refs_4_, f32[1024,256]{1,0:T(8,128)S(1)} %get-tuple-element.46.refs_5_, ...), custom_call_target="tpu_custom_call" | custom-call | flops 104857600 | bytes 524288 | tf_op jit(solution)/shard_map/core0/pallas_call | solution.py:347
  147.1 0.0 collective-permute-done.14.c_ref
  147.1 0.2 collective-permute-done.13.b_ref
  147.4 0.0 collective-permute-done.12.a_ref
  147.4 1.9 %gated_norm.1 = (bf16[256,1024]{1,0:T(8,128)(2,1)}, f32[1024,128]{1,0:T(8,128)}) custom-call(s32[5]{0:T(128)S(1)} %stack.23.at_ref.refs_0_, s32[1]{0:T(128)S(6)} %copy.14.length_ref, f32[256,256]{1,0:T(8,128)S(1)} %get-tuple-element.50.own_ref, f32[256,128]{1,0:T(8,128)S(1)} %get-tuple-element.51.state_ref, ...), custom_call_target="tpu_custom_call" | custom-call | flops 2621440 | bytes 2097152 | tf_op jit(solution)/shard_map/gated_norm/pallas_call | solution.py:379
  (10 shorter events, 0.1 us)
Async XLA Ops:
  1.3 1.0 copy-start.2
  2.2 12.7 %copy-start.5 = (f32[4096]{0:T(1024)S(1)}, f32[4096]{0:T(1024)}, u32[]{:S(2)}) copy-start(f32[4096]{0:T(1024)} %param.15) | copy-start | bytes 49156
  3.2 34.4 %all-to-all-start = ((bf16[64,8,768]{2,1,0:T(8,128)(2,1)}), bf16[64,8,768]{2,1,0:T(8,128)(2,1)S(1)}, u32[]{:S(2)}, u32[]{:S(2)}) async-start(bf16[64,8,768]{2,1,0:T(8,128)(2,1)} %cut.1), calls=%async_computation | async-start | bytes 1572864 | tf_op jit(solution)/shard_map/all_to_all | solution.py:428
  14.9 1.6 %copy-start.1 = (bf16[256,4096]{1,0:T(8,128)(2,1)S(1)}, bf16[256,4096]{1,0:T(8,128)(2,1)}, u32[]{:S(2)}) copy-start(bf16[256,4096]{1,0:T(8,128)(2,1)} %hidden_ref.1) | copy-start | bytes 6291460
  18.6 78.1 %copy-start = (bf16[256,4096]{1,0:T(8,128)(2,1)}, bf16[256,4096]{1,0:T(8,128)(2,1)S(1)}, u32[]{:S(2)}) copy-start(bf16[256,4096]{1,0:T(8,128)(2,1)S(1)} %norm.1.refs_0_) | copy-start | bytes 6291460
  18.6 31.7 %collective-permute-start.2 = (bf16[256,4096]{1,0:T(8,128)(2,1)S(1)}, bf16[256,4096]{1,0:T(8,128)(2,1)}, u32[]{:S(2)}, u32[]{:S(2)}) collective-permute-start(bf16[256,4096]{1,0:T(8,128)(2,1)S(1)} %norm.1.refs_0_), channel_id=1, source_target_pairs={{0,16},{16,0},{1,17},{17,1},{2,18},{18,2},{3,19},{19,3},{4,20},{20... | collective-permute-start | bytes 6291464 | tf_op jit(solution)/shard_map/ppermute | solution.py:401
  21.0 54.0 %collective-permute-start.5 = (bf16[256,4096]{1,0:T(8,128)(2,1)S(1)}, bf16[256,4096]{1,0:T(8,128)(2,1)}, u32[]{:S(2)}, u32[]{:S(2)}) collective-permute-start(bf16[256,4096]{1,0:T(8,128)(2,1)S(1)} %norm.1.refs_0_), channel_id=1, source_target_pairs={{0,128},{128,0},{1,129},{129,1},{2,130},{130,2},{3,131},{131,3},{4... | collective-permute-start | bytes 6291464 | tf_op jit(solution)/shard_map/ppermute | solution.py:405
  37.7 24.2 %collective-permute-start = (bf16[528,640]{1,0:T(8,128)(2,1)S(1)}, bf16[528,640]{1,0:T(8,128)(2,1)S(1)}, u32[]{:S(2)}, u32[]{:S(2)}) collective-permute-start(bf16[528,640]{1,0:T(8,128)(2,1)S(1)} %get-tuple-element.31.refs_2_), channel_id=1, source_target_pairs={{32,0},{64,32},{96,64},{8,96},{40,8},{72,40},{104,72},{0,104},{33,... | collective-permute-start | bytes 2027528 | tf_op jit(solution)/shard_map/ppermute | solution.py:395
  48.3 18.5 %collective-permute-start.1 = (bf16[528,640]{1,0:T(8,128)(2,1)S(1)}, bf16[528,640]{1,0:T(8,128)(2,1)S(1)}, u32[]{:S(2)}, u32[]{:S(2)}) collective-permute-start(bf16[528,640]{1,0:T(8,128)(2,1)S(1)} %get-tuple-element.31.refs_2_), channel_id=1, source_target_pairs={{104,0},{0,32},{32,64},{64,96},{96,8},{8,40},{40,72},{72,104},{105... | collective-permute-start | bytes 2027528 | tf_op jit(solution)/shard_map/ppermute | solution.py:395
  66.9 16.4 %collective-permute-start.3 = (bf16[528,640]{1,0:T(8,128)(2,1)S(1)}, bf16[528,640]{1,0:T(8,128)(2,1)S(1)}, u32[]{:S(2)}, u32[]{:S(2)}) collective-permute-start(bf16[528,640]{1,0:T(8,128)(2,1)S(1)} %collective-permute-done.refs_3_), channel_id=1, source_target_pairs={{32,0},{64,32},{96,64},{8,96},{40,8},{72,40},{104,72},{0,104},{33,... | collective-permute-start | bytes 2027528 | tf_op jit(solution)/shard_map/ppermute | solution.py:395
  68.8 17.6 %collective-permute-start.4 = (bf16[528,640]{1,0:T(8,128)(2,1)S(1)}, bf16[528,640]{1,0:T(8,128)(2,1)S(1)}, u32[]{:S(2)}, u32[]{:S(2)}) collective-permute-start(bf16[528,640]{1,0:T(8,128)(2,1)S(1)} %collective-permute-done.1.refs_4_), channel_id=1, source_target_pairs={{104,0},{0,32},{32,64},{64,96},{96,8},{8,40},{40,72},{72,104},{105... | collective-permute-start | bytes 2027528 | tf_op jit(solution)/shard_map/ppermute | solution.py:395
  86.4 14.9 %collective-permute-start.8 = (bf16[256,4096]{1,0:T(8,128)(2,1)}, bf16[256,4096]{1,0:T(8,128)(2,1)S(1)}, u32[]{:S(2)}, u32[]{:S(2)}) collective-permute-start(bf16[256,4096]{1,0:T(8,128)(2,1)} %collective-permute-done.5.refs_0_), channel_id=1, source_target_pairs={{0,16},{16,0},{1,17},{17,1},{2,18},{18,2},{3,19},{19,3},{4,20},{20... | collective-permute-start | bytes 6291464 | tf_op jit(solution)/shard_map/ppermute | solution.py:401
  91.4 18.7 %collective-permute-start.6 = (bf16[528,640]{1,0:T(8,128)(2,1)S(1)}, bf16[528,640]{1,0:T(8,128)(2,1)S(1)}, u32[]{:S(2)}, u32[]{:S(2)}) collective-permute-start(bf16[528,640]{1,0:T(8,128)(2,1)S(1)} %collective-permute-done.3.refs_5_), channel_id=1, source_target_pairs={{32,0},{64,32},{96,64},{8,96},{40,8},{72,40},{104,72},{0,104},{33,... | collective-permute-start | bytes 2027528 | tf_op jit(solution)/shard_map/ppermute | solution.py:395
  93.3 19.9 %collective-permute-start.7 = (bf16[528,640]{1,0:T(8,128)(2,1)S(1)}, bf16[528,640]{1,0:T(8,128)(2,1)S(1)}, u32[]{:S(2)}, u32[]{:S(2)}) collective-permute-start(bf16[528,640]{1,0:T(8,128)(2,1)S(1)} %collective-permute-done.4.refs_6_), channel_id=1, source_target_pairs={{104,0},{0,32},{32,64},{64,96},{96,8},{8,40},{40,72},{72,104},{105... | collective-permute-start | bytes 2027528 | tf_op jit(solution)/shard_map/ppermute | solution.py:395
  101.2 1.4 copy-start.12
  113.2 13.4 %collective-permute-start.10 = (bf16[272,640]{1,0:T(8,128)(2,1)S(1)}, bf16[272,640]{1,0:T(8,128)(2,1)S(1)}, u32[]{:S(2)}, u32[]{:S(2)}) collective-permute-start(bf16[272,640]{1,0:T(8,128)(2,1)S(1)} %slice.7), channel_id=1, source_target_pairs={{104,0},{0,32},{32,64},{64,96},{96,8},{8,40},{40,72},{72,104},{105... | collective-permute-start | bytes 1044488 | tf_op jit(solution)/shard_map/ppermute | solution.py:395
  115.2 11.4 %collective-permute-start.9 = (bf16[256,640]{1,0:T(8,128)(2,1)S(1)}, bf16[256,640]{1,0:T(8,128)(2,1)S(1)}, u32[]{:S(2)}, u32[]{:S(2)}) collective-permute-start(bf16[256,640]{1,0:T(8,128)(2,1)S(1)} %slice.6), channel_id=1, source_target_pairs={{32,0},{64,32},{96,64},{8,96},{40,8},{72,40},{104,72},{0,104},{33,... | collective-permute-start | bytes 983048 | tf_op jit(solution)/shard_map/ppermute | solution.py:395
  123.2 3.4 %copy-start.10 = (f32[4,2,128]{2,1,0:T(2,128)S(1)}, f32[4,2,128]{2,1,0:T(2,128)}, u32[]{:S(2)}) copy-start(f32[4,2,128]{2,1,0:T(2,128)} %refs_6_.1) | copy-start | bytes 12292
  123.2 3.4 %copy-start.11 = (f32[2,128]{1,0:T(2,128)S(1)}, f32[2,128]{1,0:T(2,128)}, u32[]{:S(2)}) copy-start(f32[2,128]{1,0:T(2,128)} %refs_7_.1) | copy-start | bytes 3076
  126.6 6.2 %copy-start.3 = (f32[4,1024]{1,0:T(4,128)S(1)}, f32[4,1024]{1,0:T(4,128)}, u32[]{:S(2)}) copy-start(f32[4,1024]{1,0:T(4,128)} %refs_10_.7) | copy-start | bytes 49156
  126.6 6.1 %copy-start.4 = (f32[1024]{0:T(1024)S(1)}, f32[1024]{0:T(1024)}, u32[]{:S(2)}) copy-start(f32[1024]{0:T(1024)} %param.17) | copy-start | bytes 12292
  126.6 6.1 %copy-start.6 = (f32[16]{0:T(128)S(1)}, f32[16]{0:T(128)}, u32[]{:S(2)}) copy-start(f32[16]{0:T(128)} %refs_1_.7) | copy-start | bytes 196
  126.6 6.1 %copy-start.7 = (f32[16]{0:T(128)S(1)}, f32[16]{0:T(128)}, u32[]{:S(2)}) copy-start(f32[16]{0:T(128)} %refs_2_.7) | copy-start | bytes 196
  126.7 6.1 %copy-start.8 = (f32[16]{0:T(128)S(1)}, f32[16]{0:T(128)}, u32[]{:S(2)}) copy-start(f32[16]{0:T(128)} %refs_3_.7) | copy-start | bytes 196
  128.4 4.4 %collective-permute-start.11 = (bf16[1024,128]{1,0:T(8,128)(2,1)S(1)}, bf16[1024,128]{1,0:T(8,128)(2,1)S(1)}, u32[]{:S(2)}, u32[]{:S(2)}) collective-permute-start(bf16[1024,128]{1,0:T(8,128)(2,1)S(1)} %get-tuple-element.48.refs_7_), channel_id=1, source_target_pairs={{0,16},{16,0},{1,17},{17,1},{2,18},{18,2},{3,19},{19,3},{4,20},{20... | collective-permute-start | bytes 786440 | tf_op jit(solution)/shard_map/ppermute | solution.py:401
  134.4 12.7 %collective-permute-start.14 = (bf16[256,384]{1,0:T(8,128)(2,1)S(1)}, bf16[256,384]{1,0:T(8,128)(2,1)S(1)}, u32[]{:S(2)}, u32[]{:S(2)}) collective-permute-start(bf16[256,384]{1,0:T(8,128)(2,1)S(1)} %core3.1), channel_id=1, source_target_pairs={{0,144},{16,128},{128,16},{144,0},{1,145},{17,129},{129,17},{145,1... | collective-permute-start | bytes 589832 | tf_op jit(solution)/shard_map/ppermute | solution.py:409
  138.5 8.8 %collective-permute-start.13 = (bf16[256,384]{1,0:T(8,128)(2,1)S(1)}, bf16[256,384]{1,0:T(8,128)(2,1)S(1)}, u32[]{:S(2)}, u32[]{:S(2)}) collective-permute-start(bf16[256,384]{1,0:T(8,128)(2,1)S(1)} %core2.1), channel_id=1, source_target_pairs={{0,128},{128,0},{1,129},{129,1},{2,130},{130,2},{3,131},{131,3},{4... | collective-permute-start | bytes 589832 | tf_op jit(solution)/shard_map/ppermute | solution.py:405
  143.2 4.2 %copy-start.9 = (f32[1024]{0:T(1024)S(1)}, f32[1024]{0:T(1024)}, u32[]{:S(2)}) copy-start(f32[1024]{0:T(1024)} %param.23) | copy-start | bytes 12292
  143.2 4.2 %collective-permute-start.12 = (bf16[256,384]{1,0:T(8,128)(2,1)S(1)}, bf16[256,384]{1,0:T(8,128)(2,1)S(1)}, u32[]{:S(2)}, u32[]{:S(2)}) collective-permute-start(bf16[256,384]{1,0:T(8,128)(2,1)S(1)} %core1.1), channel_id=1, source_target_pairs={{0,16},{16,0},{1,17},{17,1},{2,18},{18,2},{3,19},{19,3},{4,20},{20... | collective-permute-start | bytes 589832 | tf_op jit(solution)/shard_map/ppermute | solution.py:401

commit v4 on v3

--- a/solution.py
+++ b/solution.py
@@ -440,9 +440,8 @@
     together = lax.optimization_barrier
     w0, lengths_all = pack_call(block)
     w1, w7 = from_z(w0, 1), from_z(w0, -1)
-    w1, w7, other = together((w1, w7, other))
     w2, w6 = from_z(w1, 1), from_z(w7, -1)
-    w2, w6, own_x = together((w2, w6, own_x))
+    w2, w6, own_x, other = together((w2, w6, own_x, other))
     far = swap_core(own_x)
     w3, w5 = from_z(w2, 1), from_z(w6, -1)
     early = [w0, w1, w7, w2, w6]

time: 150 us -> 148 us (0.987)
  waiting for transfers between devices: 51.5 us -> 47.6 us
  starting transfers between devices: 63.1 us -> 65.3 us
    ppermute x8, waiting for transfers between devices: 34.1 us -> 29.4 us  [from_z(): lax.ppermute(value, ('zl', 'zh'), [(flat((i + distance) % 8), flat(i)) fo...]
    ppermute x8, starting transfers between devices: 29.6 us -> 31.6 us  [from_z(): lax.ppermute(value, ('zl', 'zh'), [(flat((i + distance) % 8), flat(i)) fo...]
  transfers between devices with their start and end apart: 16 -> 16, of which waited for: 10 -> 9; matrix products, arithmetic and copies ran while one was open for 0% -> 0% of each run, Pallas kernels for 15% -> 15%
where the time goes in v4:
time: 148 us
  starting transfers between devices  65.3 us (44%)
  waiting for transfers between devices  47.6 us (32%)
  Pallas kernels  28.9 us (20%)
  local copies, waits for them, and re-layouts  4.13 us (3%)
  between operations  1.66 us (1%)
    ppermute x8, starting transfers between devices, from_z(): lax.ppermute(value, ('zl', 'zh'), [(flat((i + distance) % 8), flat(i)) fo...  31.6 us
    ppermute x8, waiting for transfers between devices, from_z(): lax.ppermute(value, ('zl', 'zh'), [(flat((i + distance) % 8), flat(i)) fo...  29.4 us
    pallas_call x4, Pallas kernels, pair_call(): pl.pallas_call(functools.partial(pair_kernel, len(weights), first, total...  15.8 us
    ppermute x4, starting transfers between devices, swap_core(): return lax.ppermute(value, 'core', [(0, 1), (1, 0)])  13.3 us
    all_to_all x1, waiting for transfers between devices, on_device(): lax.all_to_all(cut_call(lengths, projection), ('xa', 'xb', 'core', 'y'),...  13.1 us
    all_to_all x1, starting transfers between devices, on_device(): lax.all_to_all(cut_call(lengths, projection), ('xa', 'xb', 'core', 'y'),...  11.6 us
    pallas_call x4, Pallas kernels, core_call(): pl.pallas_call(functools.partial(core_kernel, seqs), out_shape=tuple(shap...  6.39 us
    ppermute x2, starting transfers between devices, swap_x(): return lax.ppermute(value, 'xb', [(0, 1), (1, 0)])  6.34 us
  transfers between devices with their start and end apart: 16, of which 9 were waited for; matrix products, arithmetic and copies ran while one was open for 0% of the time, Pallas kernels for 15%

profile of v4, /device:TPU:1, one launch (start us, length us, event | category | flops | bytes accessed | tf_op | source)
XLA Modules:
  0.0 147.6 jit_solution(12569354524184136078)
XLA Ops:
  1.3 0.0 copy-start.2
  1.3 1.0 copy-done.2
  2.2 1.0 cut.1
  3.2 11.6 %all-to-all-start = ((bf16[64,8,768]{2,1,0:T(8,128)(2,1)}), bf16[64,8,768]{2,1,0:T(8,128)(2,1)S(1)}, u32[]{:S(2)}, u32[]{:S(2)}) async-start(bf16[64,8,768]{2,1,0:T(8,128)(2,1)} %cut.1), calls=%async_computation | async-start | bytes 1572864 | tf_op jit(solution)/shard_map/all_to_all | solution.py:428
  14.9 0.1 stack.23.at_ref.refs_0_
  14.9 0.0 copy-done.5
  15.0 1.6 %copy-done.1 = bf16[256,4096]{1,0:T(8,128)(2,1)S(1)} copy-done((bf16[256,4096]{1,0:T(8,128)(2,1)S(1)}, bf16[256,4096]{1,0:T(8,128)(2,1)}, u32[]{:S(2)}) %copy-start.1) | copy-done | bytes 2097176
  16.5 2.0 %norm.1.refs_0_ = bf16[256,4096]{1,0:T(8,128)(2,1)S(1)} custom-call(s32[5]{0:T(128)S(1)} %stack.23.at_ref.refs_0_, bf16[256,4096]{1,0:T(8,128)(2,1)S(1)} %copy-done.1, f32[1,4096]{1,0:T(1,128)S(1)} %bitcast.15), custom_call_target="tpu_custom_call" | custom-call | flops 8388608 | bytes 4194304 | tf_op jit(solution)/shard_map/norm/pallas_call | solution.py:77
  18.6 0.0 copy-start
  18.6 3.3 %collective-permute-start.4 = (bf16[256,4096]{1,0:T(8,128)(2,1)S(1)}, bf16[256,4096]{1,0:T(8,128)(2,1)}, u32[]{:S(2)}, u32[]{:S(2)}) collective-permute-start(bf16[256,4096]{1,0:T(8,128)(2,1)S(1)} %norm.1.refs_0_), channel_id=1, source_target_pairs={{0,128},{128,0},{1,129},{129,1},{2,130},{130,2},{3,131},{131,3},{4... | collective-permute-start | bytes 6291464 | tf_op jit(solution)/shard_map/ppermute | solution.py:405
  21.9 2.5 %collective-permute-start.5 = (bf16[256,4096]{1,0:T(8,128)(2,1)S(1)}, bf16[256,4096]{1,0:T(8,128)(2,1)}, u32[]{:S(2)}, u32[]{:S(2)}) collective-permute-start(bf16[256,4096]{1,0:T(8,128)(2,1)S(1)} %norm.1.refs_0_), channel_id=1, source_target_pairs={{0,16},{16,0},{1,17},{17,1},{2,18},{18,2},{3,19},{19,3},{4,20},{20... | collective-permute-start | bytes 6291464 | tf_op jit(solution)/shard_map/ppermute | solution.py:401
  24.5 13.1 %all-to-all-done = bf16[64,8,768]{2,1,0:T(8,128)(2,1)S(1)} async-done(((bf16[64,8,768]{2,1,0:T(8,128)(2,1)}), bf16[64,8,768]{2,1,0:T(8,128)(2,1)S(1)}, u32[]{:S(2)}, u32[]{:S(2)}) %all-to-all-start) | async-done | bytes 786464 | tf_op jit(solution)/shard_map/all_to_all | solution.py:428
  37.6 0.1 pack.1
  37.7 10.7 %collective-permute-start = (bf16[528,640]{1,0:T(8,128)(2,1)S(1)}, bf16[528,640]{1,0:T(8,128)(2,1)S(1)}, u32[]{:S(2)}, u32[]{:S(2)}) collective-permute-start(bf16[528,640]{1,0:T(8,128)(2,1)S(1)} %get-tuple-element.29.refs_2_), channel_id=1, source_target_pairs={{32,0},{64,32},{96,64},{8,96},{40,8},{72,40},{104,72},{0,104},{33,... | collective-permute-start | bytes 2027528 | tf_op jit(solution)/shard_map/ppermute | solution.py:395
  48.3 1.9 %collective-permute-start.2 = (bf16[528,640]{1,0:T(8,128)(2,1)S(1)}, bf16[528,640]{1,0:T(8,128)(2,1)S(1)}, u32[]{:S(2)}, u32[]{:S(2)}) collective-permute-start(bf16[528,640]{1,0:T(8,128)(2,1)S(1)} %get-tuple-element.29.refs_2_), channel_id=1, source_target_pairs={{104,0},{0,32},{32,64},{64,96},{96,8},{8,40},{40,72},{72,104},{105... | collective-permute-start | bytes 2027528 | tf_op jit(solution)/shard_map/ppermute | solution.py:395
  50.3 11.6 %collective-permute-done.refs_3_ = bf16[528,640]{1,0:T(8,128)(2,1)S(1)} collective-permute-done((bf16[528,640]{1,0:T(8,128)(2,1)S(1)}, bf16[528,640]{1,0:T(8,128)(2,1)S(1)}, u32[]{:S(2)}, u32[]{:S(2)}) %collective-permute-start) | collective-permute-done | bytes 675872 | tf_op jit(solution)/shard_map/ppermute | solution.py:395
  61.8 5.3 %collective-permute-start.1 = (bf16[528,640]{1,0:T(8,128)(2,1)S(1)}, bf16[528,640]{1,0:T(8,128)(2,1)S(1)}, u32[]{:S(2)}, u32[]{:S(2)}) collective-permute-start(bf16[528,640]{1,0:T(8,128)(2,1)S(1)} %collective-permute-done.refs_3_), channel_id=1, source_target_pairs={{32,0},{64,32},{96,64},{8,96},{40,8},{72,40},{104,72},{0,104},{33,... | collective-permute-start | bytes 2027528 | tf_op jit(solution)/shard_map/ppermute | solution.py:395
  67.1 0.0 collective-permute-done.2.refs_4_
  67.2 1.9 %collective-permute-start.3 = (bf16[528,640]{1,0:T(8,128)(2,1)S(1)}, bf16[528,640]{1,0:T(8,128)(2,1)S(1)}, u32[]{:S(2)}, u32[]{:S(2)}) collective-permute-start(bf16[528,640]{1,0:T(8,128)(2,1)S(1)} %collective-permute-done.2.refs_4_), channel_id=1, source_target_pairs={{104,0},{0,32},{32,64},{64,96},{96,8},{8,40},{40,72},{72,104},{105... | collective-permute-start | bytes 2027528 | tf_op jit(solution)/shard_map/ppermute | solution.py:395
  69.1 3.8 %collective-permute-done.4.refs_0_ = bf16[256,4096]{1,0:T(8,128)(2,1)} collective-permute-done((bf16[256,4096]{1,0:T(8,128)(2,1)S(1)}, bf16[256,4096]{1,0:T(8,128)(2,1)}, u32[]{:S(2)}, u32[]{:S(2)}) %collective-permute-start.4) | collective-permute-done | bytes 2097184 | tf_op jit(solution)/shard_map/ppermute | solution.py:405
  72.9 0.0 collective-permute-done.5.refs_1_
  72.9 6.8 %collective-permute-done.1.refs_5_ = bf16[528,640]{1,0:T(8,128)(2,1)S(1)} collective-permute-done((bf16[528,640]{1,0:T(8,128)(2,1)S(1)}, bf16[528,640]{1,0:T(8,128)(2,1)S(1)}, u32[]{:S(2)}, u32[]{:S(2)}) %collective-permute-start.1) | collective-permute-done | bytes 675872 | tf_op jit(solution)/shard_map/ppermute | solution.py:395
  79.7 5.1 %collective-permute-done.3.refs_6_ = bf16[528,640]{1,0:T(8,128)(2,1)S(1)} collective-permute-done((bf16[528,640]{1,0:T(8,128)(2,1)S(1)}, bf16[528,640]{1,0:T(8,128)(2,1)S(1)}, u32[]{:S(2)}, u32[]{:S(2)}) %collective-permute-start.3) | collective-permute-done | bytes 675872 | tf_op jit(solution)/shard_map/ppermute | solution.py:395
  84.8 5.0 %collective-permute-start.8 = (bf16[256,4096]{1,0:T(8,128)(2,1)}, bf16[256,4096]{1,0:T(8,128)(2,1)S(1)}, u32[]{:S(2)}, u32[]{:S(2)}) collective-permute-start(bf16[256,4096]{1,0:T(8,128)(2,1)} %collective-permute-done.4.refs_0_), channel_id=1, source_target_pairs={{0,16},{16,0},{1,17},{17,1},{2,18},{18,2},{3,19},{19,3},{4,20},{20... | collective-permute-start | bytes 6291464 | tf_op jit(solution)/shard_map/ppermute | solution.py:401
  89.8 1.9 %collective-permute-start.6 = (bf16[528,640]{1,0:T(8,128)(2,1)S(1)}, bf16[528,640]{1,0:T(8,128)(2,1)S(1)}, u32[]{:S(2)}, u32[]{:S(2)}) collective-permute-start(bf16[528,640]{1,0:T(8,128)(2,1)S(1)} %collective-permute-done.1.refs_5_), channel_id=1, source_target_pairs={{32,0},{64,32},{96,64},{8,96},{40,8},{72,40},{104,72},{0,104},{33,... | collective-permute-start | bytes 2027528 | tf_op jit(solution)/shard_map/ppermute | solution.py:395
  91.7 3.4 %collective-permute-start.7 = (bf16[528,640]{1,0:T(8,128)(2,1)S(1)}, bf16[528,640]{1,0:T(8,128)(2,1)S(1)}, u32[]{:S(2)}, u32[]{:S(2)}) collective-permute-start(bf16[528,640]{1,0:T(8,128)(2,1)S(1)} %collective-permute-done.3.refs_6_), channel_id=1, source_target_pairs={{104,0},{0,32},{32,64},{64,96},{96,8},{8,40},{40,72},{72,104},{105... | collective-permute-start | bytes 2027528 | tf_op jit(solution)/shard_map/ppermute | solution.py:395
  95.1 0.0 copy-done
  95.1 4.6 %near.1.refs_4_ = f32[512,768]{1,0:T(8,128)S(1)} custom-call(bf16[256,4096]{1,0:T(8,128)(2,1)} %copy-done, bf16[256,4096]{1,0:T(8,128)(2,1)} %collective-permute-done.5.refs_1_, bf16[528,640]{1,0:T(8,128)(2,1)S(1)} %get-tuple-element.29.refs_2_, bf16[528,640]{1,0:T(8,128)(2,1)S(1)} %collective-permute-done.refs_3_, ...), custom_call_target="tpu_custom_call" | custom-call | flops 2013265920 | bytes 4194304 | tf_op jit(solution)/shard_map/near/pallas_call | solution.py:182
  99.6 0.0 collective-permute-done.8.refs_1_
  99.6 1.4 copy-done.12
  101.0 4.5 %away.1.refs_4_ = f32[512,768]{1,0:T(8,128)S(1)} custom-call(bf16[256,4096]{1,0:T(8,128)(2,1)} %collective-permute-done.4.refs_0_, bf16[256,4096]{1,0:T(8,128)(2,1)} %copy-done.12, bf16[528,640]{1,0:T(8,128)(2,1)S(1)} %get-tuple-element.29.refs_2_, bf16[528,640]{1,0:T(8,128)(2,1)S(1)} %collective-permute-done.refs_3_, ...), custom_call_target="tpu_custom_call" | custom-call | flops 2013265920 | bytes 4194304 | tf_op jit(solution)/shard_map/away/pallas_call | solution.py:182
  105.6 2.9 %collective-permute-done.6.refs_2_ = bf16[528,640]{1,0:T(8,128)(2,1)S(1)} collective-permute-done((bf16[528,640]{1,0:T(8,128)(2,1)S(1)}, bf16[528,640]{1,0:T(8,128)(2,1)S(1)}, u32[]{:S(2)}, u32[]{:S(2)}) %collective-permute-start.6) | collective-permute-done | bytes 675872 | tf_op jit(solution)/shard_map/ppermute | solution.py:395
  108.4 3.1 %collective-permute-done.7.refs_3_ = bf16[528,640]{1,0:T(8,128)(2,1)S(1)} collective-permute-done((bf16[528,640]{1,0:T(8,128)(2,1)S(1)}, bf16[528,640]{1,0:T(8,128)(2,1)S(1)}, u32[]{:S(2)}, u32[]{:S(2)}) %collective-permute-start.7) | collective-permute-done | bytes 675872 | tf_op jit(solution)/shard_map/ppermute | solution.py:395
  111.6 1.9 %collective-permute-start.10 = (bf16[272,640]{1,0:T(8,128)(2,1)S(1)}, bf16[272,640]{1,0:T(8,128)(2,1)S(1)}, u32[]{:S(2)}, u32[]{:S(2)}) collective-permute-start(bf16[272,640]{1,0:T(8,128)(2,1)S(1)} %slice.7), channel_id=1, source_target_pairs={{104,0},{0,32},{32,64},{64,96},{96,8},{8,40},{40,72},{72,104},{105... | collective-permute-start | bytes 1044488 | tf_op jit(solution)/shard_map/ppermute | solution.py:395
  113.6 4.6 %collective-permute-start.9 = (bf16[256,640]{1,0:T(8,128)(2,1)S(1)}, bf16[256,640]{1,0:T(8,128)(2,1)S(1)}, u32[]{:S(2)}, u32[]{:S(2)}) collective-permute-start(bf16[256,640]{1,0:T(8,128)(2,1)S(1)} %slice.6), channel_id=1, source_target_pairs={{32,0},{64,32},{96,64},{8,96},{40,8},{72,40},{104,72},{0,104},{33,... | collective-permute-start | bytes 983048 | tf_op jit(solution)/shard_map/ppermute | solution.py:395
  118.2 3.4 %near_late.1 = (f32[512,768]{1,0:T(8,128)S(1)}, bf16[512,512]{1,0:T(8,128)(2,1)S(1)}) custom-call(bf16[256,4096]{1,0:T(8,128)(2,1)} %copy-done, bf16[256,4096]{1,0:T(8,128)(2,1)} %collective-permute-done.5.refs_1_, bf16[528,640]{1,0:T(8,128)(2,1)S(1)} %collective-permute-done.6.refs_2_, bf16[528,640]{1,0:T(8,128)(2,1)S(1)} %collective-permute-done.7.refs_3_, ...), custom_call_target="tpu_custom_call" | custom-call | flops 805306368 | bytes 4194304 | tf_op jit(solution)/shard_map/near_late/pallas_call | solution.py:182
  121.5 0.0 copy-start.10
  121.5 0.0 copy-start.11
  121.6 3.4 %away_late.1 = (f32[512,768]{1,0:T(8,128)S(1)}, bf16[512,512]{1,0:T(8,128)(2,1)S(1)}) custom-call(bf16[256,4096]{1,0:T(8,128)(2,1)} %collective-permute-done.4.refs_0_, bf16[256,4096]{1,0:T(8,128)(2,1)} %copy-done.12, bf16[528,640]{1,0:T(8,128)(2,1)S(1)} %collective-permute-done.6.refs_2_, bf16[528,640]{1,0:T(8,128)(2,1)S(1)} %collective-permute-done.7.refs_3_, ...), custom_call_target="tpu_custom_call" | custom-call | flops 805306368 | bytes 4194304 | tf_op jit(solution)/shard_map/away_late/pallas_call | solution.py:182
  124.9 0.0 collective-permute-done.9.refs_4_
  125.0 0.0 collective-permute-done.10.refs_5_
  125.0 0.0 copy-start.3
  125.0 0.0 copy-start.4
  125.0 0.0 copy-start.6
  125.0 0.0 copy-start.7
  125.0 0.0 copy-start.8
  125.0 1.7 %last.1 = (f32[1024,256]{1,0:T(8,128)S(1)}, bf16[1024,128]{1,0:T(8,128)(2,1)S(1)}, f32[1024,128]{1,0:T(8,128)S(1)}, f32[1024,256]{1,0:T(8,128)S(1)}) custom-call(s32[5]{0:T(128)S(1)} %stack.23.at_ref.refs_0_, bf16[512,512]{1,0:T(8,128)(2,1)S(1)} %get-tuple-element.37.refs_0_, bf16[512,512]{1,0:T(8,128)(2,1)S(1)} %get-tuple-element.39.refs_1_, ...), custom_call_target="tpu_custom_call" | custom-call | flops 805306368 | bytes 1048576 | tf_op jit(solution)/shard_map/last/pallas_call | solution.py:225
  126.7 3.4 %collective-permute-start.11 = (bf16[1024,128]{1,0:T(8,128)(2,1)S(1)}, bf16[1024,128]{1,0:T(8,128)(2,1)S(1)}, u32[]{:S(2)}, u32[]{:S(2)}) collective-permute-start(bf16[1024,128]{1,0:T(8,128)(2,1)S(1)} %get-tuple-element.44.refs_7_), channel_id=1, source_target_pairs={{0,16},{16,0},{1,17},{17,1},{2,18},{18,2},{3,19},{19,3},{4,20},{20... | collective-permute-start | bytes 786440 | tf_op jit(solution)/shard_map/ppermute | solution.py:401
  130.2 1.0 collective-permute-done.11.refs_8_
  131.1 0.0 copy-done.3
  131.2 0.0 copy-done.8
  131.2 1.6 %core3.1 = bf16[256,384]{1,0:T(8,128)(2,1)S(1)} custom-call(s32[5]{0:T(128)S(1)} %stack.23.at_ref.refs_0_, f32[16]{0:T(128)S(1)} %copy-done.6, f32[16]{0:T(128)S(1)} %copy-done.7, f32[16]{0:T(128)S(1)} %copy-done.8, f32[8,512]{1,0:T(8,128)S(1)} %get-tuple-element.27.refs_4_, f32[1024,256]{1,0:T(8,128)S(1)} %get-tuple-element.42.refs_5_, ...), custom_call_target="tpu_custom_call" | custom-call | flops 104857600 | bytes 524288 | tf_op jit(solution)/shard_map/core3/pallas_call | solution.py:347
  132.8 2.5 %collective-permute-start.14 = (bf16[256,384]{1,0:T(8,128)(2,1)S(1)}, bf16[256,384]{1,0:T(8,128)(2,1)S(1)}, u32[]{:S(2)}, u32[]{:S(2)}) collective-permute-start(bf16[256,384]{1,0:T(8,128)(2,1)S(1)} %core3.1), channel_id=1, source_target_pairs={{0,144},{16,128},{128,16},{144,0},{1,145},{17,129},{129,17},{145,1... | collective-permute-start | bytes 589832 | tf_op jit(solution)/shard_map/ppermute | solution.py:409
  135.3 1.6 %core2.1 = bf16[256,384]{1,0:T(8,128)(2,1)S(1)} custom-call(s32[5]{0:T(128)S(1)} %stack.23.at_ref.refs_0_, f32[16]{0:T(128)S(1)} %copy-done.6, f32[16]{0:T(128)S(1)} %copy-done.7, f32[16]{0:T(128)S(1)} %copy-done.8, f32[8,512]{1,0:T(8,128)S(1)} %get-tuple-element.27.refs_4_, f32[1024,256]{1,0:T(8,128)S(1)} %get-tuple-element.42.refs_5_, ...), custom_call_target="tpu_custom_call" | custom-call | flops 104857600 | bytes 524288 | tf_op jit(solution)/shard_map/core2/pallas_call | solution.py:347
  136.9 3.0 %collective-permute-start.13 = (bf16[256,384]{1,0:T(8,128)(2,1)S(1)}, bf16[256,384]{1,0:T(8,128)(2,1)S(1)}, u32[]{:S(2)}, u32[]{:S(2)}) collective-permute-start(bf16[256,384]{1,0:T(8,128)(2,1)S(1)} %core2.1), channel_id=1, source_target_pairs={{0,128},{128,0},{1,129},{129,1},{2,130},{130,2},{3,131},{131,3},{4... | collective-permute-start | bytes 589832 | tf_op jit(solution)/shard_map/ppermute | solution.py:405
  139.9 1.6 %core1.1 = bf16[256,384]{1,0:T(8,128)(2,1)S(1)} custom-call(s32[5]{0:T(128)S(1)} %stack.23.at_ref.refs_0_, f32[16]{0:T(128)S(1)} %copy-done.6, f32[16]{0:T(128)S(1)} %copy-done.7, f32[16]{0:T(128)S(1)} %copy-done.8, f32[8,512]{1,0:T(8,128)S(1)} %get-tuple-element.27.refs_4_, f32[1024,256]{1,0:T(8,128)S(1)} %get-tuple-element.42.refs_5_, ...), custom_call_target="tpu_custom_call" | custom-call | flops 104857600 | bytes 524288 | tf_op jit(solution)/shard_map/core1/pallas_call | solution.py:347
  141.5 0.0 copy-start.9
  141.6 2.3 %collective-permute-start.12 = (bf16[256,384]{1,0:T(8,128)(2,1)S(1)}, bf16[256,384]{1,0:T(8,128)(2,1)S(1)}, u32[]{:S(2)}, u32[]{:S(2)}) collective-permute-start(bf16[256,384]{1,0:T(8,128)(2,1)S(1)} %core1.1), channel_id=1, source_target_pairs={{0,16},{16,0},{1,17},{17,1},{2,18},{18,2},{3,19},{19,3},{4,20},{20... | collective-permute-start | bytes 589832 | tf_op jit(solution)/shard_map/ppermute | solution.py:401
  143.9 1.6 %core0.1 = (f32[256,256]{1,0:T(8,128)S(1)}, f32[256,128]{1,0:T(8,128)S(1)}) custom-call(s32[5]{0:T(128)S(1)} %stack.23.at_ref.refs_0_, f32[16]{0:T(128)S(1)} %copy-done.6, f32[16]{0:T(128)S(1)} %copy-done.7, f32[16]{0:T(128)S(1)} %copy-done.8, f32[8,512]{1,0:T(8,128)S(1)} %get-tuple-element.27.refs_4_, f32[1024,256]{1,0:T(8,128)S(1)} %get-tuple-element.42.refs_5_, ...), custom_call_target="tpu_custom_call" | custom-call | flops 104857600 | bytes 524288 | tf_op jit(solution)/shard_map/core0/pallas_call | solution.py:347
  145.5 0.0 collective-permute-done.14.c_ref
  145.5 0.2 collective-permute-done.13.b_ref
  145.8 0.0 collective-permute-done.12.a_ref
  145.8 0.0 copy-done.9
  145.8 1.9 %gated_norm.1 = (bf16[256,1024]{1,0:T(8,128)(2,1)}, f32[1024,128]{1,0:T(8,128)}) custom-call(s32[5]{0:T(128)S(1)} %stack.23.at_ref.refs_0_, s32[1]{0:T(128)S(6)} %copy.14.length_ref, f32[256,256]{1,0:T(8,128)S(1)} %get-tuple-element.46.own_ref, f32[256,128]{1,0:T(8,128)S(1)} %get-tuple-element.47.state_ref, ...), custom_call_target="tpu_custom_call" | custom-call | flops 2621440 | bytes 2097152 | tf_op jit(solution)/shard_map/gated_norm/pallas_call | solution.py:379
  (10 shorter events, 0.1 us)
Async XLA Ops:
  1.3 1.0 copy-start.2
  2.2 12.7 %copy-start.5 = (f32[4096]{0:T(1024)S(1)}, f32[4096]{0:T(1024)}, u32[]{:S(2)}) copy-start(f32[4096]{0:T(1024)} %param.15) | copy-start | bytes 49156
  3.2 34.4 %all-to-all-start = ((bf16[64,8,768]{2,1,0:T(8,128)(2,1)}), bf16[64,8,768]{2,1,0:T(8,128)(2,1)S(1)}, u32[]{:S(2)}, u32[]{:S(2)}) async-start(bf16[64,8,768]{2,1,0:T(8,128)(2,1)} %cut.1), calls=%async_computation | async-start | bytes 1572864 | tf_op jit(solution)/shard_map/all_to_all | solution.py:428
  14.9 1.6 %copy-start.1 = (bf16[256,4096]{1,0:T(8,128)(2,1)S(1)}, bf16[256,4096]{1,0:T(8,128)(2,1)}, u32[]{:S(2)}) copy-start(bf16[256,4096]{1,0:T(8,128)(2,1)} %hidden_ref.1) | copy-start | bytes 6291460
  18.6 76.5 %copy-start = (bf16[256,4096]{1,0:T(8,128)(2,1)}, bf16[256,4096]{1,0:T(8,128)(2,1)S(1)}, u32[]{:S(2)}) copy-start(bf16[256,4096]{1,0:T(8,128)(2,1)S(1)} %norm.1.refs_0_) | copy-start | bytes 6291460
  18.6 54.3 %collective-permute-start.4 = (bf16[256,4096]{1,0:T(8,128)(2,1)S(1)}, bf16[256,4096]{1,0:T(8,128)(2,1)}, u32[]{:S(2)}, u32[]{:S(2)}) collective-permute-start(bf16[256,4096]{1,0:T(8,128)(2,1)S(1)} %norm.1.refs_0_), channel_id=1, source_target_pairs={{0,128},{128,0},{1,129},{129,1},{2,130},{130,2},{3,131},{131,3},{4... | collective-permute-start | bytes 6291464 | tf_op jit(solution)/shard_map/ppermute | solution.py:405
  21.9 51.0 %collective-permute-start.5 = (bf16[256,4096]{1,0:T(8,128)(2,1)S(1)}, bf16[256,4096]{1,0:T(8,128)(2,1)}, u32[]{:S(2)}, u32[]{:S(2)}) collective-permute-start(bf16[256,4096]{1,0:T(8,128)(2,1)S(1)} %norm.1.refs_0_), channel_id=1, source_target_pairs={{0,16},{16,0},{1,17},{17,1},{2,18},{18,2},{3,19},{19,3},{4,20},{20... | collective-permute-start | bytes 6291464 | tf_op jit(solution)/shard_map/ppermute | solution.py:401
  37.7 24.2 %collective-permute-start = (bf16[528,640]{1,0:T(8,128)(2,1)S(1)}, bf16[528,640]{1,0:T(8,128)(2,1)S(1)}, u32[]{:S(2)}, u32[]{:S(2)}) collective-permute-start(bf16[528,640]{1,0:T(8,128)(2,1)S(1)} %get-tuple-element.29.refs_2_), channel_id=1, source_target_pairs={{32,0},{64,32},{96,64},{8,96},{40,8},{72,40},{104,72},{0,104},{33,... | collective-permute-start | bytes 2027528 | tf_op jit(solution)/shard_map/ppermute | solution.py:395
  48.3 18.8 %collective-permute-start.2 = (bf16[528,640]{1,0:T(8,128)(2,1)S(1)}, bf16[528,640]{1,0:T(8,128)(2,1)S(1)}, u32[]{:S(2)}, u32[]{:S(2)}) collective-permute-start(bf16[528,640]{1,0:T(8,128)(2,1)S(1)} %get-tuple-element.29.refs_2_), channel_id=1, source_target_pairs={{104,0},{0,32},{32,64},{64,96},{96,8},{8,40},{40,72},{72,104},{105... | collective-permute-start | bytes 2027528 | tf_op jit(solution)/shard_map/ppermute | solution.py:395
  61.8 17.9 %collective-permute-start.1 = (bf16[528,640]{1,0:T(8,128)(2,1)S(1)}, bf16[528,640]{1,0:T(8,128)(2,1)S(1)}, u32[]{:S(2)}, u32[]{:S(2)}) collective-permute-start(bf16[528,640]{1,0:T(8,128)(2,1)S(1)} %collective-permute-done.refs_3_), channel_id=1, source_target_pairs={{32,0},{64,32},{96,64},{8,96},{40,8},{72,40},{104,72},{0,104},{33,... | collective-permute-start | bytes 2027528 | tf_op jit(solution)/shard_map/ppermute | solution.py:395
  67.2 17.6 %collective-permute-start.3 = (bf16[528,640]{1,0:T(8,128)(2,1)S(1)}, bf16[528,640]{1,0:T(8,128)(2,1)S(1)}, u32[]{:S(2)}, u32[]{:S(2)}) collective-permute-start(bf16[528,640]{1,0:T(8,128)(2,1)S(1)} %collective-permute-done.2.refs_4_), channel_id=1, source_target_pairs={{104,0},{0,32},{32,64},{64,96},{96,8},{8,40},{40,72},{72,104},{105... | collective-permute-start | bytes 2027528 | tf_op jit(solution)/shard_map/ppermute | solution.py:395
  84.8 14.8 %collective-permute-start.8 = (bf16[256,4096]{1,0:T(8,128)(2,1)}, bf16[256,4096]{1,0:T(8,128)(2,1)S(1)}, u32[]{:S(2)}, u32[]{:S(2)}) collective-permute-start(bf16[256,4096]{1,0:T(8,128)(2,1)} %collective-permute-done.4.refs_0_), channel_id=1, source_target_pairs={{0,16},{16,0},{1,17},{17,1},{2,18},{18,2},{3,19},{19,3},{4,20},{20... | collective-permute-start | bytes 6291464 | tf_op jit(solution)/shard_map/ppermute | solution.py:401
  89.8 18.7 %collective-permute-start.6 = (bf16[528,640]{1,0:T(8,128)(2,1)S(1)}, bf16[528,640]{1,0:T(8,128)(2,1)S(1)}, u32[]{:S(2)}, u32[]{:S(2)}) collective-permute-start(bf16[528,640]{1,0:T(8,128)(2,1)S(1)} %collective-permute-done.1.refs_5_), channel_id=1, source_target_pairs={{32,0},{64,32},{96,64},{8,96},{40,8},{72,40},{104,72},{0,104},{33,... | collective-permute-start | bytes 2027528 | tf_op jit(solution)/shard_map/ppermute | solution.py:395
  91.7 19.9 %collective-permute-start.7 = (bf16[528,640]{1,0:T(8,128)(2,1)S(1)}, bf16[528,640]{1,0:T(8,128)(2,1)S(1)}, u32[]{:S(2)}, u32[]{:S(2)}) collective-permute-start(bf16[528,640]{1,0:T(8,128)(2,1)S(1)} %collective-permute-done.3.refs_6_), channel_id=1, source_target_pairs={{104,0},{0,32},{32,64},{64,96},{96,8},{8,40},{40,72},{72,104},{105... | collective-permute-start | bytes 2027528 | tf_op jit(solution)/shard_map/ppermute | solution.py:395
  99.6 1.4 copy-start.12
  111.6 13.3 %collective-permute-start.10 = (bf16[272,640]{1,0:T(8,128)(2,1)S(1)}, bf16[272,640]{1,0:T(8,128)(2,1)S(1)}, u32[]{:S(2)}, u32[]{:S(2)}) collective-permute-start(bf16[272,640]{1,0:T(8,128)(2,1)S(1)} %slice.7), channel_id=1, source_target_pairs={{104,0},{0,32},{32,64},{64,96},{96,8},{8,40},{40,72},{72,104},{105... | collective-permute-start | bytes 1044488 | tf_op jit(solution)/shard_map/ppermute | solution.py:395
  113.6 11.4 %collective-permute-start.9 = (bf16[256,640]{1,0:T(8,128)(2,1)S(1)}, bf16[256,640]{1,0:T(8,128)(2,1)S(1)}, u32[]{:S(2)}, u32[]{:S(2)}) collective-permute-start(bf16[256,640]{1,0:T(8,128)(2,1)S(1)} %slice.6), channel_id=1, source_target_pairs={{32,0},{64,32},{96,64},{8,96},{40,8},{72,40},{104,72},{0,104},{33,... | collective-permute-start | bytes 983048 | tf_op jit(solution)/shard_map/ppermute | solution.py:395
  121.5 3.4 %copy-start.10 = (f32[4,2,128]{2,1,0:T(2,128)S(1)}, f32[4,2,128]{2,1,0:T(2,128)}, u32[]{:S(2)}) copy-start(f32[4,2,128]{2,1,0:T(2,128)} %refs_6_.1) | copy-start | bytes 12292
  121.5 3.4 %copy-start.11 = (f32[2,128]{1,0:T(2,128)S(1)}, f32[2,128]{1,0:T(2,128)}, u32[]{:S(2)}) copy-start(f32[2,128]{1,0:T(2,128)} %refs_7_.1) | copy-start | bytes 3076
  125.0 6.2 %copy-start.3 = (f32[4,1024]{1,0:T(4,128)S(1)}, f32[4,1024]{1,0:T(4,128)}, u32[]{:S(2)}) copy-start(f32[4,1024]{1,0:T(4,128)} %refs_10_.7) | copy-start | bytes 49156
  125.0 6.2 %copy-start.4 = (f32[1024]{0:T(1024)S(1)}, f32[1024]{0:T(1024)}, u32[]{:S(2)}) copy-start(f32[1024]{0:T(1024)} %param.17) | copy-start | bytes 12292
  125.0 6.1 %copy-start.6 = (f32[16]{0:T(128)S(1)}, f32[16]{0:T(128)}, u32[]{:S(2)}) copy-start(f32[16]{0:T(128)} %refs_1_.7) | copy-start | bytes 196
  125.0 6.1 %copy-start.7 = (f32[16]{0:T(128)S(1)}, f32[16]{0:T(128)}, u32[]{:S(2)}) copy-start(f32[16]{0:T(128)} %refs_2_.7) | copy-start | bytes 196
  125.0 6.1 %copy-start.8 = (f32[16]{0:T(128)S(1)}, f32[16]{0:T(128)}, u32[]{:S(2)}) copy-start(f32[16]{0:T(128)} %refs_3_.7) | copy-start | bytes 196
  126.7 4.4 %collective-permute-start.11 = (bf16[1024,128]{1,0:T(8,128)(2,1)S(1)}, bf16[1024,128]{1,0:T(8,128)(2,1)S(1)}, u32[]{:S(2)}, u32[]{:S(2)}) collective-permute-start(bf16[1024,128]{1,0:T(8,128)(2,1)S(1)} %get-tuple-element.44.refs_7_), channel_id=1, source_target_pairs={{0,16},{16,0},{1,17},{17,1},{2,18},{18,2},{3,19},{19,3},{4,20},{20... | collective-permute-start | bytes 786440 | tf_op jit(solution)/shard_map/ppermute | solution.py:401
  132.8 12.7 %collective-permute-start.14 = (bf16[256,384]{1,0:T(8,128)(2,1)S(1)}, bf16[256,384]{1,0:T(8,128)(2,1)S(1)}, u32[]{:S(2)}, u32[]{:S(2)}) collective-permute-start(bf16[256,384]{1,0:T(8,128)(2,1)S(1)} %core3.1), channel_id=1, source_target_pairs={{0,144},{16,128},{128,16},{144,0},{1,145},{17,129},{129,17},{145,1... | collective-permute-start | bytes 589832 | tf_op jit(solution)/shard_map/ppermute | solution.py:409
  136.9 8.8 %collective-permute-start.13 = (bf16[256,384]{1,0:T(8,128)(2,1)S(1)}, bf16[256,384]{1,0:T(8,128)(2,1)S(1)}, u32[]{:S(2)}, u32[]{:S(2)}) collective-permute-start(bf16[256,384]{1,0:T(8,128)(2,1)S(1)} %core2.1), channel_id=1, source_target_pairs={{0,128},{128,0},{1,129},{129,1},{2,130},{130,2},{3,131},{131,3},{4... | collective-permute-start | bytes 589832 | tf_op jit(solution)/shard_map/ppermute | solution.py:405
  141.5 4.2 %copy-start.9 = (f32[1024]{0:T(1024)S(1)}, f32[1024]{0:T(1024)}, u32[]{:S(2)}) copy-start(f32[1024]{0:T(1024)} %param.23) | copy-start | bytes 12292
  141.6 4.2 %collective-permute-start.12 = (bf16[256,384]{1,0:T(8,128)(2,1)S(1)}, bf16[256,384]{1,0:T(8,128)(2,1)S(1)}, u32[]{:S(2)}, u32[]{:S(2)}) collective-permute-start(bf16[256,384]{1,0:T(8,128)(2,1)S(1)} %core1.1), channel_id=1, source_target_pairs={{0,16},{16,0},{1,17},{17,1},{2,18},{18,2},{3,19},{19,3},{4,20},{20... | collective-permute-start | bytes 589832 | tf_op jit(solution)/shard_map/ppermute | solution.py:401
